TPU v7x, 256 devices: a whole 4x4x8 slice. The times are simulated.
256 devices in a mesh: tm: 8 (over y, core), space: 32 (over x, z).
Axes of the slice: x: 4, y: 4, z: 8, core: 2. Of those that a mesh axis runs over, the one named last changes fastest.
Arguments:
- latent: bfloat16 [32, 64, 64, 256], P('tm', 'space'), may hold values from -24 to 24
- clip_frames: int32 [8], replicated, may hold values from 1 to 4, 16 in all
- clip_rank: int32 [8], replicated, may hold values from 0 to 7, each once
- group_of: int32 [256], replicated, may hold values from 0 to 31, as said below
- gain_first: float32 [256], replicated, may hold values from 0.1 to 1.9
- shift_first: float32 [256], replicated, may hold values from -3 to 3
- conv_first: bfloat16 [3, 3, 3, 256, 256], replicated, may hold values from -0.078125 to 0.078125
- bias_first: float32 [256], replicated, may hold values from -3 to 3
- gain_second: float32 [256], replicated, may hold values from 0.1 to 1.9
- shift_second: float32 [256], replicated, may hold values from -3 to 3
- conv_second: bfloat16 [3, 3, 3, 256, 256], replicated, may hold values from -0.078125 to 0.078125
- bias_second: float32 [256], replicated, may hold values from -3 to 3
Outputs:
- decoded: bfloat16 [16, 64, 64, 256], P('tm', 'space')
Inputs may be any that keep to these rules, and one draw needn't show every extreme that they name: `clip_frames`: the frame counts sum to 16; some clip has exactly 4 frames. `clip_rank`: each number of 0 to 7 appears once. `group_of`: each group number names exactly 8 channels.
All inputs are finite; a program needn't handle non-finite values.
Results may differ from a plain program's by a relative error of at most 0.0051.
Values may be sent and summed in bfloat16 or wider, within the bound.
No kernel may reach another device: no remote copies, remote signals or barrier semaphores. Data moves between devices by JAX's collectives and lax.ppermute only.
A program may use at most 64 MiB of HBM per device.

v0:
```python
import jax
import jax.numpy as jnp
from jax import lax
from jax.sharding import PartitionSpec as P

G = 32
WORK_F = 2


EPSILON = 1e-06
HIGH = lax.Precision.HIGHEST


def with_halo(shard, sides, width):
    for axis, dim in sides:
        size, length = (lax.axis_size(axis), shard.shape[dim])
        up = [(i, (i + 1) % size) for i in range(size - 1)]
        down = [(j, i) for i, j in up]
        last = lax.slice_in_dim(shard, length - width, length, axis=dim)
        first = lax.slice_in_dim(shard, 0, width, axis=dim)
        before = lax.ppermute(last, axis, up)
        after = lax.ppermute(first, axis, down)
        shard = jnp.concatenate([before, shard, after], axis=dim)
    return shard


def group_table(group_of):
    return (group_of[:, None] == jnp.arange(G, dtype=jnp.int32)[None, :]).astype(jnp.float32)


def clip_sums(values, frame_clip, member_groups):
    per_frame = jnp.sum(values, axis=(1, 2))
    per_clip = jnp.dot(frame_clip.T, per_frame, precision=HIGH)
    return jnp.dot(per_clip, member_groups, precision=HIGH)


def spread_back(stat_value, frame_clip, member_groups):
    per_frame = jnp.dot(frame_clip, stat_value, precision=HIGH)
    return jnp.dot(per_frame, member_groups.T, precision=HIGH)[:, None, None, :]


def normalize(field, gain, shift, frame_clip, counts, member_groups, reduce_stats):
    values = field.astype(jnp.float32)
    sums = clip_sums(values, frame_clip, member_groups)
    mean_value = reduce_stats(sums) / counts[:, None]
    centred = values - spread_back(mean_value, frame_clip, member_groups)
    spread = reduce_stats(clip_sums(centred * centred, frame_clip, member_groups)) / counts[:, None]
    scale_frame = spread_back(lax.rsqrt(spread + EPSILON), frame_clip, member_groups)
    return jax.nn.silu(centred * scale_frame * gain + shift).astype(jnp.bfloat16)


def rows_around(field):
    padded = with_halo(field, (("space", 1),), 1)
    band_index = lax.axis_index("space")
    last_band = lax.axis_size("space") - 1
    upper_rim = jnp.where(band_index == 0, padded[:, 1:2], padded[:, :1])
    lower_rim = jnp.where(band_index == last_band, padded[:, -2:-1], padded[:, -1:])
    padded = jnp.concatenate([upper_rim, padded[:, 1:-1], lower_rim], axis=1)
    return jnp.concatenate([padded[:, :, :1], padded, padded[:, :, -1:]], axis=2)


def causal_conv(taps, kernel, bias):
    frames = taps[0].shape[0]
    height = taps[0].shape[1] - 2
    columns = taps[0].shape[2] - 2
    channels = taps[0].shape[3]
    summed = jnp.zeros((frames * height * columns, channels), jnp.float32)
    for back_step in range(3):
        for row_step in range(3):
            row_slab = taps[back_step][:, row_step : row_step + height]
            widened = jnp.concatenate(
                [
                    row_slab[:, :, 0:columns],
                    row_slab[:, :, 1 : columns + 1],
                    row_slab[:, :, 2 : columns + 2],
                ],
                axis=-1,
            )
            kernel_rows = kernel[back_step, row_step].reshape(3 * channels, channels)
            summed = summed + jnp.dot(
                widened.reshape(-1, 3 * channels), kernel_rows, preferred_element_type=jnp.float32
            )
    return summed.reshape(frames, height, columns, channels) + bias


def to_stream(frames_home, lengths, clip_start):
    tm_place = lax.axis_index("tm")
    tm_count = lax.axis_size("tm")
    home_frames = frames_home.shape[0]
    position = jnp.arange(tm_count * WORK_F, dtype=jnp.int32) - clip_start[tm_place]
    inside = (position >= 0) & (position < lengths[tm_place])
    selector = (
        (position[:, None] == jnp.arange(home_frames, dtype=jnp.int32)[None, :]) & inside[:, None]
    ).astype(jnp.bfloat16)
    outgoing = jnp.dot(
        selector, frames_home.reshape(home_frames, -1), preferred_element_type=jnp.float32
    ).astype(jnp.bfloat16)
    outgoing = outgoing.reshape((tm_count, WORK_F) + frames_home.shape[1:])
    incoming = lax.all_to_all(outgoing, "tm", split_axis=0, concat_axis=0, tiled=True)
    return jnp.sum(incoming, axis=0)


def local(
    latent,
    clip_frames,
    clip_rank,
    group_of,
    gain_first,
    shift_first,
    conv_first,
    bias_first,
    gain_second,
    shift_second,
    conv_second,
    bias_second,
):
    member_groups = group_table(group_of)
    clip_start = jnp.sum(
        (clip_rank[None, :] < clip_rank[:, None]).astype(jnp.int32) * clip_frames[None, :], axis=1
    )
    pixels = latent.shape[1] * lax.axis_size("space") * latent.shape[2] * (latent.shape[3] // G)
    home_frames = latent.shape[0]
    own_length = clip_frames[lax.axis_index("tm")]
    frame_clip = (jnp.arange(home_frames, dtype=jnp.int32) < own_length).astype(jnp.float32)[
        :, None
    ]
    counts = (own_length.astype(jnp.float32) * float(pixels)).reshape(1)

    def home_taps(field):
        extended = rows_around(field)
        extended = jnp.concatenate([extended[:1], extended[:1], extended], axis=0)
        return [extended[back_step : back_step + home_frames] for back_step in range(3)]

    def band_totals(parts):
        return lax.psum(parts, "space")

    first_act = normalize(
        latent, gain_first, shift_first, frame_clip, counts, member_groups, band_totals
    )
    hidden = causal_conv(home_taps(first_act), conv_first, bias_first).astype(jnp.bfloat16)
    second_act = normalize(
        hidden, gain_second, shift_second, frame_clip, counts, member_groups, band_totals
    )
    finished = (
        latent.astype(jnp.float32) + causal_conv(home_taps(second_act), conv_second, bias_second)
    ).astype(jnp.bfloat16)
    result = to_stream(finished, clip_frames, clip_start)
    return result


def solution(mesh):
    placed = (P("tm", "space", None, None), P(), P(), P(), P(), P(), P(), P(), P(), P(), P(), P())
    return jax.shard_map(
        local, mesh=mesh, in_specs=placed, out_specs=P("tm", "space", None, None), check_vma=False
    )
```

profile of v0, /device:TPU:1, one launch (start us, length us, event | category | flops | bytes accessed | tf_op | source)
XLA Modules:
  0.0 367.4 jit_solution(11908890815530014695)
XLA Ops:
  0.0 1.2 dynamic_slice.8
  1.8 0.6 fusion.67
  2.4 1.0 convert_reduce_fusion
  3.4 0.7 convolution_bitcast_fusion.3
  4.1 0.9 fusion.38
  5.0 64.3 %psum.28 = f32[1,32]{1,0:T(1,128)S(1)} all-reduce(f32[1,32]{1,0:T(1,128)S(1)} %fusion.38), channel_id=1, replica_groups=mesh['tm'=8,'space'=32] {'space'}, use_global_device_ids=true, to_apply=%region_2.0 | all-reduce | flops 32 | bytes 256 | tf_op jit(solution)/shard_map/psum | solution.py:135
  69.4 0.9 fusion.37
  70.2 1.1 fusion.12
  71.3 0.7 convolution_bitcast_fusion.2
  72.0 0.9 fusion.36
  72.9 56.1 %psum.29 = f32[1,32]{1,0:T(1,128)S(1)} all-reduce(f32[1,32]{1,0:T(1,128)S(1)} %fusion.36), channel_id=1, replica_groups=mesh['tm'=8,'space'=32] {'space'}, use_global_device_ids=true, to_apply=%region_4.0 | all-reduce | flops 32 | bytes 256 | tf_op jit(solution)/shard_map/psum | solution.py:135
  129.0 0.9 fusion.35
  129.9 1.2 fusion.20
  131.1 0.7 fusion.83
  131.8 3.0 collective-permute-start
  134.8 1.3 collective-permute-start.1
  136.1 3.9 %fusion.73 = (bf16[1,1,3,256,256]{4,3,2,1,0:T(8,128)(2,1)}, bf16[1,1,3,256,256]{4,3,2,1,0:T(8,128)(2,1)}, bf16[1,1,3,256,256]{4,3,2,1,0:T(8,128)(2,1)}, bf16[1,1...) fusion(bf16[3,3,3,256,256]{4,3,2,1,0:T(8,128)(2,1)} %param.18), kind=kLoop, calls=%fused_computation.153 | loop fusion | bytes 7077888 | tf_op jit(solution)/shard_map/slice | solution.py:79
  140.1 1.0 fusion.72
  141.3 0.7 dynamic_slice.7
  141.9 0.9 broadcast_select_fusion.3
  143.0 0.3 maximum_maximum_fusion
  143.6 0.4 maximum_maximum_fusion.4
  144.3 0.3 fusion.77
  144.8 0.9 copy-done.11
  145.7 0.4 fusion.84
  146.3 0.7 copy-done.10
  147.0 0.4 convolution_add_fusion.15
  147.5 0.6 copy-done.9
  148.0 0.4 convolution_add_fusion.14
  148.6 0.8 copy-done.8
  149.4 0.4 convolution_add_fusion.13
  149.8 0.4 convolution_add_fusion.12
  150.3 0.5 copy-done.6
  150.8 0.4 convolution_add_fusion.11
  151.5 0.7 copy-done.5
  152.2 0.4 convolution_add_fusion.10
  152.6 0.4 convolution_add_fusion.9
  153.0 0.6 copy-done.3
  153.6 0.4 convolution_add_fusion.8
  154.0 0.7 convolution_bitcast_fusion.1
  155.0 57.8 %psum.30 = f32[1,32]{1,0:T(1,128)S(1)} all-reduce(f32[1,32]{1,0:T(1,128)S(1)} %fusion.34), channel_id=1, replica_groups=mesh['tm'=8,'space'=32] {'space'}, use_global_device_ids=true, to_apply=%region_6.7 | all-reduce | flops 32 | bytes 256 | tf_op jit(solution)/shard_map/psum | solution.py:135
  213.1 0.7 convolution_bitcast_fusion
  214.0 55.7 %psum.31 = f32[1,32]{1,0:T(1,128)S(1)} all-reduce(f32[1,32]{1,0:T(1,128)S(1)} %fusion.32), channel_id=1, replica_groups=mesh['tm'=8,'space'=32] {'space'}, use_global_device_ids=true, to_apply=%region_8.9 | all-reduce | flops 32 | bytes 256 | tf_op jit(solution)/shard_map/psum | solution.py:135
  270.3 3.4 collective-permute-start.2
  273.7 1.5 collective-permute-start.3
  275.2 0.7 iota_subtract_fusion
  275.9 1.3 compare_and_fusion
  277.1 2.3 collective-permute-done.3
  280.2 0.4 maximum_maximum_fusion.5
  280.9 0.3 fusion.76
  281.6 0.8 copy-done.2
  282.4 0.4 fusion.85
  282.9 0.4 convolution_add_fusion.7
  283.3 0.4 convolution_add_fusion.6
  283.8 0.4 convolution_add_fusion.5
  284.2 0.4 convolution_add_fusion.4
  284.6 0.4 convolution_add_fusion.3
  285.3 0.4 convolution_add_fusion.2
  285.7 0.4 convolution_add_fusion.1
  286.1 0.4 convolution_add_fusion
  286.4 0.5 copy-done
  287.3 0.5 convolution_convert_fusion
  288.0 78.6 %all_to_all.5 = bf16[8,2,2,64,256]{4,3,2,1,0:T(8,128)(2,1)S(1)} all-to-all(bf16[8,2,2,64,256]{4,3,2,1,0:T(8,128)(2,1)S(1)} %bitcast.129), channel_id=1, replica_groups=mesh['tm'=8,'space'=32] {'tm'}, dimensions={0} | all-to-all | bytes 2097152 | tf_op jit(solution)/shard_map/all_to_all | solution.py:99
  366.6 0.8 reduce_sum.62
  (73 shorter events, 5.6 us)
Async XLA Ops:
  131.8 10.1 %collective-permute-start = (bf16[4,1,64,256]{3,2,1,0:T(8,128)(2,1)}, bf16[4,1,64,256]{3,2,1,0:T(8,128)(2,1)S(1)}, u32[]{:S(2)}, u32[]{:S(2)}) collective-permute-start(bf16[4,1,64,256]{3,2,1,0:T(8,128)(2,1)} %get-tuple-element.93), channel_id=1, source_target_pairs={{0,1},{1,2},{2,3},{3,4},{4,5},{5,6},{6,7},{7,8},{8,9},{9,10},{10,1... | collective-permute-start | bytes 393224 | tf_op jit(solution)/shard_map/ppermute | solution.py:21
  134.8 7.1 %collective-permute-start.1 = (bf16[4,1,64,256]{3,2,1,0:T(8,128)(2,1)}, bf16[4,1,64,256]{3,2,1,0:T(8,128)(2,1)}, u32[]{:S(2)}, u32[]{:S(2)}) collective-permute-start(bf16[4,1,64,256]{3,2,1,0:T(8,128)(2,1)} %get-tuple-element.94), channel_id=1, source_target_pairs={{1,0},{2,1},{3,2},{4,3},{5,4},{6,5},{7,6},{8,7},{9,8},{10,9},{11,1... | collective-permute-start | bytes 393224 | tf_op jit(solution)/shard_map/ppermute | solution.py:22
  136.1 3.9 %copy-start.1 = (bf16[3,3,3,256,256]{4,3,2,1,0:T(8,128)(2,1)S(1)}, bf16[3,3,3,256,256]{4,3,2,1,0:T(8,128)(2,1)}, u32[]{:S(2)}) copy-start(bf16[3,3,3,256,256]{4,3,2,1,0:T(8,128)(2,1)} %param.22) | copy-start | bytes 10616836
  140.1 1.0 copy-start.12
  140.1 1.0 copy-start.17
  144.7 1.0 copy-start.11
  146.0 1.0 copy-start.10
  147.0 1.0 copy-start.9
  148.4 1.0 copy-start.8
  148.6 1.2 copy-start.7
  149.8 1.0 copy-start.6
  151.2 1.0 copy-start.5
  151.5 1.1 copy-start.4
  152.6 1.0 copy-start.3
  153.0 1.0 copy-start.13
  153.0 1.7 copy-start.18
  153.6 116.4 %copy-start.14 = (f32[256]{0:T(256)S(1)}, f32[256]{0:T(256)}, u32[]{:S(2)}) copy-start(f32[256]{0:T(256)} %param.21) | copy-start | bytes 3076
  153.6 116.4 %copy-start.15 = (f32[256]{0:T(256)S(1)}, f32[256]{0:T(256)}, u32[]{:S(2)}) copy-start(f32[256]{0:T(256)} %param.20) | copy-start | bytes 3076
  270.3 6.9 %collective-permute-start.2 = (bf16[4,1,64,256]{3,2,1,0:T(8,128)(2,1)S(1)}, bf16[4,1,64,256]{3,2,1,0:T(8,128)(2,1)S(1)}, u32[]{:S(2)}, u32[]{:S(2)}) collective-permute-start(bf16[4,1,64,256]{3,2,1,0:T(8,128)(2,1)S(1)} %get-tuple-element.86), channel_id=1, source_target_pairs={{0,1},{1,2},{2,3},{3,4},{4,5},{5,6},{6,7},{7,8},{8,9},{9,10},{10,1... | collective-permute-start | bytes 393224 | tf_op jit(solution)/shard_map/ppermute | solution.py:21
  273.7 5.8 %collective-permute-start.3 = (bf16[4,1,64,256]{3,2,1,0:T(8,128)(2,1)S(1)}, bf16[4,1,64,256]{3,2,1,0:T(8,128)(2,1)S(1)}, u32[]{:S(2)}, u32[]{:S(2)}) collective-permute-start(bf16[4,1,64,256]{3,2,1,0:T(8,128)(2,1)S(1)} %get-tuple-element.87), channel_id=1, source_target_pairs={{1,0},{2,1},{3,2},{4,3},{5,4},{6,5},{7,6},{8,7},{9,8},{10,9},{11,1... | collective-permute-start | bytes 393224 | tf_op jit(solution)/shard_map/ppermute | solution.py:22
  281.4 1.0 copy-start.2
  286.0 1.0 copy-start
  286.0 0.9 copy-start.16
where the time goes:
time: 368 us; the launch traced here: 367 us
  blocking collectives  313 us (85%)
  local copies, waits for them, and re-layouts  16.1 us (4%)
  matrix products  14.4 us (4%)
  other arithmetic  11.7 us (3%)
  starting transfers between devices  9.18 us (2%)
    psum x4, blocking collectives, band_totals(): return lax.psum(parts, 'space')  234 us
    all_to_all x1, blocking collectives, to_stream(): lax.all_to_all(outgoing, 'tm', split_axis=0, concat_axis=0, tiled=True)  78.6 us
  transfers between devices with their start and end apart: 4, of which 1 were waited for; matrix products, arithmetic and copies ran while one was open for 2% of the time, Pallas kernels for 0%

commit v1 on v0

v1 whole, which is shorter than its diff:
```python
import functools

import jax
import jax.numpy as jnp
from jax import lax
from jax.experimental import pallas as pl
from jax.experimental.pallas import tpu as pltpu
from jax.sharding import PartitionSpec as P

G = 32
LANES = 128
EPSILON = 1e-06
HIGH = lax.Precision.HIGHEST
F32 = jnp.float32
BF16 = jnp.bfloat16
VMEM = pl.BlockSpec(memory_space=pltpu.VMEM)
SMEM = pl.BlockSpec(memory_space=pltpu.SMEM)
HBM = pl.BlockSpec(memory_space=pl.ANY)
LIMIT = 40 * 1024 * 1024


def dot_high(a, b, contract):
    return lax.dot_general(a, b, ((contract[:1], contract[1:]), ((), ())), precision=HIGH, preferred_element_type=F32)


def member_rows(group_row, first):
    channels = group_row.shape[1]
    rows = lax.broadcasted_iota(jnp.int32, (LANES, channels), 0)
    return (rows - first == group_row).astype(F32)


def clip_start_of(frames_ref, rank_ref, clip):
    start = jnp.int32(0)
    for k in range(frames_ref.shape[0]):
        start = start + jnp.where(rank_ref[k] < rank_ref[clip], frames_ref[k], 0)
    return start


def local_stats(field_ref, length, group_row):
    frames, height, columns, channels = field_ref.shape
    pixels = height * columns
    scale = 1.0 / (length.astype(F32) * float(pixels * (channels // G)))
    live = [jnp.where(f < length, 1.0, 0.0).astype(F32) for f in range(frames)]

    def frame(f):
        return field_ref[f].astype(F32).reshape(pixels, channels)

    total = jnp.zeros((1, channels), F32)
    for f in range(frames):
        total = total + live[f] * jnp.sum(frame(f), axis=0, keepdims=True)
    mean_rows = member_rows(group_row, 0)
    group_mean = dot_high(jnp.broadcast_to(total, (8, channels)), mean_rows, (1, 1)) * scale
    mean = dot_high(group_mean, mean_rows, (1, 0))[:1]
    spread = jnp.zeros((1, channels), F32)
    for f in range(frames):
        centred = frame(f) - mean
        spread = spread + live[f] * jnp.sum(centred * centred, axis=0, keepdims=True)
    group_spread = dot_high(jnp.broadcast_to(spread, (8, channels)), member_rows(group_row, G), (1, 1))
    return (group_mean + group_spread)[:1]


def combine_stats(parts, length, pixels, group_row):
    bands = parts.shape[0]
    channels = group_row.shape[1]
    per_band = length.astype(F32) * float(pixels * (channels // G))
    lane = lax.broadcasted_iota(jnp.int32, (1, LANES), 1)
    sums = jnp.sum(parts, axis=0, keepdims=True)
    mean = sums * (1.0 / bands)
    away = parts - mean
    between = jnp.sum(away * away, axis=0, keepdims=True) * per_band
    spread = jnp.where(lane < G, between, jnp.where(lane < 2 * G, sums, 0.0))
    mean = jnp.where(lane < G, mean, 0.0)
    which = lax.broadcasted_iota(jnp.int32, (8, LANES), 0)
    both = jnp.where(which == 0, mean, spread)
    spread_back = dot_high(both, member_rows(group_row, 0) + member_rows(group_row, G), (1, 0))
    variance = spread_back[1:2] / (per_band * bands)
    return spread_back[:1], lax.rsqrt(variance + EPSILON)


def activate(field_ref, above_ref, below_ref, act_ref, mean, scale, shift):
    frames, height, columns, channels = field_ref.shape
    band = lax.axis_index("space")
    top = band == 0
    bottom = band == lax.axis_size("space") - 1
    for f in range(frames):
        for r in range(height + 2):
            if r == 0:
                value = jnp.where(top, field_ref[f, 0], above_ref[f])
            elif r == height + 1:
                value = jnp.where(bottom, field_ref[f, height - 1], below_ref[f])
            else:
                value = field_ref[f, r - 1]
            half = ((value.astype(F32) - mean) * scale + shift) * 0.5
            act = half * jnp.tanh(half) + half
            left = jnp.concatenate([act[:1], act[:-1]], axis=0)
            right = jnp.concatenate([act[1:], act[-1:]], axis=0)
            for step, taken in enumerate((left, act, right)):
                taken = taken.astype(BF16)
                lanes = slice(step * channels, (step + 1) * channels)
                for place in (0, 1, 2) if f == 0 else (f + 2,):
                    act_ref[place, r, :, lanes] = taken


def convolve(act_ref, weight_ref, sem, kernel_hbm, acc_ref, frames, height):
    columns, width = act_ref.shape[2:]
    rows = frames * height * columns
    for tap in range(9):
        back_step, row_step = divmod(tap, 3)
        pltpu.make_async_copy(kernel_hbm.at[tap], weight_ref.at[tap], sem.at[tap]).wait()
        slab = act_ref[back_step : back_step + frames, row_step : row_step + height].reshape(rows, width)
        part = jnp.dot(slab, weight_ref[tap], preferred_element_type=F32)
        if tap == 0:
            acc_ref[...] = part
        else:
            acc_ref[...] += part


def start_weights(kernel_hbm, weight_ref, sem):
    for tap in range(9):
        pltpu.make_async_copy(kernel_hbm.at[tap], weight_ref.at[tap], sem.at[tap]).start()


def stats_kernel(frames_ref, field_ref, group_ref, parts_ref, first_ref, last_ref):
    length = frames_ref[lax.axis_index("tm")]
    height = field_ref.shape[1]
    first_ref[...] = field_ref[:, 0]
    last_ref[...] = field_ref[:, height - 1]
    row = local_stats(field_ref, length, group_ref[...])
    parts_ref[...] = jnp.broadcast_to(row[None], parts_ref.shape)


def first_kernel(
    frames_ref, parts_ref, field_ref, above_ref, below_ref, group_ref, gain_ref, shift_ref, bias_ref, kernel_hbm,
    hidden_ref, out_parts_ref, first_ref, last_ref,
    weight_ref, act_ref, acc_ref, sem,
):
    start_weights(kernel_hbm, weight_ref, sem)
    frames, height, columns, channels = field_ref.shape
    length = frames_ref[lax.axis_index("tm")]
    mean, inverse = combine_stats(parts_ref[:, 0], length, height * columns, group_ref[...])
    activate(field_ref, above_ref, below_ref, act_ref, mean, inverse * gain_ref[...], shift_ref[...])
    convolve(act_ref, weight_ref, sem, kernel_hbm, acc_ref, frames, height)
    hidden = (acc_ref[...] + bias_ref[...]).astype(BF16).reshape(hidden_ref.shape)
    hidden_ref[...] = hidden
    first_ref[...] = hidden_ref[:, 0]
    last_ref[...] = hidden_ref[:, height - 1]
    row = local_stats(hidden_ref, length, group_ref[...])
    out_parts_ref[...] = jnp.broadcast_to(row[None], out_parts_ref.shape)


def second_kernel(
    frames_ref, rank_ref, parts_ref, field_ref, above_ref, below_ref, latent_ref, group_ref, gain_ref, shift_ref,
    bias_ref, kernel_hbm,
    keep_ref, send_ref,
    weight_ref, act_ref, acc_ref, sem,
):
    start_weights(kernel_hbm, weight_ref, sem)
    frames, height, columns, channels = field_ref.shape
    clip = lax.axis_index("tm")
    core = lax.rem(clip, 2)
    length = frames_ref[clip]
    start = clip_start_of(frames_ref, rank_ref, clip)
    mean, inverse = combine_stats(parts_ref[:, 0], length, height * columns, group_ref[...])
    activate(field_ref, above_ref, below_ref, act_ref, mean, inverse * gain_ref[...], shift_ref[...])
    convolve(act_ref, weight_ref, sem, kernel_hbm, acc_ref, frames, height)
    pixels = height * columns
    for f in range(frames):
        total = acc_ref[f * pixels : (f + 1) * pixels] + bias_ref[...]
        total = latent_ref[f].astype(F32) + total.reshape(height, columns, channels)
        total = total.astype(BF16)
        place = lax.rem(start + f, 4)
        slot = lax.rem(place, 2)
        stays = place // 2 == core

        @pl.when(stays)
        def _():
            keep_ref[slot] = total

        @pl.when(jnp.logical_not(stays))
        def _():
            send_ref[slot] = total


def spread_kernel(frames_ref, rank_ref, keep_ref, got_ref, out_ref):
    clip = lax.axis_index("tm")
    core = lax.rem(clip, 2)
    other = clip + 1 - 2 * core
    start = clip_start_of(frames_ref, rank_ref, other)
    length = frames_ref[other]
    for chip in range(out_ref.shape[0]):
        for slot in range(2):
            place = 4 * chip + 2 * core + slot - start
            theirs = (place >= 0) & (place < length)
            out_ref[chip, slot] = jnp.where(theirs, got_ref[slot], keep_ref[slot])


def pick_kernel(frames_ref, rank_ref, got_hbm, out_hbm, sem):
    clip = lax.axis_index("tm")
    copies = []
    for slot in range(2):
        place = 2 * clip + slot
        source = jnp.int32(0)
        for k in range(frames_ref.shape[0]):
            offset = place - clip_start_of(frames_ref, rank_ref, k)
            source = source + jnp.where((offset >= 0) & (offset < frames_ref[k]), k // 2, 0)
        copies.append(pltpu.make_async_copy(got_hbm.at[source, slot], out_hbm.at[slot], sem.at[slot]))
    for copy in copies:
        copy.start()
    for copy in copies:
        copy.wait()


def call(kernel, in_specs, outs, scratch=(), out_spec=VMEM):
    return pl.pallas_call(
        kernel,
        in_specs=in_specs,
        out_specs=[out_spec] * len(outs),
        out_shape=[jax.ShapeDtypeStruct(shape, kind) for shape, kind in outs],
        scratch_shapes=list(scratch),
        compiler_params=pltpu.CompilerParams(vmem_limit_bytes=LIMIT),
    )


def local(
    latent,
    clip_frames,
    clip_rank,
    group_of,
    gain_first,
    shift_first,
    conv_first,
    bias_first,
    gain_second,
    shift_second,
    conv_second,
    bias_second,
):
    frames, height, columns, channels = latent.shape
    bands = lax.axis_size("space")
    clips = lax.axis_size("tm")
    row = lambda v: v.reshape(1, channels)
    taps = lambda k: k.reshape(9, 3 * channels, channels)
    group_row = row(group_of)
    edge = ((frames, columns, channels), BF16)
    parts_out = ((bands, 1, LANES), F32)

    def gather(parts):
        return lax.all_to_all(parts, "space", 0, 0, tiled=True)

    def halos(first, last):
        above = lax.ppermute(last, "space", [(i, (i + 1) % bands) for i in range(bands)])
        below = lax.ppermute(first, "space", [((i + 1) % bands, i) for i in range(bands)])
        return above, below

    work = [
        pltpu.VMEM((9, 3 * channels, channels), BF16),
        pltpu.VMEM((frames + 2, height + 2, columns, 3 * channels), BF16),
        pltpu.VMEM((frames * height * columns, channels), F32),
        pltpu.SemaphoreType.DMA((9,)),
    ]

    parts, first, last = call(stats_kernel, [SMEM, VMEM, VMEM], [parts_out, edge, edge])(clip_frames, latent, group_row)
    above, below = halos(first, last)
    parts = gather(parts)
    hidden, parts, first, last = call(
        first_kernel, [SMEM] + [VMEM] * 8 + [HBM], [(latent.shape, BF16), parts_out, edge, edge], work
    )(clip_frames, parts, latent, above, below, group_row, row(gain_first), row(shift_first), row(bias_first), taps(conv_first))
    above, below = halos(first, last)
    parts = gather(parts)
    half = ((2, height, columns, channels), BF16)
    keep, send = call(second_kernel, [SMEM] * 2 + [VMEM] * 9 + [HBM], [half, half], work)(
        clip_frames, clip_rank, parts, hidden, above, below, latent, group_row, row(gain_second), row(shift_second),
        row(bias_second), taps(conv_second),
    )
    got = lax.ppermute(send, "tm", [(i, i ^ 1) for i in range(clips)])
    chips = clips // 2
    (spread,) = call(spread_kernel, [SMEM] * 2 + [VMEM] * 2, [((chips,) + half[0], BF16)])(clip_frames, clip_rank, keep, got)
    groups = [[core + 2 * chip for chip in range(chips)] for core in range(2)]
    spread = lax.all_to_all(spread, "tm", 0, 0, axis_index_groups=groups, tiled=True)
    (out,) = call(pick_kernel, [SMEM] * 2 + [HBM], [half], [pltpu.SemaphoreType.DMA((2,))], HBM)(clip_frames, clip_rank, spread)
    return out


def solution(mesh):
    placed = (P("tm", "space", None, None), P(), P(), P(), P(), P(), P(), P(), P(), P(), P(), P())
    return jax.shard_map(
        local, mesh=mesh, in_specs=placed, out_specs=P("tm", "space", None, None), check_vma=False
    )
```

time: 368 us -> 82.8 us (0.23)
  blocking collectives: 313 us -> 38.5 us
  Pallas kernels: 0 us -> 18.5 us
  matrix products: 14.4 us -> 0 us
  other arithmetic: 11.7 us -> 0 us
  local copies, waits for them, and re-layouts: 16.1 us -> 6.36 us
  starting transfers between devices: 9.18 us -> 18.1 us
    psum x4 -> x0, blocking collectives: 234 us -> none  [band_totals(): return lax.psum(parts, 'space')]
    all_to_all x1 -> x3, blocking collectives: 78.6 us -> 38.5 us  [the longest x2 25.9 us: gather(): return lax.all_to_all(parts, 'space', 0, 0, tiled=True)]
    pallas_call x0 -> x5, Pallas kernels: none -> 18.5 us  [the longest x1 8.06 us: local(): call(first_kernel, [SMEM] + [VMEM] * 8 + [HBM], [(latent.shape, BF16), pa...]
    dot_general x31 -> x0, matrix products: 14.4 us -> none  [the longest x18 6.7 us: causal_conv(): jnp.dot(widened.reshape(-1, 3 * channels), kernel_rows, preferred_element...]
    ppermute x4 -> x5, starting transfers between devices: 9.18 us -> 18.1 us  [the longest x2 10.7 us: halos(): lax.ppermute(first, 'space', [((i + 1) % bands, i) for i in range(bands)])]
    slice x11 -> x0, local copies, waits for them, and re-layouts: 7.44 us -> none  [the longest x2 4.92 us: causal_conv(): kernel_rows = kernel[back_step, row_step].reshape(3 * channels, channels)]
  transfers between devices with their start and end apart: 4 -> 5, of which waited for: 1 -> 1; matrix products, arithmetic and copies ran while one was open for 2% -> 0% of each run, Pallas kernels for 0% -> 0%
where the time goes in v1:
time: 82.8 us; the launch traced here: 82.5 us
  blocking collectives  38.5 us (46%)
  Pallas kernels  18.5 us (22%)
  starting transfers between devices  18.1 us (22%)
  local copies, waits for them, and re-layouts  6.36 us (8%)
  waiting for transfers between devices  1 us (1%)
    all_to_all x2, blocking collectives, gather(): return lax.all_to_all(parts, 'space', 0, 0, tiled=True)  25.9 us
    all_to_all x1, blocking collectives, local(): lax.all_to_all(spread, 'tm', 0, 0, axis_index_groups=groups, tiled=True)  12.6 us
    ppermute x2, starting transfers between devices, halos(): lax.ppermute(first, 'space', [((i + 1) % bands, i) for i in range(bands)])  10.7 us
    pallas_call x1, Pallas kernels, local(): call(first_kernel, [SMEM] + [VMEM] * 8 + [HBM], [(latent.shape, BF16), pa...  8.06 us
    pallas_call x1, Pallas kernels, local(): call(second_kernel, [SMEM] * 2 + [VMEM] * 9 + [HBM], [half, half], work)  7.09 us
    unnamed x24, local copies, waits for them, and re-layouts  6.36 us
    ppermute x1, starting transfers between devices, local(): got = lax.ppermute(send, 'tm', [(i, i ^ 1) for i in range(clips)])  4.46 us
    ppermute x2, starting transfers between devices, halos(): lax.ppermute(last, 'space', [(i, (i + 1) % bands) for i in range(bands)])  2.96 us
  transfers between devices with their start and end apart: 5, of which 1 were waited for; matrix products, arithmetic and copies ran while one was open for 0% of the time, Pallas kernels for 0%

profile of v1, /device:TPU:1, one launch (start us, length us, event | category | flops | bytes accessed | tf_op | source)
XLA Modules:
  0.0 82.5 jit_solution(3496307105749590770)
XLA Ops:
  0.0 0.0 copy-start.5
  0.0 0.0 copy-start.9
  0.0 0.0 copy-start.2
  0.0 1.0 %copy-done.2 = bf16[4,2,64,256]{3,2,1,0:T(8,128)(2,1)S(1)} copy-done((bf16[4,2,64,256]{3,2,1,0:T(8,128)(2,1)S(1)}, bf16[4,2,64,256]{3,2,1,0:T(8,128)(2,1)}, u32[]{:S(2)}) %copy-start.2) | copy-done | bytes 262168
  1.0 0.0 copy-start.3
  1.0 0.7 copy-done.3
  1.6 0.0 copy-start.4
  1.6 0.7 copy-done.4
  2.3 0.0 copy-start.10
  2.3 0.0 copy-start.11
  2.3 1.4 %shard_map.118 = (f32[32,1,128]{2,1,0:T(1,128)S(1)}, bf16[4,64,256]{2,1,0:T(8,128)(2,1)S(1)}, bf16[4,64,256]{2,1,0:T(8,128)(2,1)S(1)}) custom-call(s32[8]{0:T(128)S(1)} %copy-done.3, bf16[4,2,64,256]{3,2,1,0:T(8,128)(2,1)S(1)} %copy-done.2, s32[1,256]{1,0:T(1,128)S(1)} %bitcast.11), custom_call_target="tpu_custom_call" | custom-call | tf_op jit(solution)/shard_map/pallas_call | solution.py:262
  3.8 2.5 %collective-permute-start = (bf16[4,64,256]{2,1,0:T(8,128)(2,1)S(1)}, bf16[4,64,256]{2,1,0:T(8,128)(2,1)S(1)}, u32[]{:S(2)}, u32[]{:S(2)}) collective-permute-start(bf16[4,64,256]{2,1,0:T(8,128)(2,1)S(1)} %get-tuple-element.15), channel_id=1, source_target_pairs={{0,1},{1,2},{2,3},{3,4},{4,5},{5,6},{6,7},{7,8},{8,9},{9,10},{10,1... | collective-permute-start | bytes 393224 | tf_op jit(solution)/shard_map/ppermute | solution.py:251
  6.3 6.2 %collective-permute-start.1 = (bf16[4,64,256]{2,1,0:T(8,128)(2,1)S(1)}, bf16[4,64,256]{2,1,0:T(8,128)(2,1)S(1)}, u32[]{:S(2)}, u32[]{:S(2)}) collective-permute-start(bf16[4,64,256]{2,1,0:T(8,128)(2,1)S(1)} %get-tuple-element.16), channel_id=1, source_target_pairs={{1,0},{2,1},{3,2},{4,3},{5,4},{6,5},{7,6},{8,7},{9,8},{10,9},{11,1... | collective-permute-start | bytes 393224 | tf_op jit(solution)/shard_map/ppermute | solution.py:252
  12.5 14.3 %all_to_all.15.parts_ref = f32[32,1,128]{2,1,0:T(1,128)S(1)} all-to-all(f32[32,1,128]{2,1,0:T(1,128)S(1)} %get-tuple-element.14), channel_id=1, replica_groups=mesh['tm'=8,'space'=32] {'space'}, dimensions={0} | all-to-all | bytes 32768 | tf_op jit(solution)/shard_map/all_to_all | solution.py:248
  26.8 0.0 collective-permute-done.above_ref
  26.8 0.0 collective-permute-done.1.below_ref
  26.8 0.0 copy-start
  26.8 2.0 %copy-done = bf16[3,3,3,256,256]{4,3,2,1,0:T(8,128)(2,1)S(1)} copy-done((bf16[3,3,3,256,256]{4,3,2,1,0:T(8,128)(2,1)S(1)}, bf16[3,3,3,256,256]{4,3,2,1,0:T(8,128)(2,1)}, u32[]{:S(2)}) %copy-start) | copy-done | bytes 3538968
  28.8 0.0 copy-start.6
  28.8 0.7 copy-done.6
  29.5 0.0 copy-start.7
  29.5 0.7 copy-done.7
  30.2 0.0 copy-start.8
  30.2 0.7 copy-done.8
  30.9 0.0 copy-start.1
  30.9 8.1 %shard_map.119 = (bf16[4,2,64,256]{3,2,1,0:T(8,128)(2,1)S(1)}, f32[32,1,128]{2,1,0:T(1,128)S(1)}, bf16[4,64,256]{2,1,0:T(8,128)(2,1)S(1)}, bf16[4,64,256]{2,1,0:T(8,128)(2,1)S(1)}) custom-call(s32[8]{0:T(128)S(1)} %copy-done.3, f32[32,1,128]{2,1,0:T(1,128)S(1)} %all_to_all.15.parts_ref, bf16[4,2,64,256]{3,2,1,0:T(8,128)(2,1)S(1)} %copy-done.2, ...), custom_call_target="tpu_custom_call" | custom-call | tf_op jit(solution)/shard_map/pallas_call | solution.py:265
  38.9 0.4 collective-permute-start.2
  39.3 4.4 %collective-permute-start.3 = (bf16[4,64,256]{2,1,0:T(8,128)(2,1)S(1)}, bf16[4,64,256]{2,1,0:T(8,128)(2,1)S(1)}, u32[]{:S(2)}, u32[]{:S(2)}) collective-permute-start(bf16[4,64,256]{2,1,0:T(8,128)(2,1)S(1)} %get-tuple-element.20), channel_id=1, source_target_pairs={{1,0},{2,1},{3,2},{4,3},{5,4},{6,5},{7,6},{8,7},{9,8},{10,9},{11,1... | collective-permute-start | bytes 393224 | tf_op jit(solution)/shard_map/ppermute | solution.py:252
  43.8 11.6 %all_to_all.16.parts_ref = f32[32,1,128]{2,1,0:T(1,128)S(1)} all-to-all(f32[32,1,128]{2,1,0:T(1,128)S(1)} %get-tuple-element.17), channel_id=1, replica_groups=mesh['tm'=8,'space'=32] {'space'}, dimensions={0} | all-to-all | bytes 32768 | tf_op jit(solution)/shard_map/all_to_all | solution.py:248
  55.4 0.0 collective-permute-done.2.above_ref
  55.4 0.0 collective-permute-done.3.below_ref
  55.4 0.0 copy-done.5
  55.4 0.0 copy-done.9
  55.4 0.0 copy-done.10
  55.4 0.0 copy-done.11
  55.4 0.0 copy-done.1
  55.4 7.1 %shard_map.120 = (bf16[2,2,64,256]{3,2,1,0:T(8,128)(2,1)S(1)}, bf16[2,2,64,256]{3,2,1,0:T(8,128)(2,1)S(1)}) custom-call(s32[8]{0:T(128)S(1)} %copy-done.3, s32[8]{0:T(128)S(1)} %copy-done.5, f32[32,1,128]{2,1,0:T(1,128)S(1)} %all_to_all.16.parts_ref, bf16[4,2,64,256]{3,2,1,0:T(8,128)(2,1)S(1)} %get-tuple-element.18.field_ref, ...), custom_call_target="tpu_custom_call" | custom-call | tf_op jit(solution)/shard_map/pallas_call | solution.py:271
  62.5 4.5 %collective-permute-start.4 = (bf16[2,2,64,256]{3,2,1,0:T(8,128)(2,1)S(1)}, bf16[2,2,64,256]{3,2,1,0:T(8,128)(2,1)S(1)}, u32[]{:S(2)}, u32[]{:S(2)}) collective-permute-start(bf16[2,2,64,256]{3,2,1,0:T(8,128)(2,1)S(1)} %get-tuple-element.22), channel_id=1, source_target_pairs={{0,32},{32,0},{64,96},{96,64},{128,160},{160,128},{192,224},{224,1... | collective-permute-start | bytes 393224 | tf_op jit(solution)/shard_map/ppermute | solution.py:275
  67.0 1.0 %collective-permute-done.4.got_ref = bf16[2,2,64,256]{3,2,1,0:T(8,128)(2,1)S(1)} collective-permute-done((bf16[2,2,64,256]{3,2,1,0:T(8,128)(2,1)S(1)}, bf16[2,2,64,256]{3,2,1,0:T(8,128)(2,1)S(1)}, u32[]{:S(2)}, u32[]{:S(2)}) %collective-permute-start.4) | collective-permute-done | bytes 131104 | tf_op jit(solution)/shard_map/ppermute | solution.py:275
  68.0 0.6 shard_map.121
  68.6 12.6 %all_to_all.17.got_hbm = bf16[4,2,2,64,256]{4,3,2,1,0:T(8,128)(2,1)S(1)} all-to-all(bf16[4,2,2,64,256]{4,3,2,1,0:T(8,128)(2,1)S(1)} %shard_map.121), channel_id=1, replica_groups={{0,64,128,192},{32,96,160,224},{1,65,129,193},{33,97,161,225},{2,66,130..., dimensions={0} | all-to-all | bytes 1048576 | tf_op jit(solution)/shard_map/all_to_all | solution.py:279
  81.2 1.3 %shard_map.122 = bf16[2,2,64,256]{3,2,1,0:T(8,128)(2,1)} custom-call(s32[8]{0:T(128)S(1)} %copy-done.3, s32[8]{0:T(128)S(1)} %copy-done.5, bf16[4,2,2,64,256]{4,3,2,1,0:T(8,128)(2,1)S(1)} %all_to_all.17.got_hbm), custom_call_target="tpu_custom_call" | custom-call | tf_op jit(solution)/shard_map/pallas_call | solution.py:280
Async XLA Ops:
  0.0 55.4 %copy-start.5 = (s32[8]{0:T(128)S(1)}, s32[8]{0:T(128)}, u32[]{:S(2)}) copy-start(s32[8]{0:T(128)} %rank_ref.5) | copy-start | bytes 100
  0.0 55.4 %copy-start.9 = (f32[256]{0:T(256)S(1)}, f32[256]{0:T(256)}, u32[]{:S(2)}) copy-start(f32[256]{0:T(256)} %param.20) | copy-start | bytes 3076
  0.0 1.0 %copy-start.2 = (bf16[4,2,64,256]{3,2,1,0:T(8,128)(2,1)S(1)}, bf16[4,2,64,256]{3,2,1,0:T(8,128)(2,1)}, u32[]{:S(2)}) copy-start(bf16[4,2,64,256]{3,2,1,0:T(8,128)(2,1)} %latent_ref.1) | copy-start | bytes 786436
  1.0 0.7 copy-start.3
  1.6 0.7 copy-start.4
  2.3 53.1 %copy-start.10 = (f32[256]{0:T(256)S(1)}, f32[256]{0:T(256)}, u32[]{:S(2)}) copy-start(f32[256]{0:T(256)} %param.21) | copy-start | bytes 3076
  2.3 53.1 %copy-start.11 = (f32[256]{0:T(256)S(1)}, f32[256]{0:T(256)}, u32[]{:S(2)}) copy-start(f32[256]{0:T(256)} %param.23) | copy-start | bytes 3076
  3.8 23.0 %collective-permute-start = (bf16[4,64,256]{2,1,0:T(8,128)(2,1)S(1)}, bf16[4,64,256]{2,1,0:T(8,128)(2,1)S(1)}, u32[]{:S(2)}, u32[]{:S(2)}) collective-permute-start(bf16[4,64,256]{2,1,0:T(8,128)(2,1)S(1)} %get-tuple-element.15), channel_id=1, source_target_pairs={{0,1},{1,2},{2,3},{3,4},{4,5},{5,6},{6,7},{7,8},{8,9},{9,10},{10,1... | collective-permute-start | bytes 393224 | tf_op jit(solution)/shard_map/ppermute | solution.py:251
  6.3 20.5 %collective-permute-start.1 = (bf16[4,64,256]{2,1,0:T(8,128)(2,1)S(1)}, bf16[4,64,256]{2,1,0:T(8,128)(2,1)S(1)}, u32[]{:S(2)}, u32[]{:S(2)}) collective-permute-start(bf16[4,64,256]{2,1,0:T(8,128)(2,1)S(1)} %get-tuple-element.16), channel_id=1, source_target_pairs={{1,0},{2,1},{3,2},{4,3},{5,4},{6,5},{7,6},{8,7},{9,8},{10,9},{11,1... | collective-permute-start | bytes 393224 | tf_op jit(solution)/shard_map/ppermute | solution.py:252
  26.8 2.0 %copy-start = (bf16[3,3,3,256,256]{4,3,2,1,0:T(8,128)(2,1)S(1)}, bf16[3,3,3,256,256]{4,3,2,1,0:T(8,128)(2,1)}, u32[]{:S(2)}) copy-start(bf16[3,3,3,256,256]{4,3,2,1,0:T(8,128)(2,1)} %param.18) | copy-start | bytes 10616836
  28.8 0.7 copy-start.6
  29.5 0.7 copy-start.7
  30.2 0.7 copy-start.8
  30.9 24.6 %copy-start.1 = (bf16[3,3,3,256,256]{4,3,2,1,0:T(8,128)(2,1)S(1)}, bf16[3,3,3,256,256]{4,3,2,1,0:T(8,128)(2,1)}, u32[]{:S(2)}) copy-start(bf16[3,3,3,256,256]{4,3,2,1,0:T(8,128)(2,1)} %param.22) | copy-start | bytes 10616836
  38.9 16.5 %collective-permute-start.2 = (bf16[4,64,256]{2,1,0:T(8,128)(2,1)S(1)}, bf16[4,64,256]{2,1,0:T(8,128)(2,1)S(1)}, u32[]{:S(2)}, u32[]{:S(2)}) collective-permute-start(bf16[4,64,256]{2,1,0:T(8,128)(2,1)S(1)} %get-tuple-element.19), channel_id=1, source_target_pairs={{0,1},{1,2},{2,3},{3,4},{4,5},{5,6},{6,7},{7,8},{8,9},{9,10},{10,1... | collective-permute-start | bytes 393224 | tf_op jit(solution)/shard_map/ppermute | solution.py:251
  39.3 16.0 %collective-permute-start.3 = (bf16[4,64,256]{2,1,0:T(8,128)(2,1)S(1)}, bf16[4,64,256]{2,1,0:T(8,128)(2,1)S(1)}, u32[]{:S(2)}, u32[]{:S(2)}) collective-permute-start(bf16[4,64,256]{2,1,0:T(8,128)(2,1)S(1)} %get-tuple-element.20), channel_id=1, source_target_pairs={{1,0},{2,1},{3,2},{4,3},{5,4},{6,5},{7,6},{8,7},{9,8},{10,9},{11,1... | collective-permute-start | bytes 393224 | tf_op jit(solution)/shard_map/ppermute | solution.py:252
  62.5 5.4 %collective-permute-start.4 = (bf16[2,2,64,256]{3,2,1,0:T(8,128)(2,1)S(1)}, bf16[2,2,64,256]{3,2,1,0:T(8,128)(2,1)S(1)}, u32[]{:S(2)}, u32[]{:S(2)}) collective-permute-start(bf16[2,2,64,256]{3,2,1,0:T(8,128)(2,1)S(1)} %get-tuple-element.22), channel_id=1, source_target_pairs={{0,32},{32,0},{64,96},{96,64},{128,160},{160,128},{192,224},{224,1... | collective-permute-start | bytes 393224 | tf_op jit(solution)/shard_map/ppermute | solution.py:275

commit v2 on v1

--- a/solution.py
+++ b/solution.py
@@ -15,8 +15,8 @@
 BF16 = jnp.bfloat16
 VMEM = pl.BlockSpec(memory_space=pltpu.VMEM)
 SMEM = pl.BlockSpec(memory_space=pltpu.SMEM)
-HBM = pl.BlockSpec(memory_space=pl.ANY)
-LIMIT = 40 * 1024 * 1024
+HBM = pl.BlockSpec(memory_space=pltpu.HBM)
+LIMIT = 20 * 1024 * 1024
 
 
 def dot_high(a, b, contract):
@@ -101,12 +101,11 @@
                     act_ref[place, r, :, lanes] = taken
 
 
-def convolve(act_ref, weight_ref, sem, kernel_hbm, acc_ref, frames, height):
+def convolve(act_ref, weight_ref, acc_ref, frames, height):
     columns, width = act_ref.shape[2:]
     rows = frames * height * columns
     for tap in range(9):
         back_step, row_step = divmod(tap, 3)
-        pltpu.make_async_copy(kernel_hbm.at[tap], weight_ref.at[tap], sem.at[tap]).wait()
         slab = act_ref[back_step : back_step + frames, row_step : row_step + height].reshape(rows, width)
         part = jnp.dot(slab, weight_ref[tap], preferred_element_type=F32)
         if tap == 0:
@@ -115,31 +114,43 @@
             acc_ref[...] += part
 
 
-def start_weights(kernel_hbm, weight_ref, sem):
-    for tap in range(9):
-        pltpu.make_async_copy(kernel_hbm.at[tap], weight_ref.at[tap], sem.at[tap]).start()
-
-
-def stats_kernel(frames_ref, field_ref, group_ref, parts_ref, first_ref, last_ref):
-    length = frames_ref[lax.axis_index("tm")]
-    height = field_ref.shape[1]
-    first_ref[...] = field_ref[:, 0]
-    last_ref[...] = field_ref[:, height - 1]
-    row = local_stats(field_ref, length, group_ref[...])
+def in_hbm(array):
+    return pltpu.with_memory_space_constraint(array, pltpu.HBM)
+
+
+def stats_kernel(frames_hbm, rank_hbm, latent_hbm, *rest):
+    rows = len(rest) // 2 - 4
+    rows_hbm, rest = rest[:rows], rest[rows:]
+    parts_ref, first_ref, last_ref, latent_ref, frames_ref, rank_ref = rest[:6]
+    rows_ref, (frames_smem, sem) = rest[6 : 6 + rows], rest[6 + rows :]
+    group_ref = rows_ref[0]
+    pairs = [(frames_hbm, frames_smem), (latent_hbm, latent_ref)]
+    pairs += list(zip(rows_hbm, rows_ref)) + [(frames_hbm, frames_ref), (rank_hbm, rank_ref)]
+    copies = [pltpu.make_async_copy(source, target, sem.at[i]) for i, (source, target) in enumerate(pairs)]
+    for copy in copies:
+        copy.start()
+    for copy in copies[:3]:
+        copy.wait()
+    length = frames_smem[lax.axis_index("tm")]
+    height = latent_ref.shape[1]
+    first_ref[...] = latent_ref[:, 0]
+    last_ref[...] = latent_ref[:, height - 1]
+    row = local_stats(latent_ref, length, group_ref[...])
     parts_ref[...] = jnp.broadcast_to(row[None], parts_ref.shape)
+    for copy in copies[3:]:
+        copy.wait()
 
 
 def first_kernel(
-    frames_ref, parts_ref, field_ref, above_ref, below_ref, group_ref, gain_ref, shift_ref, bias_ref, kernel_hbm,
+    frames_ref, parts_ref, field_ref, above_ref, below_ref, group_ref, gain_ref, shift_ref, bias_ref, weight_ref,
     hidden_ref, out_parts_ref, first_ref, last_ref,
-    weight_ref, act_ref, acc_ref, sem,
+    act_ref, acc_ref,
 ):
-    start_weights(kernel_hbm, weight_ref, sem)
     frames, height, columns, channels = field_ref.shape
     length = frames_ref[lax.axis_index("tm")]
     mean, inverse = combine_stats(parts_ref[:, 0], length, height * columns, group_ref[...])
     activate(field_ref, above_ref, below_ref, act_ref, mean, inverse * gain_ref[...], shift_ref[...])
-    convolve(act_ref, weight_ref, sem, kernel_hbm, acc_ref, frames, height)
+    convolve(act_ref, weight_ref, acc_ref, frames, height)
     hidden = (acc_ref[...] + bias_ref[...]).astype(BF16).reshape(hidden_ref.shape)
     hidden_ref[...] = hidden
     first_ref[...] = hidden_ref[:, 0]
@@ -150,11 +161,10 @@
 
 def second_kernel(
     frames_ref, rank_ref, parts_ref, field_ref, above_ref, below_ref, latent_ref, group_ref, gain_ref, shift_ref,
-    bias_ref, kernel_hbm,
+    bias_ref, weight_ref,
     keep_ref, send_ref,
-    weight_ref, act_ref, acc_ref, sem,
+    act_ref, acc_ref,
 ):
-    start_weights(kernel_hbm, weight_ref, sem)
     frames, height, columns, channels = field_ref.shape
     clip = lax.axis_index("tm")
     core = lax.rem(clip, 2)
@@ -162,7 +172,7 @@
     start = clip_start_of(frames_ref, rank_ref, clip)
     mean, inverse = combine_stats(parts_ref[:, 0], length, height * columns, group_ref[...])
     activate(field_ref, above_ref, below_ref, act_ref, mean, inverse * gain_ref[...], shift_ref[...])
-    convolve(act_ref, weight_ref, sem, kernel_hbm, acc_ref, frames, height)
+    convolve(act_ref, weight_ref, acc_ref, frames, height)
     pixels = height * columns
     for f in range(frames):
         total = acc_ref[f * pixels : (f + 1) * pixels] + bias_ref[...]
@@ -210,7 +220,7 @@
         copy.wait()
 
 
-def call(kernel, in_specs, outs, scratch=(), out_spec=VMEM):
+def call(kernel, in_specs, outs, scratch=(), out_spec=VMEM, cost=None):
     return pl.pallas_call(
         kernel,
         in_specs=in_specs,
@@ -218,6 +228,7 @@
         out_shape=[jax.ShapeDtypeStruct(shape, kind) for shape, kind in outs],
         scratch_shapes=list(scratch),
         compiler_params=pltpu.CompilerParams(vmem_limit_bytes=LIMIT),
+        cost_estimate=cost,
     )
 
 
@@ -253,31 +264,36 @@
         return above, below
 
     work = [
-        pltpu.VMEM((9, 3 * channels, channels), BF16),
         pltpu.VMEM((frames + 2, height + 2, columns, 3 * channels), BF16),
         pltpu.VMEM((frames * height * columns, channels), F32),
-        pltpu.SemaphoreType.DMA((9,)),
     ]
 
-    parts, first, last = call(stats_kernel, [SMEM, VMEM, VMEM], [parts_out, edge, edge])(clip_frames, latent, group_row)
+    vectors = [row(v) for v in (group_of, gain_first, shift_first, bias_first, gain_second, shift_second, bias_second)]
+    outs = [parts_out, edge, edge, (latent.shape, BF16), (clip_frames.shape, jnp.int32), (clip_rank.shape, jnp.int32)]
+    outs += [(v.shape, v.dtype) for v in vectors]
+    parts, first, last, latent, clip_frames, clip_rank, *vectors = call(
+        stats_kernel, [HBM] * (3 + len(vectors)), outs,
+        [pltpu.SMEM(clip_frames.shape, jnp.int32), pltpu.SemaphoreType.DMA((4 + len(vectors),))],
+        cost=pl.CostEstimate(flops=1 << 32, bytes_accessed=1 << 24, transcendentals=0),
+    )(*map(in_hbm, (clip_frames, clip_rank, latent, *vectors)))
+    group_row = vectors[0]
     above, below = halos(first, last)
     parts = gather(parts)
     hidden, parts, first, last = call(
-        first_kernel, [SMEM] + [VMEM] * 8 + [HBM], [(latent.shape, BF16), parts_out, edge, edge], work
-    )(clip_frames, parts, latent, above, below, group_row, row(gain_first), row(shift_first), row(bias_first), taps(conv_first))
+        first_kernel, [SMEM] + [VMEM] * 9, [(latent.shape, BF16), parts_out, edge, edge], work
+    )(clip_frames, parts, latent, above, below, *vectors[:4], taps(conv_first))
     above, below = halos(first, last)
     parts = gather(parts)
     half = ((2, height, columns, channels), BF16)
-    keep, send = call(second_kernel, [SMEM] * 2 + [VMEM] * 9 + [HBM], [half, half], work)(
-        clip_frames, clip_rank, parts, hidden, above, below, latent, group_row, row(gain_second), row(shift_second),
-        row(bias_second), taps(conv_second),
+    keep, send = call(second_kernel, [SMEM] * 2 + [VMEM] * 10, [half, half], work)(
+        clip_frames, clip_rank, parts, hidden, above, below, latent, group_row, *vectors[4:], taps(conv_second),
     )
     got = lax.ppermute(send, "tm", [(i, i ^ 1) for i in range(clips)])
     chips = clips // 2
     (spread,) = call(spread_kernel, [SMEM] * 2 + [VMEM] * 2, [((chips,) + half[0], BF16)])(clip_frames, clip_rank, keep, got)
     groups = [[core + 2 * chip for chip in range(chips)] for core in range(2)]
     spread = lax.all_to_all(spread, "tm", 0, 0, axis_index_groups=groups, tiled=True)
-    (out,) = call(pick_kernel, [SMEM] * 2 + [HBM], [half], [pltpu.SemaphoreType.DMA((2,))], HBM)(clip_frames, clip_rank, spread)
+    (out,) = call(pick_kernel, [SMEM] * 2 + [pl.BlockSpec(memory_space=pl.ANY)], [half], [pltpu.SemaphoreType.DMA((2,))], HBM)(clip_frames, clip_rank, spread)
     return out
 
 

time: 82.8 us -> 69 us (0.83)
  Pallas kernels: 18.5 us -> 11.2 us
  local copies, waits for them, and re-layouts: 6.36 us -> 0.01 us
    pallas_call x4, Pallas kernels: 17.9 us -> 10.6 us  [the longest x1 4.09 us: local(): call(first_kernel, [SMEM] + [VMEM] * 9, [(latent.shape, BF16), parts_out,...]
    unnamed x24 -> x4, local copies, waits for them, and re-layouts: 6.36 us -> 0.01 us
where the time goes in v2:
time: 69 us; the launch traced here: 68.8 us
  blocking collectives  38.5 us (56%)
  starting transfers between devices  18.1 us (26%)
  Pallas kernels  11.2 us (16%)
  waiting for transfers between devices  1 us (1%)
    all_to_all x2, blocking collectives, gather(): return lax.all_to_all(parts, 'space', 0, 0, tiled=True)  25.9 us
    all_to_all x1, blocking collectives, local(): lax.all_to_all(spread, 'tm', 0, 0, axis_index_groups=groups, tiled=True)  12.6 us
    ppermute x2, starting transfers between devices, halos(): lax.ppermute(first, 'space', [((i + 1) % bands, i) for i in range(bands)])  10.7 us
    ppermute x1, starting transfers between devices, local(): got = lax.ppermute(send, 'tm', [(i, i ^ 1) for i in range(clips)])  4.47 us
    pallas_call x1, Pallas kernels, local(): call(first_kernel, [SMEM] + [VMEM] * 9, [(latent.shape, BF16), parts_out,...  4.09 us
    pallas_call x1, Pallas kernels, local(): call(second_kernel, [SMEM] * 2 + [VMEM] * 10, [half, half], work)  3.05 us
    ppermute x2, starting transfers between devices, halos(): lax.ppermute(last, 'space', [(i, (i + 1) % bands) for i in range(bands)])  2.96 us
    pallas_call x1, Pallas kernels, local(): call(stats_kernel, [HBM] * (3 + len(vectors)), outs, [pltpu.SMEM(clip_fra...  2.13 us
  transfers between devices with their start and end apart: 5, of which 1 were waited for; matrix products, arithmetic and copies ran while one was open for 0% of the time, Pallas kernels for 0%

profile of v2, /device:TPU:1, one launch (start us, length us, event | category | flops | bytes accessed | tf_op | source)
XLA Modules:
  0.0 68.8 jit_solution(10911000669199032194)
XLA Ops:
  0.0 0.0 copy-start
  0.0 2.1 %shard_map.118 = (f32[32,1,128]{2,1,0:T(1,128)S(1)}, bf16[4,64,256]{2,1,0:T(8,128)(2,1)S(1)}, bf16[4,64,256]{2,1,0:T(8,128)(2,1)S(1)}, bf16[4,2,64,256]{3,2,1,0:...) custom-call(s32[8]{0:T(128)} %frames_hbm.1, ...), custom_call_target="tpu_custom_call" | custom-call | flops 4294967296 | bytes 16777216 | tf_op jit(solution)/shard_map/pallas_call | solution.py:274
  2.1 0.0 copy-start.1
  2.2 2.5 %collective-permute-start = (bf16[4,64,256]{2,1,0:T(8,128)(2,1)S(1)}, bf16[4,64,256]{2,1,0:T(8,128)(2,1)S(1)}, u32[]{:S(2)}, u32[]{:S(2)}) collective-permute-start(bf16[4,64,256]{2,1,0:T(8,128)(2,1)S(1)} %get-tuple-element.28), channel_id=1, source_target_pairs={{0,1},{1,2},{2,3},{3,4},{4,5},{5,6},{6,7},{7,8},{8,9},{9,10},{10,1... | collective-permute-start | bytes 393224 | tf_op jit(solution)/shard_map/ppermute | solution.py:262
  4.7 6.2 %collective-permute-start.1 = (bf16[4,64,256]{2,1,0:T(8,128)(2,1)S(1)}, bf16[4,64,256]{2,1,0:T(8,128)(2,1)S(1)}, u32[]{:S(2)}, u32[]{:S(2)}) collective-permute-start(bf16[4,64,256]{2,1,0:T(8,128)(2,1)S(1)} %get-tuple-element.29), channel_id=1, source_target_pairs={{1,0},{2,1},{3,2},{4,3},{5,4},{6,5},{7,6},{8,7},{9,8},{10,9},{11,1... | collective-permute-start | bytes 393224 | tf_op jit(solution)/shard_map/ppermute | solution.py:263
  10.9 14.3 %all_to_all.15.parts_ref = f32[32,1,128]{2,1,0:T(1,128)S(1)} all-to-all(f32[32,1,128]{2,1,0:T(1,128)S(1)} %get-tuple-element.26), channel_id=1, replica_groups=mesh['tm'=8,'space'=32] {'space'}, dimensions={0} | all-to-all | bytes 32768 | tf_op jit(solution)/shard_map/all_to_all | solution.py:259
  25.2 0.0 collective-permute-done.above_ref
  25.2 0.0 collective-permute-done.1.below_ref
  25.2 0.0 copy-done
  25.2 4.1 %shard_map.119 = (bf16[4,2,64,256]{3,2,1,0:T(8,128)(2,1)S(1)}, f32[32,1,128]{2,1,0:T(1,128)S(1)}, bf16[4,64,256]{2,1,0:T(8,128)(2,1)S(1)}, bf16[4,64,256]{2,1,0:T(8,128)(2,1)S(1)}) custom-call(s32[8]{0:T(128)S(1)} %get-tuple-element.24.frames_ref, f32[32,1,128]{2,1,0:T(1,128)S(1)} %all_to_all.15.parts_ref, ...), custom_call_target="tpu_custom_call" | custom-call | tf_op jit(solution)/shard_map/pallas_call | solution.py:282
  29.3 0.4 collective-permute-start.2
  29.7 4.4 %collective-permute-start.3 = (bf16[4,64,256]{2,1,0:T(8,128)(2,1)S(1)}, bf16[4,64,256]{2,1,0:T(8,128)(2,1)S(1)}, u32[]{:S(2)}, u32[]{:S(2)}) collective-permute-start(bf16[4,64,256]{2,1,0:T(8,128)(2,1)S(1)} %get-tuple-element.37), channel_id=1, source_target_pairs={{1,0},{2,1},{3,2},{4,3},{5,4},{6,5},{7,6},{8,7},{9,8},{10,9},{11,1... | collective-permute-start | bytes 393224 | tf_op jit(solution)/shard_map/ppermute | solution.py:263
  34.2 11.6 %all_to_all.16.parts_ref = f32[32,1,128]{2,1,0:T(1,128)S(1)} all-to-all(f32[32,1,128]{2,1,0:T(1,128)S(1)} %get-tuple-element.34), channel_id=1, replica_groups=mesh['tm'=8,'space'=32] {'space'}, dimensions={0} | all-to-all | bytes 32768 | tf_op jit(solution)/shard_map/all_to_all | solution.py:259
  45.8 0.0 collective-permute-done.2.above_ref
  45.8 0.0 collective-permute-done.3.below_ref
  45.8 0.0 copy-done.1
  45.8 3.1 %shard_map.120 = (bf16[2,2,64,256]{3,2,1,0:T(8,128)(2,1)S(1)}, bf16[2,2,64,256]{3,2,1,0:T(8,128)(2,1)S(1)}) custom-call(s32[8]{0:T(128)S(1)} %get-tuple-element.24.frames_ref, s32[8]{0:T(128)S(1)} %get-tuple-element.25.rank_ref, f32[32,1,128]{2,1,0:T(1,128)S(1)} %all_to_all.16.parts_ref, bf16[4,2,64,256]{3,2,1,0:T(8,128)(2,1)S(1)} %get-tuple-element.35.field_ref, ...), custom_call_target="tpu_custom_call" | custom-call | tf_op jit(solution)/shard_map/pallas_call | solution.py:288
  48.8 4.5 %collective-permute-start.4 = (bf16[2,2,64,256]{3,2,1,0:T(8,128)(2,1)S(1)}, bf16[2,2,64,256]{3,2,1,0:T(8,128)(2,1)S(1)}, u32[]{:S(2)}, u32[]{:S(2)}) collective-permute-start(bf16[2,2,64,256]{3,2,1,0:T(8,128)(2,1)S(1)} %get-tuple-element.42), channel_id=1, source_target_pairs={{0,32},{32,0},{64,96},{96,64},{128,160},{160,128},{192,224},{224,1... | collective-permute-start | bytes 393224 | tf_op jit(solution)/shard_map/ppermute | solution.py:291
  53.3 1.0 %collective-permute-done.4.got_ref = bf16[2,2,64,256]{3,2,1,0:T(8,128)(2,1)S(1)} collective-permute-done((bf16[2,2,64,256]{3,2,1,0:T(8,128)(2,1)S(1)}, bf16[2,2,64,256]{3,2,1,0:T(8,128)(2,1)S(1)}, u32[]{:S(2)}, u32[]{:S(2)}) %collective-permute-start.4) | collective-permute-done | bytes 131104 | tf_op jit(solution)/shard_map/ppermute | solution.py:291
  54.3 0.6 shard_map.121
  54.9 12.6 %all_to_all.17.got_hbm = bf16[4,2,2,64,256]{4,3,2,1,0:T(8,128)(2,1)S(1)} all-to-all(bf16[4,2,2,64,256]{4,3,2,1,0:T(8,128)(2,1)S(1)} %shard_map.121), channel_id=1, replica_groups={{0,64,128,192},{32,96,160,224},{1,65,129,193},{33,97,161,225},{2,66,130..., dimensions={0} | all-to-all | bytes 1048576 | tf_op jit(solution)/shard_map/all_to_all | solution.py:295
  67.5 1.3 %shard_map.122 = bf16[2,2,64,256]{3,2,1,0:T(8,128)(2,1)} custom-call(s32[8]{0:T(128)S(1)} %get-tuple-element.24.frames_ref, s32[8]{0:T(128)S(1)} %get-tuple-element.25.rank_ref, bf16[4,2,2,64,256]{4,3,2,1,0:T(8,128)(2,1)S(1)} %all_to_all.17.got_hbm), custom_call_target="tpu_custom_call" | custom-call | tf_op jit(solution)/shard_map/pallas_call | solution.py:296
Async XLA Ops:
  0.0 25.2 %copy-start = (bf16[3,3,3,256,256]{4,3,2,1,0:T(8,128)(2,1)S(1)}, bf16[3,3,3,256,256]{4,3,2,1,0:T(8,128)(2,1)}, u32[]{:S(2)}) copy-start(bf16[3,3,3,256,256]{4,3,2,1,0:T(8,128)(2,1)} %param.18) | copy-start | bytes 10616836
  2.1 43.6 %copy-start.1 = (bf16[3,3,3,256,256]{4,3,2,1,0:T(8,128)(2,1)S(1)}, bf16[3,3,3,256,256]{4,3,2,1,0:T(8,128)(2,1)}, u32[]{:S(2)}) copy-start(bf16[3,3,3,256,256]{4,3,2,1,0:T(8,128)(2,1)} %param.22) | copy-start | bytes 10616836
  2.2 23.0 %collective-permute-start = (bf16[4,64,256]{2,1,0:T(8,128)(2,1)S(1)}, bf16[4,64,256]{2,1,0:T(8,128)(2,1)S(1)}, u32[]{:S(2)}, u32[]{:S(2)}) collective-permute-start(bf16[4,64,256]{2,1,0:T(8,128)(2,1)S(1)} %get-tuple-element.28), channel_id=1, source_target_pairs={{0,1},{1,2},{2,3},{3,4},{4,5},{5,6},{6,7},{7,8},{8,9},{9,10},{10,1... | collective-permute-start | bytes 393224 | tf_op jit(solution)/shard_map/ppermute | solution.py:262
  4.7 20.5 %collective-permute-start.1 = (bf16[4,64,256]{2,1,0:T(8,128)(2,1)S(1)}, bf16[4,64,256]{2,1,0:T(8,128)(2,1)S(1)}, u32[]{:S(2)}, u32[]{:S(2)}) collective-permute-start(bf16[4,64,256]{2,1,0:T(8,128)(2,1)S(1)} %get-tuple-element.29), channel_id=1, source_target_pairs={{1,0},{2,1},{3,2},{4,3},{5,4},{6,5},{7,6},{8,7},{9,8},{10,9},{11,1... | collective-permute-start | bytes 393224 | tf_op jit(solution)/shard_map/ppermute | solution.py:263
  29.3 16.5 %collective-permute-start.2 = (bf16[4,64,256]{2,1,0:T(8,128)(2,1)S(1)}, bf16[4,64,256]{2,1,0:T(8,128)(2,1)S(1)}, u32[]{:S(2)}, u32[]{:S(2)}) collective-permute-start(bf16[4,64,256]{2,1,0:T(8,128)(2,1)S(1)} %get-tuple-element.36), channel_id=1, source_target_pairs={{0,1},{1,2},{2,3},{3,4},{4,5},{5,6},{6,7},{7,8},{8,9},{9,10},{10,1... | collective-permute-start | bytes 393224 | tf_op jit(solution)/shard_map/ppermute | solution.py:262
  29.7 16.0 %collective-permute-start.3 = (bf16[4,64,256]{2,1,0:T(8,128)(2,1)S(1)}, bf16[4,64,256]{2,1,0:T(8,128)(2,1)S(1)}, u32[]{:S(2)}, u32[]{:S(2)}) collective-permute-start(bf16[4,64,256]{2,1,0:T(8,128)(2,1)S(1)} %get-tuple-element.37), channel_id=1, source_target_pairs={{1,0},{2,1},{3,2},{4,3},{5,4},{6,5},{7,6},{8,7},{9,8},{10,9},{11,1... | collective-permute-start | bytes 393224 | tf_op jit(solution)/shard_map/ppermute | solution.py:263
  48.8 5.5 %collective-permute-start.4 = (bf16[2,2,64,256]{3,2,1,0:T(8,128)(2,1)S(1)}, bf16[2,2,64,256]{3,2,1,0:T(8,128)(2,1)S(1)}, u32[]{:S(2)}, u32[]{:S(2)}) collective-permute-start(bf16[2,2,64,256]{3,2,1,0:T(8,128)(2,1)S(1)} %get-tuple-element.42), channel_id=1, source_target_pairs={{0,32},{32,0},{64,96},{96,64},{128,160},{160,128},{192,224},{224,1... | collective-permute-start | bytes 393224 | tf_op jit(solution)/shard_map/ppermute | solution.py:291

commit v3 on v2

--- a/solution.py
+++ b/solution.py
@@ -77,41 +77,36 @@
     return spread_back[:1], lax.rsqrt(variance + EPSILON)
 
 
-def activate(field_ref, above_ref, below_ref, act_ref, mean, scale, shift):
-    frames, height, columns, channels = field_ref.shape
-    band = lax.axis_index("space")
-    top = band == 0
-    bottom = band == lax.axis_size("space") - 1
-    for f in range(frames):
-        for r in range(height + 2):
-            if r == 0:
-                value = jnp.where(top, field_ref[f, 0], above_ref[f])
-            elif r == height + 1:
-                value = jnp.where(bottom, field_ref[f, height - 1], below_ref[f])
-            else:
-                value = field_ref[f, r - 1]
-            half = ((value.astype(F32) - mean) * scale + shift) * 0.5
+def activate(rows, act_ref, mean, scale, shift):
+    channels = mean.shape[1]
+    for f in range(act_ref.shape[0]):
+        for r in range(act_ref.shape[1]):
+            half = ((rows(f, r).astype(F32) - mean) * scale + shift) * 0.5
             act = half * jnp.tanh(half) + half
             left = jnp.concatenate([act[:1], act[:-1]], axis=0)
             right = jnp.concatenate([act[1:], act[-1:]], axis=0)
             for step, taken in enumerate((left, act, right)):
-                taken = taken.astype(BF16)
-                lanes = slice(step * channels, (step + 1) * channels)
-                for place in (0, 1, 2) if f == 0 else (f + 2,):
-                    act_ref[place, r, :, lanes] = taken
-
-
-def convolve(act_ref, weight_ref, acc_ref, frames, height):
-    columns, width = act_ref.shape[2:]
-    rows = frames * height * columns
-    for tap in range(9):
-        back_step, row_step = divmod(tap, 3)
-        slab = act_ref[back_step : back_step + frames, row_step : row_step + height].reshape(rows, width)
-        part = jnp.dot(slab, weight_ref[tap], preferred_element_type=F32)
-        if tap == 0:
-            acc_ref[...] = part
-        else:
-            acc_ref[...] += part
+                act_ref[f, r, :, step * channels : (step + 1) * channels] = taken.astype(BF16)
+
+
+def convolve(act_ref, weight_ref, acc_refs):
+    frames, height, columns, width = act_ref.shape
+    height = height - 2
+    for back_step, acc_ref in enumerate(acc_refs):
+        used = frames - 2 + back_step
+        slabs = [act_ref[:used, j : j + height].reshape(used * height * columns, width) for j in range(3)]
+        kernel = weight_ref[3 * back_step : 3 * back_step + 3].reshape(3 * width, -1)
+        part = jnp.dot(jnp.concatenate(slabs, axis=1), kernel, preferred_element_type=F32)
+        acc_ref[...] = part.reshape(acc_ref.shape)
+
+
+def frame_sum(acc_refs, f, zero):
+    return acc_refs[0][max(f - 2, 0) + zero] + acc_refs[1][max(f - 1, 0) + zero] + acc_refs[2][f + zero]
+
+
+def band_ends():
+    band = lax.axis_index("space")
+    return band == 0, band == lax.axis_size("space") - 1
 
 
 def in_hbm(array):
@@ -119,10 +114,10 @@
 
 
 def stats_kernel(frames_hbm, rank_hbm, latent_hbm, *rest):
-    rows = len(rest) // 2 - 4
+    rows = len(rest) // 2 - 3
     rows_hbm, rest = rest[:rows], rest[rows:]
-    parts_ref, first_ref, last_ref, latent_ref, frames_ref, rank_ref = rest[:6]
-    rows_ref, (frames_smem, sem) = rest[6 : 6 + rows], rest[6 + rows :]
+    parts_ref, latent_ref, frames_ref, rank_ref = rest[:4]
+    rows_ref, (frames_smem, sem) = rest[4 : 4 + rows], rest[4 + rows :]
     group_ref = rows_ref[0]
     pairs = [(frames_hbm, frames_smem), (latent_hbm, latent_ref)]
     pairs += list(zip(rows_hbm, rows_ref)) + [(frames_hbm, frames_ref), (rank_hbm, rank_ref)]
@@ -132,9 +127,6 @@
     for copy in copies[:3]:
         copy.wait()
     length = frames_smem[lax.axis_index("tm")]
-    height = latent_ref.shape[1]
-    first_ref[...] = latent_ref[:, 0]
-    last_ref[...] = latent_ref[:, height - 1]
     row = local_stats(latent_ref, length, group_ref[...])
     parts_ref[...] = jnp.broadcast_to(row[None], parts_ref.shape)
     for copy in copies[3:]:
@@ -143,41 +135,58 @@
 
 def first_kernel(
     frames_ref, parts_ref, field_ref, above_ref, below_ref, group_ref, gain_ref, shift_ref, bias_ref, weight_ref,
-    hidden_ref, out_parts_ref, first_ref, last_ref,
-    act_ref, acc_ref,
+    hidden_ref, out_parts_ref,
+    own_ref, act_ref, *acc_refs,
 ):
     frames, height, columns, channels = field_ref.shape
     length = frames_ref[lax.axis_index("tm")]
+    zero = jnp.minimum(length, 0)
+    top, bottom = band_ends()
     mean, inverse = combine_stats(parts_ref[:, 0], length, height * columns, group_ref[...])
-    activate(field_ref, above_ref, below_ref, act_ref, mean, inverse * gain_ref[...], shift_ref[...])
-    convolve(act_ref, weight_ref, acc_ref, frames, height)
-    hidden = (acc_ref[...] + bias_ref[...]).astype(BF16).reshape(hidden_ref.shape)
-    hidden_ref[...] = hidden
-    first_ref[...] = hidden_ref[:, 0]
-    last_ref[...] = hidden_ref[:, height - 1]
-    row = local_stats(hidden_ref, length, group_ref[...])
+
+    def rows(f, r):
+        if r < 2:
+            row = above_ref[f, height - 2 + r]
+            return jnp.where(top, field_ref[f, 0], row) if r == 1 else row
+        if r >= height + 2:
+            row = below_ref[f, r - height - 2]
+            return jnp.where(bottom, field_ref[f, height - 1], row) if r == height + 2 else row
+        return field_ref[f, r - 2]
+
+    activate(rows, act_ref, mean, inverse * gain_ref[...], shift_ref[...])
+    convolve(act_ref, weight_ref, acc_refs)
+    for f in range(frames):
+        hidden = (frame_sum(acc_refs, f, zero) + bias_ref[...]).astype(BF16)
+        hidden_ref[f] = hidden
+        own_ref[f] = hidden[1 : height + 1]
+    row = local_stats(own_ref, length, group_ref[...])
     out_parts_ref[...] = jnp.broadcast_to(row[None], out_parts_ref.shape)
 
 
 def second_kernel(
-    frames_ref, rank_ref, parts_ref, field_ref, above_ref, below_ref, latent_ref, group_ref, gain_ref, shift_ref,
-    bias_ref, weight_ref,
+    frames_ref, rank_ref, parts_ref, hidden_ref, latent_ref, group_ref, gain_ref, shift_ref, bias_ref, weight_ref,
     keep_ref, send_ref,
-    act_ref, acc_ref,
+    act_ref, *acc_refs,
 ):
-    frames, height, columns, channels = field_ref.shape
+    frames, height, columns, channels = latent_ref.shape
     clip = lax.axis_index("tm")
     core = lax.rem(clip, 2)
     length = frames_ref[clip]
+    zero = jnp.minimum(length, 0)
     start = clip_start_of(frames_ref, rank_ref, clip)
+    top, bottom = band_ends()
     mean, inverse = combine_stats(parts_ref[:, 0], length, height * columns, group_ref[...])
-    activate(field_ref, above_ref, below_ref, act_ref, mean, inverse * gain_ref[...], shift_ref[...])
-    convolve(act_ref, weight_ref, acc_ref, frames, height)
-    pixels = height * columns
+
+    def rows(f, r):
+        row = hidden_ref[f, r]
+        if r == 0:
+            return jnp.where(top, hidden_ref[f, 1], row)
+        return jnp.where(bottom, hidden_ref[f, height], row) if r == height + 1 else row
+
+    activate(rows, act_ref, mean, inverse * gain_ref[...], shift_ref[...])
+    convolve(act_ref, weight_ref, acc_refs)
     for f in range(frames):
-        total = acc_ref[f * pixels : (f + 1) * pixels] + bias_ref[...]
-        total = latent_ref[f].astype(F32) + total.reshape(height, columns, channels)
-        total = total.astype(BF16)
+        total = (latent_ref[f].astype(F32) + (frame_sum(acc_refs, f, zero) + bias_ref[...])).astype(BF16)
         place = lax.rem(start + f, 4)
         slot = lax.rem(place, 2)
         stays = place // 2 == core
@@ -252,41 +261,36 @@
     row = lambda v: v.reshape(1, channels)
     taps = lambda k: k.reshape(9, 3 * channels, channels)
     group_row = row(group_of)
-    edge = ((frames, columns, channels), BF16)
     parts_out = ((bands, 1, LANES), F32)
 
     def gather(parts):
         return lax.all_to_all(parts, "space", 0, 0, tiled=True)
 
-    def halos(first, last):
-        above = lax.ppermute(last, "space", [(i, (i + 1) % bands) for i in range(bands)])
-        below = lax.ppermute(first, "space", [((i + 1) % bands, i) for i in range(bands)])
-        return above, below
-
-    work = [
-        pltpu.VMEM((frames + 2, height + 2, columns, 3 * channels), BF16),
-        pltpu.VMEM((frames * height * columns, channels), F32),
-    ]
+    def work(height):
+        accs = [pltpu.VMEM((frames - 2 + i, height, columns, channels), F32) for i in range(3)]
+        return [pltpu.VMEM((frames, height + 2, columns, 3 * channels), BF16)] + accs
 
     vectors = [row(v) for v in (group_of, gain_first, shift_first, bias_first, gain_second, shift_second, bias_second)]
-    outs = [parts_out, edge, edge, (latent.shape, BF16), (clip_frames.shape, jnp.int32), (clip_rank.shape, jnp.int32)]
+    outs = [parts_out, (latent.shape, BF16), (clip_frames.shape, jnp.int32), (clip_rank.shape, jnp.int32)]
     outs += [(v.shape, v.dtype) for v in vectors]
-    parts, first, last, latent, clip_frames, clip_rank, *vectors = call(
+    parts, latent, clip_frames, clip_rank, *vectors = call(
         stats_kernel, [HBM] * (3 + len(vectors)), outs,
         [pltpu.SMEM(clip_frames.shape, jnp.int32), pltpu.SemaphoreType.DMA((4 + len(vectors),))],
         cost=pl.CostEstimate(flops=1 << 32, bytes_accessed=1 << 24, transcendentals=0),
     )(*map(in_hbm, (clip_frames, clip_rank, latent, *vectors)))
     group_row = vectors[0]
-    above, below = halos(first, last)
+    above = lax.ppermute(latent, "space", [(i, (i + 1) % bands) for i in range(bands)])
+    below = lax.ppermute(latent, "space", [((i + 1) % bands, i) for i in range(bands)])
     parts = gather(parts)
-    hidden, parts, first, last = call(
-        first_kernel, [SMEM] + [VMEM] * 9, [(latent.shape, BF16), parts_out, edge, edge], work
+    hidden, parts = call(
+        first_kernel, [SMEM] + [VMEM] * 9,
+        [((frames, height + 2, columns, channels), BF16), parts_out],
+        [pltpu.VMEM(latent.shape, BF16)] + work(height + 2),
     )(clip_frames, parts, latent, above, below, *vectors[:4], taps(conv_first))
-    above, below = halos(first, last)
     parts = gather(parts)
     half = ((2, height, columns, channels), BF16)
-    keep, send = call(second_kernel, [SMEM] * 2 + [VMEM] * 10, [half, half], work)(
-        clip_frames, clip_rank, parts, hidden, above, below, latent, group_row, *vectors[4:], taps(conv_second),
+    keep, send = call(second_kernel, [SMEM] * 2 + [VMEM] * 8, [half, half], work(height))(
+        clip_frames, clip_rank, parts, hidden, latent, group_row, *vectors[4:], taps(conv_second),
     )
     got = lax.ppermute(send, "tm", [(i, i ^ 1) for i in range(clips)])
     chips = clips // 2

time: 69 us -> 64.9 us (0.941)
  starting transfers between devices: 18.1 us -> 12.6 us
  Pallas kernels: 11.2 us -> 12 us
    ppermute x4 -> x2, starting transfers between devices: 13.6 us -> 8.68 us  [the longest x1 8.68 us: local(): lax.ppermute(latent, 'space', [((i + 1) % bands, i) for i in range(bands)])]
    pallas_call x2, Pallas kernels: 7.14 us -> 7.98 us  [the longest x1 5.33 us: local(): call(first_kernel, [SMEM] + [VMEM] * 9, [((frames, height + 2, columns, c...]
  transfers between devices with their start and end apart: 5 -> 3, of which waited for: 1 -> 1; matrix products, arithmetic and copies ran while one was open for 0% -> 0% of each run, Pallas kernels for 0% -> 0%
where the time goes in v3:
time: 64.9 us; the launch traced here: 64.7 us
  blocking collectives  39.1 us (60%)
  starting transfers between devices  12.6 us (19%)
  Pallas kernels  12 us (18%)
  waiting for transfers between devices  0.99 us (2%)
    all_to_all x2, blocking collectives, gather(): return lax.all_to_all(parts, 'space', 0, 0, tiled=True)  26.5 us
    all_to_all x1, blocking collectives, local(): lax.all_to_all(spread, 'tm', 0, 0, axis_index_groups=groups, tiled=True)  12.6 us
    ppermute x1, starting transfers between devices, local(): lax.ppermute(latent, 'space', [((i + 1) % bands, i) for i in range(bands)])  8.68 us
    pallas_call x1, Pallas kernels, local(): call(first_kernel, [SMEM] + [VMEM] * 9, [((frames, height + 2, columns, c...  5.33 us
    ppermute x1, starting transfers between devices, local(): got = lax.ppermute(send, 'tm', [(i, i ^ 1) for i in range(clips)])  3.89 us
    pallas_call x1, Pallas kernels, local(): call(second_kernel, [SMEM] * 2 + [VMEM] * 8, [half, half], work(height))  2.65 us
    pallas_call x1, Pallas kernels, local(): call(stats_kernel, [HBM] * (3 + len(vectors)), outs, [pltpu.SMEM(clip_fra...  2.1 us
  transfers between devices with their start and end apart: 3, of which 1 were waited for; matrix products, arithmetic and copies ran while one was open for 0% of the time, Pallas kernels for 0%

profile of v3, /device:TPU:1, one launch (start us, length us, event | category | flops | bytes accessed | tf_op | source)
XLA Modules:
  0.0 64.7 jit_solution(7494425276955013825)
XLA Ops:
  0.0 0.0 copy-start
  0.0 2.1 %shard_map.118 = (f32[32,1,128]{2,1,0:T(1,128)S(1)}, bf16[4,2,64,256]{3,2,1,0:T(8,128)(2,1)S(1)}, s32[8]{0:T(128)S(1)}, s32[8]{0:T(128)S(1)}, s32[1,256]{1,0:T(1...) custom-call(s32[8]{0:T(128)} %frames_hbm.1, ...), custom_call_target="tpu_custom_call" | custom-call | flops 4294967296 | bytes 16777216 | tf_op jit(solution)/shard_map/pallas_call | solution.py:276
  2.1 0.0 copy-start.1
  2.1 8.7 %collective-permute-start.1 = (bf16[4,2,64,256]{3,2,1,0:T(8,128)(2,1)S(1)}, bf16[4,2,64,256]{3,2,1,0:T(8,128)(2,1)S(1)}, u32[]{:S(2)}, u32[]{:S(2)}) collective-permute-start(bf16[4,2,64,256]{3,2,1,0:T(8,128)(2,1)S(1)} %get-tuple-element.23.field_ref.latent_ref), channel_id=1, source_target_pairs={{1,0},{2,1},{3,2},{4,3},{5,4},{6,5},{7,6},{8,7},{9,8},{10,9},{11,1... | collective-permute-start | bytes 786440 | tf_op jit(solution)/shard_map/ppermute | solution.py:283
  10.8 0.0 collective-permute-start
  10.8 14.9 %all_to_all.15.parts_ref = f32[32,1,128]{2,1,0:T(1,128)S(1)} all-to-all(f32[32,1,128]{2,1,0:T(1,128)S(1)} %get-tuple-element.22), channel_id=1, replica_groups=mesh['tm'=8,'space'=32] {'space'}, dimensions={0} | all-to-all | bytes 32768 | tf_op jit(solution)/shard_map/all_to_all | solution.py:267
  25.7 0.0 collective-permute-done.1.below_ref
  25.7 0.0 collective-permute-done.above_ref
  25.7 0.0 copy-done
  25.7 5.3 %shard_map.119 = (bf16[4,4,64,256]{3,2,1,0:T(8,128)(2,1)S(1)}, f32[32,1,128]{2,1,0:T(1,128)S(1)}) custom-call(s32[8]{0:T(128)S(1)} %get-tuple-element.20.frames_ref, f32[32,1,128]{2,1,0:T(1,128)S(1)} %all_to_all.15.parts_ref, bf16[4,2,64,256]{3,2,1,0:T(8,128)(2,1)S(1)} %get-tuple-element.23.field_ref.latent_ref, ...), custom_call_target="tpu_custom_call" | custom-call | tf_op jit(solution)/shard_map/pallas_call | solution.py:285
  31.0 11.6 %all_to_all.16.parts_ref = f32[32,1,128]{2,1,0:T(1,128)S(1)} all-to-all(f32[32,1,128]{2,1,0:T(1,128)S(1)} %get-tuple-element.28), channel_id=1, replica_groups=mesh['tm'=8,'space'=32] {'space'}, dimensions={0} | all-to-all | bytes 32768 | tf_op jit(solution)/shard_map/all_to_all | solution.py:267
  42.6 0.0 copy-done.1
  42.6 2.7 %shard_map.120 = (bf16[2,2,64,256]{3,2,1,0:T(8,128)(2,1)S(1)}, bf16[2,2,64,256]{3,2,1,0:T(8,128)(2,1)S(1)}) custom-call(s32[8]{0:T(128)S(1)} %get-tuple-element.20.frames_ref, s32[8]{0:T(128)S(1)} %get-tuple-element.21.rank_ref, f32[32,1,128]{2,1,0:T(1,128)S(1)} %all_to_all.16.parts_ref, bf16[4,4,64,256]{3,2,1,0:T(8,128)(2,1)S(1)} %get-tuple-element.29.hidden_ref, ...), custom_call_target="tpu_custom_call" | custom-call | tf_op jit(solution)/shard_map/pallas_call | solution.py:292
  45.3 3.9 %collective-permute-start.2 = (bf16[2,2,64,256]{3,2,1,0:T(8,128)(2,1)S(1)}, bf16[2,2,64,256]{3,2,1,0:T(8,128)(2,1)S(1)}, u32[]{:S(2)}, u32[]{:S(2)}) collective-permute-start(bf16[2,2,64,256]{3,2,1,0:T(8,128)(2,1)S(1)} %get-tuple-element.34), channel_id=1, source_target_pairs={{0,32},{32,0},{64,96},{96,64},{128,160},{160,128},{192,224},{224,1... | collective-permute-start | bytes 393224 | tf_op jit(solution)/shard_map/ppermute | solution.py:295
  49.2 1.0 %collective-permute-done.2.got_ref = bf16[2,2,64,256]{3,2,1,0:T(8,128)(2,1)S(1)} collective-permute-done((bf16[2,2,64,256]{3,2,1,0:T(8,128)(2,1)S(1)}, bf16[2,2,64,256]{3,2,1,0:T(8,128)(2,1)S(1)}, u32[]{:S(2)}, u32[]{:S(2)}) %collective-permute-start.2) | collective-permute-done | bytes 131104 | tf_op jit(solution)/shard_map/ppermute | solution.py:295
  50.2 0.6 shard_map.121
  50.8 12.6 %all_to_all.17.got_hbm = bf16[4,2,2,64,256]{4,3,2,1,0:T(8,128)(2,1)S(1)} all-to-all(bf16[4,2,2,64,256]{4,3,2,1,0:T(8,128)(2,1)S(1)} %shard_map.121), channel_id=1, replica_groups={{0,64,128,192},{32,96,160,224},{1,65,129,193},{33,97,161,225},{2,66,130..., dimensions={0} | all-to-all | bytes 1048576 | tf_op jit(solution)/shard_map/all_to_all | solution.py:299
  63.4 1.3 %shard_map.122 = bf16[2,2,64,256]{3,2,1,0:T(8,128)(2,1)} custom-call(s32[8]{0:T(128)S(1)} %get-tuple-element.20.frames_ref, s32[8]{0:T(128)S(1)} %get-tuple-element.21.rank_ref, bf16[4,2,2,64,256]{4,3,2,1,0:T(8,128)(2,1)S(1)} %all_to_all.17.got_hbm), custom_call_target="tpu_custom_call" | custom-call | tf_op jit(solution)/shard_map/pallas_call | solution.py:300
Async XLA Ops:
  0.0 25.7 %copy-start = (bf16[3,3,3,256,256]{4,3,2,1,0:T(8,128)(2,1)S(1)}, bf16[3,3,3,256,256]{4,3,2,1,0:T(8,128)(2,1)}, u32[]{:S(2)}) copy-start(bf16[3,3,3,256,256]{4,3,2,1,0:T(8,128)(2,1)} %param.18) | copy-start | bytes 10616836
  2.1 40.5 %copy-start.1 = (bf16[3,3,3,256,256]{4,3,2,1,0:T(8,128)(2,1)S(1)}, bf16[3,3,3,256,256]{4,3,2,1,0:T(8,128)(2,1)}, u32[]{:S(2)}) copy-start(bf16[3,3,3,256,256]{4,3,2,1,0:T(8,128)(2,1)} %param.22) | copy-start | bytes 10616836
  2.1 23.6 %collective-permute-start.1 = (bf16[4,2,64,256]{3,2,1,0:T(8,128)(2,1)S(1)}, bf16[4,2,64,256]{3,2,1,0:T(8,128)(2,1)S(1)}, u32[]{:S(2)}, u32[]{:S(2)}) collective-permute-start(bf16[4,2,64,256]{3,2,1,0:T(8,128)(2,1)S(1)} %get-tuple-element.23.field_ref.latent_ref), channel_id=1, source_target_pairs={{1,0},{2,1},{3,2},{4,3},{5,4},{6,5},{7,6},{8,7},{9,8},{10,9},{11,1... | collective-permute-start | bytes 786440 | tf_op jit(solution)/shard_map/ppermute | solution.py:283
  10.8 14.9 %collective-permute-start = (bf16[4,2,64,256]{3,2,1,0:T(8,128)(2,1)S(1)}, bf16[4,2,64,256]{3,2,1,0:T(8,128)(2,1)S(1)}, u32[]{:S(2)}, u32[]{:S(2)}) collective-permute-start(bf16[4,2,64,256]{3,2,1,0:T(8,128)(2,1)S(1)} %get-tuple-element.23.field_ref.latent_ref), channel_id=1, source_target_pairs={{0,1},{1,2},{2,3},{3,4},{4,5},{5,6},{6,7},{7,8},{8,9},{9,10},{10,1... | collective-permute-start | bytes 786440 | tf_op jit(solution)/shard_map/ppermute | solution.py:282
  45.3 4.9 %collective-permute-start.2 = (bf16[2,2,64,256]{3,2,1,0:T(8,128)(2,1)S(1)}, bf16[2,2,64,256]{3,2,1,0:T(8,128)(2,1)S(1)}, u32[]{:S(2)}, u32[]{:S(2)}) collective-permute-start(bf16[2,2,64,256]{3,2,1,0:T(8,128)(2,1)S(1)} %get-tuple-element.34), channel_id=1, source_target_pairs={{0,32},{32,0},{64,96},{96,64},{128,160},{160,128},{192,224},{224,1... | collective-permute-start | bytes 393224 | tf_op jit(solution)/shard_map/ppermute | solution.py:295

commit v4 on v3

--- a/solution.py
+++ b/solution.py
@@ -270,6 +270,8 @@
         accs = [pltpu.VMEM((frames - 2 + i, height, columns, channels), F32) for i in range(3)]
         return [pltpu.VMEM((frames, height + 2, columns, 3 * channels), BF16)] + accs
 
+    above = lax.ppermute(latent, "space", [(i, (i + 1) % bands) for i in range(bands)])
+    below = lax.ppermute(latent, "space", [((i + 1) % bands, i) for i in range(bands)])
     vectors = [row(v) for v in (group_of, gain_first, shift_first, bias_first, gain_second, shift_second, bias_second)]
     outs = [parts_out, (latent.shape, BF16), (clip_frames.shape, jnp.int32), (clip_rank.shape, jnp.int32)]
     outs += [(v.shape, v.dtype) for v in vectors]
@@ -279,8 +281,6 @@
         cost=pl.CostEstimate(flops=1 << 32, bytes_accessed=1 << 24, transcendentals=0),
     )(*map(in_hbm, (clip_frames, clip_rank, latent, *vectors)))
     group_row = vectors[0]
-    above = lax.ppermute(latent, "space", [(i, (i + 1) % bands) for i in range(bands)])
-    below = lax.ppermute(latent, "space", [((i + 1) % bands, i) for i in range(bands)])
     parts = gather(parts)
     hidden, parts = call(
         first_kernel, [SMEM] + [VMEM] * 9,

time: 64.9 us -> 65.1 us (level)
  transfers between devices with their start and end apart: 3 -> 3, of which waited for: 1 -> 1; matrix products, arithmetic and copies ran while one was open for 0% -> 0% of each run, Pallas kernels for 0% -> 3%
where the time goes in v4:
time: 65.1 us; the launch traced here: 64.9 us
  blocking collectives  39.4 us (61%)
  starting transfers between devices  12.5 us (19%)
  Pallas kernels  12 us (18%)
  waiting for transfers between devices  0.99 us (2%)
    all_to_all x2, blocking collectives, gather(): return lax.all_to_all(parts, 'space', 0, 0, tiled=True)  26.8 us
    all_to_all x1, blocking collectives, local(): lax.all_to_all(spread, 'tm', 0, 0, axis_index_groups=groups, tiled=True)  12.6 us
    ppermute x1, starting transfers between devices, local(): lax.ppermute(latent, 'space', [((i + 1) % bands, i) for i in range(bands)])  8.6 us
    pallas_call x1, Pallas kernels, local(): call(first_kernel, [SMEM] + [VMEM] * 9, [((frames, height + 2, columns, c...  5.33 us
    ppermute x1, starting transfers between devices, local(): got = lax.ppermute(send, 'tm', [(i, i ^ 1) for i in range(clips)])  3.89 us
    pallas_call x1, Pallas kernels, local(): call(second_kernel, [SMEM] * 2 + [VMEM] * 8, [half, half], work(height))  2.66 us
    pallas_call x1, Pallas kernels, local(): call(stats_kernel, [HBM] * (3 + len(vectors)), outs, [pltpu.SMEM(clip_fra...  2.1 us
  transfers between devices with their start and end apart: 3, of which 1 were waited for; matrix products, arithmetic and copies ran while one was open for 0% of the time, Pallas kernels for 3%

profile of v4, /device:TPU:1, one launch (start us, length us, event | category | flops | bytes accessed | tf_op | source)
XLA Modules:
  0.0 64.9 jit_solution(3850874571798126233)
XLA Ops:
  0.0 8.6 %collective-permute-start.1 = (bf16[4,2,64,256]{3,2,1,0:T(8,128)(2,1)}, bf16[4,2,64,256]{3,2,1,0:T(8,128)(2,1)S(1)}, u32[]{:S(2)}, u32[]{:S(2)}) collective-permute-start(bf16[4,2,64,256]{3,2,1,0:T(8,128)(2,1)} %latent_hbm.1), channel_id=1, source_target_pairs={{1,0},{2,1},{3,2},{4,3},{5,4},{6,5},{7,6},{8,7},{9,8},{10,9},{11,1... | collective-permute-start | bytes 786440 | tf_op jit(solution)/shard_map/ppermute | solution.py:274
  8.6 0.0 collective-permute-start
  8.6 0.0 copy-start
  8.6 2.1 %shard_map.118 = (f32[32,1,128]{2,1,0:T(1,128)S(1)}, bf16[4,2,64,256]{3,2,1,0:T(8,128)(2,1)S(1)}, s32[8]{0:T(128)S(1)}, s32[8]{0:T(128)S(1)}, s32[1,256]{1,0:T(1...) custom-call(s32[8]{0:T(128)} %frames_hbm.1, ...), custom_call_target="tpu_custom_call" | custom-call | flops 4294967296 | bytes 16777216 | tf_op jit(solution)/shard_map/pallas_call | solution.py:278
  10.7 0.0 copy-start.1
  10.7 15.2 %all_to_all.15.parts_ref = f32[32,1,128]{2,1,0:T(1,128)S(1)} all-to-all(f32[32,1,128]{2,1,0:T(1,128)S(1)} %get-tuple-element.22), channel_id=1, replica_groups=mesh['tm'=8,'space'=32] {'space'}, dimensions={0} | all-to-all | bytes 32768 | tf_op jit(solution)/shard_map/all_to_all | solution.py:267
  25.9 0.0 collective-permute-done.1.below_ref
  25.9 0.0 collective-permute-done.above_ref
  25.9 0.0 copy-done
  25.9 5.3 %shard_map.119 = (bf16[4,4,64,256]{3,2,1,0:T(8,128)(2,1)S(1)}, f32[32,1,128]{2,1,0:T(1,128)S(1)}) custom-call(s32[8]{0:T(128)S(1)} %get-tuple-element.20.frames_ref, f32[32,1,128]{2,1,0:T(1,128)S(1)} %all_to_all.15.parts_ref, bf16[4,2,64,256]{3,2,1,0:T(8,128)(2,1)S(1)} %get-tuple-element.23.field_ref.latent_ref, ...), custom_call_target="tpu_custom_call" | custom-call | tf_op jit(solution)/shard_map/pallas_call | solution.py:285
  31.2 11.6 %all_to_all.16.parts_ref = f32[32,1,128]{2,1,0:T(1,128)S(1)} all-to-all(f32[32,1,128]{2,1,0:T(1,128)S(1)} %get-tuple-element.28), channel_id=1, replica_groups=mesh['tm'=8,'space'=32] {'space'}, dimensions={0} | all-to-all | bytes 32768 | tf_op jit(solution)/shard_map/all_to_all | solution.py:267
  42.8 0.0 copy-done.1
  42.8 2.7 %shard_map.120 = (bf16[2,2,64,256]{3,2,1,0:T(8,128)(2,1)S(1)}, bf16[2,2,64,256]{3,2,1,0:T(8,128)(2,1)S(1)}) custom-call(s32[8]{0:T(128)S(1)} %get-tuple-element.20.frames_ref, s32[8]{0:T(128)S(1)} %get-tuple-element.21.rank_ref, f32[32,1,128]{2,1,0:T(1,128)S(1)} %all_to_all.16.parts_ref, bf16[4,4,64,256]{3,2,1,0:T(8,128)(2,1)S(1)} %get-tuple-element.29.hidden_ref, ...), custom_call_target="tpu_custom_call" | custom-call | tf_op jit(solution)/shard_map/pallas_call | solution.py:292
  45.5 3.9 %collective-permute-start.2 = (bf16[2,2,64,256]{3,2,1,0:T(8,128)(2,1)S(1)}, bf16[2,2,64,256]{3,2,1,0:T(8,128)(2,1)S(1)}, u32[]{:S(2)}, u32[]{:S(2)}) collective-permute-start(bf16[2,2,64,256]{3,2,1,0:T(8,128)(2,1)S(1)} %get-tuple-element.34), channel_id=1, source_target_pairs={{0,32},{32,0},{64,96},{96,64},{128,160},{160,128},{192,224},{224,1... | collective-permute-start | bytes 393224 | tf_op jit(solution)/shard_map/ppermute | solution.py:295
  49.4 1.0 %collective-permute-done.2.got_ref = bf16[2,2,64,256]{3,2,1,0:T(8,128)(2,1)S(1)} collective-permute-done((bf16[2,2,64,256]{3,2,1,0:T(8,128)(2,1)S(1)}, bf16[2,2,64,256]{3,2,1,0:T(8,128)(2,1)S(1)}, u32[]{:S(2)}, u32[]{:S(2)}) %collective-permute-start.2) | collective-permute-done | bytes 131104 | tf_op jit(solution)/shard_map/ppermute | solution.py:295
  50.4 0.6 shard_map.121
  51.0 12.6 %all_to_all.17.got_hbm = bf16[4,2,2,64,256]{4,3,2,1,0:T(8,128)(2,1)S(1)} all-to-all(bf16[4,2,2,64,256]{4,3,2,1,0:T(8,128)(2,1)S(1)} %shard_map.121), channel_id=1, replica_groups={{0,64,128,192},{32,96,160,224},{1,65,129,193},{33,97,161,225},{2,66,130..., dimensions={0} | all-to-all | bytes 1048576 | tf_op jit(solution)/shard_map/all_to_all | solution.py:299
  63.6 1.3 %shard_map.122 = bf16[2,2,64,256]{3,2,1,0:T(8,128)(2,1)} custom-call(s32[8]{0:T(128)S(1)} %get-tuple-element.20.frames_ref, s32[8]{0:T(128)S(1)} %get-tuple-element.21.rank_ref, bf16[4,2,2,64,256]{4,3,2,1,0:T(8,128)(2,1)S(1)} %all_to_all.17.got_hbm), custom_call_target="tpu_custom_call" | custom-call | tf_op jit(solution)/shard_map/pallas_call | solution.py:300
Async XLA Ops:
  0.0 25.9 %collective-permute-start.1 = (bf16[4,2,64,256]{3,2,1,0:T(8,128)(2,1)}, bf16[4,2,64,256]{3,2,1,0:T(8,128)(2,1)S(1)}, u32[]{:S(2)}, u32[]{:S(2)}) collective-permute-start(bf16[4,2,64,256]{3,2,1,0:T(8,128)(2,1)} %latent_hbm.1), channel_id=1, source_target_pairs={{1,0},{2,1},{3,2},{4,3},{5,4},{6,5},{7,6},{8,7},{9,8},{10,9},{11,1... | collective-permute-start | bytes 786440 | tf_op jit(solution)/shard_map/ppermute | solution.py:274
  8.6 17.3 %collective-permute-start = (bf16[4,2,64,256]{3,2,1,0:T(8,128)(2,1)}, bf16[4,2,64,256]{3,2,1,0:T(8,128)(2,1)S(1)}, u32[]{:S(2)}, u32[]{:S(2)}) collective-permute-start(bf16[4,2,64,256]{3,2,1,0:T(8,128)(2,1)} %latent_hbm.1), channel_id=1, source_target_pairs={{0,1},{1,2},{2,3},{3,4},{4,5},{5,6},{6,7},{7,8},{8,9},{9,10},{10,1... | collective-permute-start | bytes 786440 | tf_op jit(solution)/shard_map/ppermute | solution.py:273
  8.6 17.3 %copy-start = (bf16[3,3,3,256,256]{4,3,2,1,0:T(8,128)(2,1)S(1)}, bf16[3,3,3,256,256]{4,3,2,1,0:T(8,128)(2,1)}, u32[]{:S(2)}) copy-start(bf16[3,3,3,256,256]{4,3,2,1,0:T(8,128)(2,1)} %param.18) | copy-start | bytes 10616836
  10.7 32.1 %copy-start.1 = (bf16[3,3,3,256,256]{4,3,2,1,0:T(8,128)(2,1)S(1)}, bf16[3,3,3,256,256]{4,3,2,1,0:T(8,128)(2,1)}, u32[]{:S(2)}) copy-start(bf16[3,3,3,256,256]{4,3,2,1,0:T(8,128)(2,1)} %param.22) | copy-start | bytes 10616836
  45.5 4.9 %collective-permute-start.2 = (bf16[2,2,64,256]{3,2,1,0:T(8,128)(2,1)S(1)}, bf16[2,2,64,256]{3,2,1,0:T(8,128)(2,1)S(1)}, u32[]{:S(2)}, u32[]{:S(2)}) collective-permute-start(bf16[2,2,64,256]{3,2,1,0:T(8,128)(2,1)S(1)} %get-tuple-element.34), channel_id=1, source_target_pairs={{0,32},{32,0},{64,96},{96,64},{128,160},{160,128},{192,224},{224,1... | collective-permute-start | bytes 393224 | tf_op jit(solution)/shard_map/ppermute | solution.py:295

commit v5 on v4

--- a/solution.py
+++ b/solution.py
@@ -16,6 +16,7 @@
 VMEM = pl.BlockSpec(memory_space=pltpu.VMEM)
 SMEM = pl.BlockSpec(memory_space=pltpu.SMEM)
 HBM = pl.BlockSpec(memory_space=pltpu.HBM)
+ANY = pl.BlockSpec(memory_space=pl.ANY)
 LIMIT = 20 * 1024 * 1024
 
 
@@ -200,31 +201,37 @@
             send_ref[slot] = total
 
 
-def spread_kernel(frames_ref, rank_ref, keep_ref, got_ref, out_ref):
+def spread_kernel(frames_ref, rank_ref, keep_ref, got_ref, *out_refs):
     clip = lax.axis_index("tm")
     core = lax.rem(clip, 2)
+    chips = len(out_refs)
     other = clip + 1 - 2 * core
     start = clip_start_of(frames_ref, rank_ref, other)
     length = frames_ref[other]
-    for chip in range(out_ref.shape[0]):
+    for step, out_ref in enumerate(out_refs):
+        chip = lax.rem(clip // 2 + step, chips)
         for slot in range(2):
             place = 4 * chip + 2 * core + slot - start
             theirs = (place >= 0) & (place < length)
-            out_ref[chip, slot] = jnp.where(theirs, got_ref[slot], keep_ref[slot])
-
-
-def pick_kernel(frames_ref, rank_ref, got_hbm, out_hbm, sem):
+            out_ref[slot] = jnp.where(theirs, got_ref[slot], keep_ref[slot])
+
+
+def pick_kernel(frames_ref, rank_ref, *rest):
+    *got_refs, out_hbm, sem = rest
     clip = lax.axis_index("tm")
+    chips = len(got_refs)
+    starts = [clip_start_of(frames_ref, rank_ref, k) for k in range(frames_ref.shape[0])]
     copies = []
     for slot in range(2):
         place = 2 * clip + slot
         source = jnp.int32(0)
-        for k in range(frames_ref.shape[0]):
-            offset = place - clip_start_of(frames_ref, rank_ref, k)
-            source = source + jnp.where((offset >= 0) & (offset < frames_ref[k]), k // 2, 0)
-        copies.append(pltpu.make_async_copy(got_hbm.at[source, slot], out_hbm.at[slot], sem.at[slot]))
-    for copy in copies:
-        copy.start()
+        for k, start in enumerate(starts):
+            source = source + jnp.where((place >= start) & (place < start + frames_ref[k]), k // 2, 0)
+        step = lax.rem(clip // 2 - source + chips, chips)
+        for k, got_ref in enumerate(got_refs):
+            copy = pltpu.make_async_copy(got_ref.at[slot], out_hbm.at[slot], sem.at[slot])
+            pl.when(step == k)(copy.start)
+        copies.append(copy)
     for copy in copies:
         copy.wait()
 
@@ -294,10 +301,13 @@
     )
     got = lax.ppermute(send, "tm", [(i, i ^ 1) for i in range(clips)])
     chips = clips // 2
-    (spread,) = call(spread_kernel, [SMEM] * 2 + [VMEM] * 2, [((chips,) + half[0], BF16)])(clip_frames, clip_rank, keep, got)
-    groups = [[core + 2 * chip for chip in range(chips)] for core in range(2)]
-    spread = lax.all_to_all(spread, "tm", 0, 0, axis_index_groups=groups, tiled=True)
-    (out,) = call(pick_kernel, [SMEM] * 2 + [pl.BlockSpec(memory_space=pl.ANY)], [half], [pltpu.SemaphoreType.DMA((2,))], HBM)(clip_frames, clip_rank, spread)
+    got = list(call(spread_kernel, [SMEM] * 2 + [VMEM] * 2, [half] * chips)(clip_frames, clip_rank, keep, got))
+    for step in range(1, chips):
+        along = [(i, (i + 2 * step) % clips) for i in range(clips)]
+        got[step] = lax.ppermute(got[step], "tm", along)
+    (out,) = call(pick_kernel, [SMEM] * 2 + [ANY] * chips, [half], [pltpu.SemaphoreType.DMA((2,))], HBM)(
+        clip_frames, clip_rank, *got
+    )
     return out
 
 

time: 65.1 us -> 62.5 us (0.960)
  blocking collectives: 39.4 us -> 26.8 us
  starting transfers between devices: 12.5 us -> 17.6 us
  waiting for transfers between devices: 0.99 us -> 5.99 us
    all_to_all x1 -> x0, blocking collectives: 12.6 us -> none  [local(): lax.all_to_all(spread, 'tm', 0, 0, axis_index_groups=groups, tiled=True)]
    ppermute x0 -> x3, starting transfers between devices: none -> 5.06 us  [local(): got[step] = lax.ppermute(got[step], 'tm', along)]
    ppermute x0 -> x3, waiting for transfers between devices: none -> 5 us  [local(): got[step] = lax.ppermute(got[step], 'tm', along)]
  transfers between devices with their start and end apart: 3 -> 6, of which waited for: 1 -> 3; matrix products, arithmetic and copies ran while one was open for 0% -> 0% of each run, Pallas kernels for 3% -> 3%
where the time goes in v5:
time: 62.5 us; the launch traced here: 62.3 us
  blocking collectives  26.8 us (43%)
  starting transfers between devices  17.6 us (28%)
  Pallas kernels  12 us (19%)
  waiting for transfers between devices  5.99 us (10%)
    all_to_all x2, blocking collectives, gather(): return lax.all_to_all(parts, 'space', 0, 0, tiled=True)  26.8 us
    ppermute x1, starting transfers between devices, local(): lax.ppermute(latent, 'space', [((i + 1) % bands, i) for i in range(bands)])  8.6 us
    pallas_call x1, Pallas kernels, local(): call(first_kernel, [SMEM] + [VMEM] * 9, [((frames, height + 2, columns, c...  5.33 us
    ppermute x3, starting transfers between devices, local(): got[step] = lax.ppermute(got[step], 'tm', along)  5.06 us
    ppermute x3, waiting for transfers between devices, local(): got[step] = lax.ppermute(got[step], 'tm', along)  5 us
    ppermute x1, starting transfers between devices, local(): got = lax.ppermute(send, 'tm', [(i, i ^ 1) for i in range(clips)])  3.89 us
    pallas_call x1, Pallas kernels, local(): call(second_kernel, [SMEM] * 2 + [VMEM] * 8, [half, half], work(height))  2.66 us
    pallas_call x1, Pallas kernels, local(): call(stats_kernel, [HBM] * (3 + len(vectors)), outs, [pltpu.SMEM(clip_fra...  2.1 us
  transfers between devices with their start and end apart: 6, of which 3 were waited for; matrix products, arithmetic and copies ran while one was open for 0% of the time, Pallas kernels for 3%

profile of v5, /device:TPU:1, one launch (start us, length us, event | category | flops | bytes accessed | tf_op | source)
XLA Modules:
  0.0 62.3 jit_solution(16303747882807097919)
XLA Ops:
  0.0 8.6 %collective-permute-start.1 = (bf16[4,2,64,256]{3,2,1,0:T(8,128)(2,1)}, bf16[4,2,64,256]{3,2,1,0:T(8,128)(2,1)S(1)}, u32[]{:S(2)}, u32[]{:S(2)}) collective-permute-start(bf16[4,2,64,256]{3,2,1,0:T(8,128)(2,1)} %latent_hbm.1), channel_id=1, source_target_pairs={{1,0},{2,1},{3,2},{4,3},{5,4},{6,5},{7,6},{8,7},{9,8},{10,9},{11,1... | collective-permute-start | bytes 786440 | tf_op jit(solution)/shard_map/ppermute | solution.py:281
  8.6 0.0 collective-permute-start
  8.6 0.0 copy-start
  8.6 2.1 %shard_map.118 = (f32[32,1,128]{2,1,0:T(1,128)S(1)}, bf16[4,2,64,256]{3,2,1,0:T(8,128)(2,1)S(1)}, s32[8]{0:T(128)S(1)}, s32[8]{0:T(128)S(1)}, s32[1,256]{1,0:T(1...) custom-call(s32[8]{0:T(128)} %frames_hbm.1, ...), custom_call_target="tpu_custom_call" | custom-call | flops 4294967296 | bytes 16777216 | tf_op jit(solution)/shard_map/pallas_call | solution.py:285
  10.7 0.0 copy-start.1
  10.7 15.2 %all_to_all.10.parts_ref = f32[32,1,128]{2,1,0:T(1,128)S(1)} all-to-all(f32[32,1,128]{2,1,0:T(1,128)S(1)} %get-tuple-element.26), channel_id=1, replica_groups=mesh['tm'=8,'space'=32] {'space'}, dimensions={0} | all-to-all | bytes 32768 | tf_op jit(solution)/shard_map/all_to_all | solution.py:274
  25.9 0.0 collective-permute-done.1.below_ref
  25.9 0.0 collective-permute-done.above_ref
  25.9 0.0 copy-done
  25.9 5.3 %shard_map.119 = (bf16[4,4,64,256]{3,2,1,0:T(8,128)(2,1)S(1)}, f32[32,1,128]{2,1,0:T(1,128)S(1)}) custom-call(s32[8]{0:T(128)S(1)} %get-tuple-element.24.frames_ref, f32[32,1,128]{2,1,0:T(1,128)S(1)} %all_to_all.10.parts_ref, bf16[4,2,64,256]{3,2,1,0:T(8,128)(2,1)S(1)} %get-tuple-element.27.field_ref.latent_ref, ...), custom_call_target="tpu_custom_call" | custom-call | tf_op jit(solution)/shard_map/pallas_call | solution.py:292
  31.2 11.6 %all_to_all.11.parts_ref = f32[32,1,128]{2,1,0:T(1,128)S(1)} all-to-all(f32[32,1,128]{2,1,0:T(1,128)S(1)} %get-tuple-element.32), channel_id=1, replica_groups=mesh['tm'=8,'space'=32] {'space'}, dimensions={0} | all-to-all | bytes 32768 | tf_op jit(solution)/shard_map/all_to_all | solution.py:274
  42.8 0.0 copy-done.1
  42.8 2.7 %shard_map.120 = (bf16[2,2,64,256]{3,2,1,0:T(8,128)(2,1)S(1)}, bf16[2,2,64,256]{3,2,1,0:T(8,128)(2,1)S(1)}) custom-call(s32[8]{0:T(128)S(1)} %get-tuple-element.24.frames_ref, s32[8]{0:T(128)S(1)} %get-tuple-element.25.rank_ref, f32[32,1,128]{2,1,0:T(1,128)S(1)} %all_to_all.11.parts_ref, bf16[4,4,64,256]{3,2,1,0:T(8,128)(2,1)S(1)} %get-tuple-element.33.hidden_ref, ...), custom_call_target="tpu_custom_call" | custom-call | tf_op jit(solution)/shard_map/pallas_call | solution.py:299
  45.5 3.9 %collective-permute-start.2 = (bf16[2,2,64,256]{3,2,1,0:T(8,128)(2,1)S(1)}, bf16[2,2,64,256]{3,2,1,0:T(8,128)(2,1)S(1)}, u32[]{:S(2)}, u32[]{:S(2)}) collective-permute-start(bf16[2,2,64,256]{3,2,1,0:T(8,128)(2,1)S(1)} %get-tuple-element.38), channel_id=1, source_target_pairs={{0,32},{32,0},{64,96},{96,64},{128,160},{160,128},{192,224},{224,1... | collective-permute-start | bytes 393224 | tf_op jit(solution)/shard_map/ppermute | solution.py:302
  49.4 1.0 %collective-permute-done.2.got_ref = bf16[2,2,64,256]{3,2,1,0:T(8,128)(2,1)S(1)} collective-permute-done((bf16[2,2,64,256]{3,2,1,0:T(8,128)(2,1)S(1)}, bf16[2,2,64,256]{3,2,1,0:T(8,128)(2,1)S(1)}, u32[]{:S(2)}, u32[]{:S(2)}) %collective-permute-start.2) | collective-permute-done | bytes 131104 | tf_op jit(solution)/shard_map/ppermute | solution.py:302
  50.4 0.6 shard_map.121
  51.0 1.4 %collective-permute-start.3 = (bf16[2,2,64,256]{3,2,1,0:T(8,128)(2,1)S(1)}, bf16[2,2,64,256]{3,2,1,0:T(8,128)(2,1)S(1)}, u32[]{:S(2)}, u32[]{:S(2)}) collective-permute-start(bf16[2,2,64,256]{3,2,1,0:T(8,128)(2,1)S(1)} %get-tuple-element.40), channel_id=1, source_target_pairs={{0,64},{32,96},{64,128},{96,160},{128,192},{160,224},{192,0},{224,... | collective-permute-start | bytes 393224 | tf_op jit(solution)/shard_map/ppermute | solution.py:307
  52.4 2.6 %collective-permute-start.4 = (bf16[2,2,64,256]{3,2,1,0:T(8,128)(2,1)S(1)}, bf16[2,2,64,256]{3,2,1,0:T(8,128)(2,1)S(1)}, u32[]{:S(2)}, u32[]{:S(2)}) collective-permute-start(bf16[2,2,64,256]{3,2,1,0:T(8,128)(2,1)S(1)} %get-tuple-element.41), channel_id=1, source_target_pairs={{0,128},{32,160},{64,192},{96,224},{128,0},{160,32},{192,64},{224,... | collective-permute-start | bytes 393224 | tf_op jit(solution)/shard_map/ppermute | solution.py:307
  55.0 1.1 %collective-permute-start.5 = (bf16[2,2,64,256]{3,2,1,0:T(8,128)(2,1)S(1)}, bf16[2,2,64,256]{3,2,1,0:T(8,128)(2,1)S(1)}, u32[]{:S(2)}, u32[]{:S(2)}) collective-permute-start(bf16[2,2,64,256]{3,2,1,0:T(8,128)(2,1)S(1)} %get-tuple-element.42), channel_id=1, source_target_pairs={{0,192},{32,224},{64,0},{96,32},{128,64},{160,96},{192,128},{224,1... | collective-permute-start | bytes 393224 | tf_op jit(solution)/shard_map/ppermute | solution.py:307
  56.1 1.1 %collective-permute-done.3.rest_1_ = bf16[2,2,64,256]{3,2,1,0:T(8,128)(2,1)S(1)} collective-permute-done((bf16[2,2,64,256]{3,2,1,0:T(8,128)(2,1)S(1)}, bf16[2,2,64,256]{3,2,1,0:T(8,128)(2,1)S(1)}, u32[]{:S(2)}, u32[]{:S(2)}) %collective-permute-start.3) | collective-permute-done | bytes 131104 | tf_op jit(solution)/shard_map/ppermute | solution.py:307
  57.1 3.9 %collective-permute-done.4.rest_2_ = bf16[2,2,64,256]{3,2,1,0:T(8,128)(2,1)S(1)} collective-permute-done((bf16[2,2,64,256]{3,2,1,0:T(8,128)(2,1)S(1)}, bf16[2,2,64,256]{3,2,1,0:T(8,128)(2,1)S(1)}, u32[]{:S(2)}, u32[]{:S(2)}) %collective-permute-start.4) | collective-permute-done | bytes 131104 | tf_op jit(solution)/shard_map/ppermute | solution.py:307
  61.1 0.0 collective-permute-done.5.rest_3_
  61.1 1.3 %shard_map.122 = bf16[2,2,64,256]{3,2,1,0:T(8,128)(2,1)} custom-call(s32[8]{0:T(128)S(1)} %get-tuple-element.24.frames_ref, s32[8]{0:T(128)S(1)} %get-tuple-element.25.rank_ref, bf16[2,2,64,256]{3,2,1,0:T(8,128)(2,1)S(1)} %get-tuple-element.39.rest_0_, bf16[2,2,64,256]{3,2,1,0:T(8,128)(2,1)S(1)} %collective-permute-done.3.rest_1_, ...), custom_call_target="tpu_custom_call" | custom-call | tf_op jit(solution)/shard_map/pallas_call | solution.py:308
Async XLA Ops:
  0.0 25.9 %collective-permute-start.1 = (bf16[4,2,64,256]{3,2,1,0:T(8,128)(2,1)}, bf16[4,2,64,256]{3,2,1,0:T(8,128)(2,1)S(1)}, u32[]{:S(2)}, u32[]{:S(2)}) collective-permute-start(bf16[4,2,64,256]{3,2,1,0:T(8,128)(2,1)} %latent_hbm.1), channel_id=1, source_target_pairs={{1,0},{2,1},{3,2},{4,3},{5,4},{6,5},{7,6},{8,7},{9,8},{10,9},{11,1... | collective-permute-start | bytes 786440 | tf_op jit(solution)/shard_map/ppermute | solution.py:281
  8.6 17.3 %collective-permute-start = (bf16[4,2,64,256]{3,2,1,0:T(8,128)(2,1)}, bf16[4,2,64,256]{3,2,1,0:T(8,128)(2,1)S(1)}, u32[]{:S(2)}, u32[]{:S(2)}) collective-permute-start(bf16[4,2,64,256]{3,2,1,0:T(8,128)(2,1)} %latent_hbm.1), channel_id=1, source_target_pairs={{0,1},{1,2},{2,3},{3,4},{4,5},{5,6},{6,7},{7,8},{8,9},{9,10},{10,1... | collective-permute-start | bytes 786440 | tf_op jit(solution)/shard_map/ppermute | solution.py:280
  8.6 17.3 %copy-start = (bf16[3,3,3,256,256]{4,3,2,1,0:T(8,128)(2,1)S(1)}, bf16[3,3,3,256,256]{4,3,2,1,0:T(8,128)(2,1)}, u32[]{:S(2)}) copy-start(bf16[3,3,3,256,256]{4,3,2,1,0:T(8,128)(2,1)} %param.18) | copy-start | bytes 10616836
  10.7 32.1 %copy-start.1 = (bf16[3,3,3,256,256]{4,3,2,1,0:T(8,128)(2,1)S(1)}, bf16[3,3,3,256,256]{4,3,2,1,0:T(8,128)(2,1)}, u32[]{:S(2)}) copy-start(bf16[3,3,3,256,256]{4,3,2,1,0:T(8,128)(2,1)} %param.22) | copy-start | bytes 10616836
  45.5 4.9 %collective-permute-start.2 = (bf16[2,2,64,256]{3,2,1,0:T(8,128)(2,1)S(1)}, bf16[2,2,64,256]{3,2,1,0:T(8,128)(2,1)S(1)}, u32[]{:S(2)}, u32[]{:S(2)}) collective-permute-start(bf16[2,2,64,256]{3,2,1,0:T(8,128)(2,1)S(1)} %get-tuple-element.38), channel_id=1, source_target_pairs={{0,32},{32,0},{64,96},{96,64},{128,160},{160,128},{192,224},{224,1... | collective-permute-start | bytes 393224 | tf_op jit(solution)/shard_map/ppermute | solution.py:302
  51.0 6.2 %collective-permute-start.3 = (bf16[2,2,64,256]{3,2,1,0:T(8,128)(2,1)S(1)}, bf16[2,2,64,256]{3,2,1,0:T(8,128)(2,1)S(1)}, u32[]{:S(2)}, u32[]{:S(2)}) collective-permute-start(bf16[2,2,64,256]{3,2,1,0:T(8,128)(2,1)S(1)} %get-tuple-element.40), channel_id=1, source_target_pairs={{0,64},{32,96},{64,128},{96,160},{128,192},{160,224},{192,0},{224,... | collective-permute-start | bytes 393224 | tf_op jit(solution)/shard_map/ppermute | solution.py:307
  52.4 8.7 %collective-permute-start.4 = (bf16[2,2,64,256]{3,2,1,0:T(8,128)(2,1)S(1)}, bf16[2,2,64,256]{3,2,1,0:T(8,128)(2,1)S(1)}, u32[]{:S(2)}, u32[]{:S(2)}) collective-permute-start(bf16[2,2,64,256]{3,2,1,0:T(8,128)(2,1)S(1)} %get-tuple-element.41), channel_id=1, source_target_pairs={{0,128},{32,160},{64,192},{96,224},{128,0},{160,32},{192,64},{224,... | collective-permute-start | bytes 393224 | tf_op jit(solution)/shard_map/ppermute | solution.py:307
  55.0 6.1 %collective-permute-start.5 = (bf16[2,2,64,256]{3,2,1,0:T(8,128)(2,1)S(1)}, bf16[2,2,64,256]{3,2,1,0:T(8,128)(2,1)S(1)}, u32[]{:S(2)}, u32[]{:S(2)}) collective-permute-start(bf16[2,2,64,256]{3,2,1,0:T(8,128)(2,1)S(1)} %get-tuple-element.42), channel_id=1, source_target_pairs={{0,192},{32,224},{64,0},{96,32},{128,64},{160,96},{192,128},{224,1... | collective-permute-start | bytes 393224 | tf_op jit(solution)/shard_map/ppermute | solution.py:307

commit v6 on v5

--- a/solution.py
+++ b/solution.py
@@ -10,7 +10,6 @@
 G = 32
 LANES = 128
 EPSILON = 1e-06
-HIGH = lax.Precision.HIGHEST
 F32 = jnp.float32
 BF16 = jnp.bfloat16
 VMEM = pl.BlockSpec(memory_space=pltpu.VMEM)
@@ -20,14 +19,9 @@
 LIMIT = 20 * 1024 * 1024
 
 
-def dot_high(a, b, contract):
-    return lax.dot_general(a, b, ((contract[:1], contract[1:]), ((), ())), precision=HIGH, preferred_element_type=F32)
-
-
-def member_rows(group_row, first):
-    channels = group_row.shape[1]
-    rows = lax.broadcasted_iota(jnp.int32, (LANES, channels), 0)
-    return (rows - first == group_row).astype(F32)
+def member_rows(group_row):
+    rows = lax.broadcasted_iota(jnp.int32, (LANES, group_row.shape[1]), 0)
+    return ((rows == group_row) | (rows - G == group_row)).astype(F32).astype(BF16)
 
 
 def clip_start_of(frames_ref, rank_ref, clip):
@@ -37,27 +31,48 @@
     return start
 
 
+def in_thirds(row):
+    first = row.astype(BF16)
+    row = row - first.astype(F32)
+    second = row.astype(BF16)
+    return [first, second, (row - second.astype(F32)).astype(BF16)]
+
+
+def dot_rows(rows, members, side):
+    pieces = [piece for row in rows for piece in in_thirds(row)]
+    pad = jnp.zeros((16 - len(pieces), pieces[0].shape[1]), BF16)
+    left = jnp.concatenate(pieces + [pad], axis=0)
+    product = lax.dot_general(left, members, (((1,), (side,)), ((), ())), preferred_element_type=F32)
+    return [jnp.sum(product[3 * i : 3 * i + 3], axis=0, keepdims=True) for i in range(len(rows))]
+
+
 def local_stats(field_ref, length, group_row):
     frames, height, columns, channels = field_ref.shape
     pixels = height * columns
-    scale = 1.0 / (length.astype(F32) * float(pixels * (channels // G)))
+    entries = length.astype(F32) * float(pixels)
     live = [jnp.where(f < length, 1.0, 0.0).astype(F32) for f in range(frames)]
+    members = member_rows(group_row)
+    share = float(G) / channels
 
     def frame(f):
         return field_ref[f].astype(F32).reshape(pixels, channels)
 
-    total = jnp.zeros((1, channels), F32)
+    mean = jnp.zeros((1, channels), F32)
     for f in range(frames):
-        total = total + live[f] * jnp.sum(frame(f), axis=0, keepdims=True)
-    mean_rows = member_rows(group_row, 0)
-    group_mean = dot_high(jnp.broadcast_to(total, (8, channels)), mean_rows, (1, 1)) * scale
-    mean = dot_high(group_mean, mean_rows, (1, 0))[:1]
+        mean = mean + live[f] * jnp.sum(frame(f), axis=0, keepdims=True)
+    mean = mean * (1.0 / entries)
+    (group_mean,) = dot_rows([mean], members, 1)
+    group_mean = group_mean * share
+    lane = lax.broadcasted_iota(jnp.int32, (1, LANES), 1)
+    group_mean = jnp.where(lane < G, group_mean, 0.0)
+    (mean_back,) = dot_rows([group_mean], members, 0)
     spread = jnp.zeros((1, channels), F32)
     for f in range(frames):
         centred = frame(f) - mean
         spread = spread + live[f] * jnp.sum(centred * centred, axis=0, keepdims=True)
-    group_spread = dot_high(jnp.broadcast_to(spread, (8, channels)), member_rows(group_row, G), (1, 1))
-    return (group_mean + group_spread)[:1]
+    away = mean - mean_back
+    (group_spread,) = dot_rows([spread + away * away * entries], members, 1)
+    return jnp.where(lane < G, group_mean, group_spread)
 
 
 def combine_stats(parts, length, pixels, group_row):
@@ -71,30 +86,30 @@
     between = jnp.sum(away * away, axis=0, keepdims=True) * per_band
     spread = jnp.where(lane < G, between, jnp.where(lane < 2 * G, sums, 0.0))
     mean = jnp.where(lane < G, mean, 0.0)
-    which = lax.broadcasted_iota(jnp.int32, (8, LANES), 0)
-    both = jnp.where(which == 0, mean, spread)
-    spread_back = dot_high(both, member_rows(group_row, 0) + member_rows(group_row, G), (1, 0))
-    variance = spread_back[1:2] / (per_band * bands)
-    return spread_back[:1], lax.rsqrt(variance + EPSILON)
-
-
-def activate(rows, act_ref, mean, scale, shift):
-    channels = mean.shape[1]
-    for f in range(act_ref.shape[0]):
-        for r in range(act_ref.shape[1]):
-            half = ((rows(f, r).astype(F32) - mean) * scale + shift) * 0.5
-            act = half * jnp.tanh(half) + half
-            left = jnp.concatenate([act[:1], act[:-1]], axis=0)
-            right = jnp.concatenate([act[1:], act[-1:]], axis=0)
-            for step, taken in enumerate((left, act, right)):
-                act_ref[f, r, :, step * channels : (step + 1) * channels] = taken.astype(BF16)
-
-
-def convolve(act_ref, weight_ref, acc_refs):
+    mean_back, spread_back = dot_rows([mean, spread], member_rows(group_row), 0)
+    return mean_back, lax.rsqrt(spread_back / (per_band * bands) + EPSILON)
+
+
+def activate(rows, act_ref, slope, offset, f):
+    channels = slope.shape[1]
+    for r in range(act_ref.shape[1]):
+        half = rows(f, r).astype(F32) * slope + offset
+        act = half * jnp.tanh(half) + half
+        left = jnp.concatenate([act[:1], act[:-1]], axis=0)
+        right = jnp.concatenate([act[1:], act[-1:]], axis=0)
+        for step, taken in enumerate((left, act, right)):
+            act_ref[f, r, :, step * channels : (step + 1) * channels] = taken.astype(BF16)
+
+
+def convolve(rows, act_ref, weight_ref, acc_refs, slope, offset):
     frames, height, columns, width = act_ref.shape
     height = height - 2
+    ready = 0
     for back_step, acc_ref in enumerate(acc_refs):
         used = frames - 2 + back_step
+        for f in range(ready, used):
+            activate(rows, act_ref, slope, offset, f)
+        ready = used
         slabs = [act_ref[:used, j : j + height].reshape(used * height * columns, width) for j in range(3)]
         kernel = weight_ref[3 * back_step : 3 * back_step + 3].reshape(3 * width, -1)
         part = jnp.dot(jnp.concatenate(slabs, axis=1), kernel, preferred_element_type=F32)
@@ -144,6 +159,8 @@
     zero = jnp.minimum(length, 0)
     top, bottom = band_ends()
     mean, inverse = combine_stats(parts_ref[:, 0], length, height * columns, group_ref[...])
+    slope = inverse * gain_ref[...] * 0.5
+    offset = shift_ref[...] * 0.5 - mean * slope
 
     def rows(f, r):
         if r < 2:
@@ -154,8 +171,7 @@
             return jnp.where(bottom, field_ref[f, height - 1], row) if r == height + 2 else row
         return field_ref[f, r - 2]
 
-    activate(rows, act_ref, mean, inverse * gain_ref[...], shift_ref[...])
-    convolve(act_ref, weight_ref, acc_refs)
+    convolve(rows, act_ref, weight_ref, acc_refs, slope, offset)
     for f in range(frames):
         hidden = (frame_sum(acc_refs, f, zero) + bias_ref[...]).astype(BF16)
         hidden_ref[f] = hidden
@@ -177,6 +193,8 @@
     start = clip_start_of(frames_ref, rank_ref, clip)
     top, bottom = band_ends()
     mean, inverse = combine_stats(parts_ref[:, 0], length, height * columns, group_ref[...])
+    slope = inverse * gain_ref[...] * 0.5
+    offset = shift_ref[...] * 0.5 - mean * slope
 
     def rows(f, r):
         row = hidden_ref[f, r]
@@ -184,8 +202,7 @@
             return jnp.where(top, hidden_ref[f, 1], row)
         return jnp.where(bottom, hidden_ref[f, height], row) if r == height + 1 else row
 
-    activate(rows, act_ref, mean, inverse * gain_ref[...], shift_ref[...])
-    convolve(act_ref, weight_ref, acc_refs)
+    convolve(rows, act_ref, weight_ref, acc_refs, slope, offset)
     for f in range(frames):
         total = (latent_ref[f].astype(F32) + (frame_sum(acc_refs, f, zero) + bias_ref[...])).astype(BF16)
         place = lax.rem(start + f, 4)

time: 62.5 us -> 61 us (0.976)
  Pallas kernels: 12 us -> 10.5 us
    pallas_call x1, Pallas kernels: 5.33 us -> 4.4 us  [local(): call(first_kernel, [SMEM] + [VMEM] * 9, [((frames, height + 2, columns, c...]
where the time goes in v6:
time: 61 us; the launch traced here: 60.8 us
  blocking collectives  26.8 us (44%)
  starting transfers between devices  17.6 us (29%)
  Pallas kernels  10.5 us (17%)
  waiting for transfers between devices  5.99 us (10%)
    all_to_all x2, blocking collectives, gather(): return lax.all_to_all(parts, 'space', 0, 0, tiled=True)  26.8 us
    ppermute x1, starting transfers between devices, local(): lax.ppermute(latent, 'space', [((i + 1) % bands, i) for i in range(bands)])  8.6 us
    ppermute x3, starting transfers between devices, local(): got[step] = lax.ppermute(got[step], 'tm', along)  5.06 us
    ppermute x3, waiting for transfers between devices, local(): got[step] = lax.ppermute(got[step], 'tm', along)  5 us
    pallas_call x1, Pallas kernels, local(): call(first_kernel, [SMEM] + [VMEM] * 9, [((frames, height + 2, columns, c...  4.4 us
    ppermute x1, starting transfers between devices, local(): got = lax.ppermute(send, 'tm', [(i, i ^ 1) for i in range(clips)])  3.89 us
    pallas_call x1, Pallas kernels, local(): call(second_kernel, [SMEM] * 2 + [VMEM] * 8, [half, half], work(height))  2.49 us
    pallas_call x1, Pallas kernels, local(): call(stats_kernel, [HBM] * (3 + len(vectors)), outs, [pltpu.SMEM(clip_fra...  1.68 us
  transfers between devices with their start and end apart: 6, of which 3 were waited for; matrix products, arithmetic and copies ran while one was open for 0% of the time, Pallas kernels for 3%

profile of v6, /device:TPU:1, one launch (start us, length us, event | category | flops | bytes accessed | tf_op | source)
XLA Modules:
  0.0 60.8 jit_solution(712153774636123789)
XLA Ops:
  0.0 8.6 %collective-permute-start.1 = (bf16[4,2,64,256]{3,2,1,0:T(8,128)(2,1)}, bf16[4,2,64,256]{3,2,1,0:T(8,128)(2,1)S(1)}, u32[]{:S(2)}, u32[]{:S(2)}) collective-permute-start(bf16[4,2,64,256]{3,2,1,0:T(8,128)(2,1)} %latent_hbm.1), channel_id=1, source_target_pairs={{1,0},{2,1},{3,2},{4,3},{5,4},{6,5},{7,6},{8,7},{9,8},{10,9},{11,1... | collective-permute-start | bytes 786440 | tf_op jit(solution)/shard_map/ppermute | solution.py:298
  8.6 0.0 collective-permute-start
  8.6 0.0 copy-start
  8.6 1.7 %shard_map.118 = (f32[32,1,128]{2,1,0:T(1,128)S(1)}, bf16[4,2,64,256]{3,2,1,0:T(8,128)(2,1)S(1)}, s32[8]{0:T(128)S(1)}, s32[8]{0:T(128)S(1)}, s32[1,256]{1,0:T(1...) custom-call(s32[8]{0:T(128)} %frames_hbm.1, ...), custom_call_target="tpu_custom_call" | custom-call | flops 4294967296 | bytes 16777216 | tf_op jit(solution)/shard_map/pallas_call | solution.py:302
  10.3 0.0 copy-start.1
  10.3 15.2 %all_to_all.10.parts_ref = f32[32,1,128]{2,1,0:T(1,128)S(1)} all-to-all(f32[32,1,128]{2,1,0:T(1,128)S(1)} %get-tuple-element.26), channel_id=1, replica_groups=mesh['tm'=8,'space'=32] {'space'}, dimensions={0} | all-to-all | bytes 32768 | tf_op jit(solution)/shard_map/all_to_all | solution.py:291
  25.5 0.0 collective-permute-done.1.below_ref
  25.5 0.0 collective-permute-done.above_ref
  25.5 0.0 copy-done
  25.5 4.4 %shard_map.119 = (bf16[4,4,64,256]{3,2,1,0:T(8,128)(2,1)S(1)}, f32[32,1,128]{2,1,0:T(1,128)S(1)}) custom-call(s32[8]{0:T(128)S(1)} %get-tuple-element.24.frames_ref, f32[32,1,128]{2,1,0:T(1,128)S(1)} %all_to_all.10.parts_ref, bf16[4,2,64,256]{3,2,1,0:T(8,128)(2,1)S(1)} %get-tuple-element.27.field_ref.latent_ref, ...), custom_call_target="tpu_custom_call" | custom-call | tf_op jit(solution)/shard_map/pallas_call | solution.py:309
  29.9 11.6 %all_to_all.11.parts_ref = f32[32,1,128]{2,1,0:T(1,128)S(1)} all-to-all(f32[32,1,128]{2,1,0:T(1,128)S(1)} %get-tuple-element.32), channel_id=1, replica_groups=mesh['tm'=8,'space'=32] {'space'}, dimensions={0} | all-to-all | bytes 32768 | tf_op jit(solution)/shard_map/all_to_all | solution.py:291
  41.5 0.0 copy-done.1
  41.5 2.5 %shard_map.120 = (bf16[2,2,64,256]{3,2,1,0:T(8,128)(2,1)S(1)}, bf16[2,2,64,256]{3,2,1,0:T(8,128)(2,1)S(1)}) custom-call(s32[8]{0:T(128)S(1)} %get-tuple-element.24.frames_ref, s32[8]{0:T(128)S(1)} %get-tuple-element.25.rank_ref, f32[32,1,128]{2,1,0:T(1,128)S(1)} %all_to_all.11.parts_ref, bf16[4,4,64,256]{3,2,1,0:T(8,128)(2,1)S(1)} %get-tuple-element.33.hidden_ref, ...), custom_call_target="tpu_custom_call" | custom-call | tf_op jit(solution)/shard_map/pallas_call | solution.py:316
  44.0 3.9 %collective-permute-start.2 = (bf16[2,2,64,256]{3,2,1,0:T(8,128)(2,1)S(1)}, bf16[2,2,64,256]{3,2,1,0:T(8,128)(2,1)S(1)}, u32[]{:S(2)}, u32[]{:S(2)}) collective-permute-start(bf16[2,2,64,256]{3,2,1,0:T(8,128)(2,1)S(1)} %get-tuple-element.38), channel_id=1, source_target_pairs={{0,32},{32,0},{64,96},{96,64},{128,160},{160,128},{192,224},{224,1... | collective-permute-start | bytes 393224 | tf_op jit(solution)/shard_map/ppermute | solution.py:319
  47.9 1.0 %collective-permute-done.2.got_ref = bf16[2,2,64,256]{3,2,1,0:T(8,128)(2,1)S(1)} collective-permute-done((bf16[2,2,64,256]{3,2,1,0:T(8,128)(2,1)S(1)}, bf16[2,2,64,256]{3,2,1,0:T(8,128)(2,1)S(1)}, u32[]{:S(2)}, u32[]{:S(2)}) %collective-permute-start.2) | collective-permute-done | bytes 131104 | tf_op jit(solution)/shard_map/ppermute | solution.py:319
  48.9 0.6 shard_map.121
  49.5 1.4 %collective-permute-start.3 = (bf16[2,2,64,256]{3,2,1,0:T(8,128)(2,1)S(1)}, bf16[2,2,64,256]{3,2,1,0:T(8,128)(2,1)S(1)}, u32[]{:S(2)}, u32[]{:S(2)}) collective-permute-start(bf16[2,2,64,256]{3,2,1,0:T(8,128)(2,1)S(1)} %get-tuple-element.40), channel_id=1, source_target_pairs={{0,64},{32,96},{64,128},{96,160},{128,192},{160,224},{192,0},{224,... | collective-permute-start | bytes 393224 | tf_op jit(solution)/shard_map/ppermute | solution.py:324
  50.9 2.6 %collective-permute-start.4 = (bf16[2,2,64,256]{3,2,1,0:T(8,128)(2,1)S(1)}, bf16[2,2,64,256]{3,2,1,0:T(8,128)(2,1)S(1)}, u32[]{:S(2)}, u32[]{:S(2)}) collective-permute-start(bf16[2,2,64,256]{3,2,1,0:T(8,128)(2,1)S(1)} %get-tuple-element.41), channel_id=1, source_target_pairs={{0,128},{32,160},{64,192},{96,224},{128,0},{160,32},{192,64},{224,... | collective-permute-start | bytes 393224 | tf_op jit(solution)/shard_map/ppermute | solution.py:324
  53.5 1.1 %collective-permute-start.5 = (bf16[2,2,64,256]{3,2,1,0:T(8,128)(2,1)S(1)}, bf16[2,2,64,256]{3,2,1,0:T(8,128)(2,1)S(1)}, u32[]{:S(2)}, u32[]{:S(2)}) collective-permute-start(bf16[2,2,64,256]{3,2,1,0:T(8,128)(2,1)S(1)} %get-tuple-element.42), channel_id=1, source_target_pairs={{0,192},{32,224},{64,0},{96,32},{128,64},{160,96},{192,128},{224,1... | collective-permute-start | bytes 393224 | tf_op jit(solution)/shard_map/ppermute | solution.py:324
  54.5 1.1 %collective-permute-done.3.rest_1_ = bf16[2,2,64,256]{3,2,1,0:T(8,128)(2,1)S(1)} collective-permute-done((bf16[2,2,64,256]{3,2,1,0:T(8,128)(2,1)S(1)}, bf16[2,2,64,256]{3,2,1,0:T(8,128)(2,1)S(1)}, u32[]{:S(2)}, u32[]{:S(2)}) %collective-permute-start.3) | collective-permute-done | bytes 131104 | tf_op jit(solution)/shard_map/ppermute | solution.py:324
  55.6 3.9 %collective-permute-done.4.rest_2_ = bf16[2,2,64,256]{3,2,1,0:T(8,128)(2,1)S(1)} collective-permute-done((bf16[2,2,64,256]{3,2,1,0:T(8,128)(2,1)S(1)}, bf16[2,2,64,256]{3,2,1,0:T(8,128)(2,1)S(1)}, u32[]{:S(2)}, u32[]{:S(2)}) %collective-permute-start.4) | collective-permute-done | bytes 131104 | tf_op jit(solution)/shard_map/ppermute | solution.py:324
  59.5 0.0 collective-permute-done.5.rest_3_
  59.5 1.3 %shard_map.122 = bf16[2,2,64,256]{3,2,1,0:T(8,128)(2,1)} custom-call(s32[8]{0:T(128)S(1)} %get-tuple-element.24.frames_ref, s32[8]{0:T(128)S(1)} %get-tuple-element.25.rank_ref, bf16[2,2,64,256]{3,2,1,0:T(8,128)(2,1)S(1)} %get-tuple-element.39.rest_0_, bf16[2,2,64,256]{3,2,1,0:T(8,128)(2,1)S(1)} %collective-permute-done.3.rest_1_, ...), custom_call_target="tpu_custom_call" | custom-call | tf_op jit(solution)/shard_map/pallas_call | solution.py:325
Async XLA Ops:
  0.0 25.5 %collective-permute-start.1 = (bf16[4,2,64,256]{3,2,1,0:T(8,128)(2,1)}, bf16[4,2,64,256]{3,2,1,0:T(8,128)(2,1)S(1)}, u32[]{:S(2)}, u32[]{:S(2)}) collective-permute-start(bf16[4,2,64,256]{3,2,1,0:T(8,128)(2,1)} %latent_hbm.1), channel_id=1, source_target_pairs={{1,0},{2,1},{3,2},{4,3},{5,4},{6,5},{7,6},{8,7},{9,8},{10,9},{11,1... | collective-permute-start | bytes 786440 | tf_op jit(solution)/shard_map/ppermute | solution.py:298
  8.6 16.9 %collective-permute-start = (bf16[4,2,64,256]{3,2,1,0:T(8,128)(2,1)}, bf16[4,2,64,256]{3,2,1,0:T(8,128)(2,1)S(1)}, u32[]{:S(2)}, u32[]{:S(2)}) collective-permute-start(bf16[4,2,64,256]{3,2,1,0:T(8,128)(2,1)} %latent_hbm.1), channel_id=1, source_target_pairs={{0,1},{1,2},{2,3},{3,4},{4,5},{5,6},{6,7},{7,8},{8,9},{9,10},{10,1... | collective-permute-start | bytes 786440 | tf_op jit(solution)/shard_map/ppermute | solution.py:297
  8.6 16.9 %copy-start = (bf16[3,3,3,256,256]{4,3,2,1,0:T(8,128)(2,1)S(1)}, bf16[3,3,3,256,256]{4,3,2,1,0:T(8,128)(2,1)}, u32[]{:S(2)}) copy-start(bf16[3,3,3,256,256]{4,3,2,1,0:T(8,128)(2,1)} %param.18) | copy-start | bytes 10616836
  10.3 31.2 %copy-start.1 = (bf16[3,3,3,256,256]{4,3,2,1,0:T(8,128)(2,1)S(1)}, bf16[3,3,3,256,256]{4,3,2,1,0:T(8,128)(2,1)}, u32[]{:S(2)}) copy-start(bf16[3,3,3,256,256]{4,3,2,1,0:T(8,128)(2,1)} %param.22) | copy-start | bytes 10616836
  44.0 4.9 %collective-permute-start.2 = (bf16[2,2,64,256]{3,2,1,0:T(8,128)(2,1)S(1)}, bf16[2,2,64,256]{3,2,1,0:T(8,128)(2,1)S(1)}, u32[]{:S(2)}, u32[]{:S(2)}) collective-permute-start(bf16[2,2,64,256]{3,2,1,0:T(8,128)(2,1)S(1)} %get-tuple-element.38), channel_id=1, source_target_pairs={{0,32},{32,0},{64,96},{96,64},{128,160},{160,128},{192,224},{224,1... | collective-permute-start | bytes 393224 | tf_op jit(solution)/shard_map/ppermute | solution.py:319
  49.5 6.1 %collective-permute-start.3 = (bf16[2,2,64,256]{3,2,1,0:T(8,128)(2,1)S(1)}, bf16[2,2,64,256]{3,2,1,0:T(8,128)(2,1)S(1)}, u32[]{:S(2)}, u32[]{:S(2)}) collective-permute-start(bf16[2,2,64,256]{3,2,1,0:T(8,128)(2,1)S(1)} %get-tuple-element.40), channel_id=1, source_target_pairs={{0,64},{32,96},{64,128},{96,160},{128,192},{160,224},{192,0},{224,... | collective-permute-start | bytes 393224 | tf_op jit(solution)/shard_map/ppermute | solution.py:324
  50.9 8.7 %collective-permute-start.4 = (bf16[2,2,64,256]{3,2,1,0:T(8,128)(2,1)S(1)}, bf16[2,2,64,256]{3,2,1,0:T(8,128)(2,1)S(1)}, u32[]{:S(2)}, u32[]{:S(2)}) collective-permute-start(bf16[2,2,64,256]{3,2,1,0:T(8,128)(2,1)S(1)} %get-tuple-element.41), channel_id=1, source_target_pairs={{0,128},{32,160},{64,192},{96,224},{128,0},{160,32},{192,64},{224,... | collective-permute-start | bytes 393224 | tf_op jit(solution)/shard_map/ppermute | solution.py:324
  53.5 6.1 %collective-permute-start.5 = (bf16[2,2,64,256]{3,2,1,0:T(8,128)(2,1)S(1)}, bf16[2,2,64,256]{3,2,1,0:T(8,128)(2,1)S(1)}, u32[]{:S(2)}, u32[]{:S(2)}) collective-permute-start(bf16[2,2,64,256]{3,2,1,0:T(8,128)(2,1)S(1)} %get-tuple-element.42), channel_id=1, source_target_pairs={{0,192},{32,224},{64,0},{96,32},{128,64},{160,96},{192,128},{224,1... | collective-permute-start | bytes 393224 | tf_op jit(solution)/shard_map/ppermute | solution.py:324

commit v7 on v6

--- a/solution.py
+++ b/solution.py
@@ -101,16 +101,18 @@
             act_ref[f, r, :, step * channels : (step + 1) * channels] = taken.astype(BF16)
 
 
-def convolve(rows, act_ref, weight_ref, acc_refs, slope, offset):
-    frames, height, columns, width = act_ref.shape
-    height = height - 2
+def convolve(rows, act_ref, weight_ref, acc_refs, slope, offset, taken):
+    frames, _, columns, width = act_ref.shape
     ready = 0
     for back_step, acc_ref in enumerate(acc_refs):
         used = frames - 2 + back_step
         for f in range(ready, used):
             activate(rows, act_ref, slope, offset, f)
         ready = used
-        slabs = [act_ref[:used, j : j + height].reshape(used * height * columns, width) for j in range(3)]
+        slabs = []
+        for places in taken:
+            slab = jnp.concatenate([act_ref[:used, pl.ds(place, 1)] for place in places], axis=1)
+            slabs.append(slab.reshape(used * len(places) * columns, width))
         kernel = weight_ref[3 * back_step : 3 * back_step + 3].reshape(3 * width, -1)
         part = jnp.dot(jnp.concatenate(slabs, axis=1), kernel, preferred_element_type=F32)
         acc_ref[...] = part.reshape(acc_ref.shape)
@@ -150,38 +152,31 @@
 
 
 def first_kernel(
-    frames_ref, parts_ref, field_ref, above_ref, below_ref, group_ref, gain_ref, shift_ref, bias_ref, weight_ref,
+    frames_ref, parts_ref, field_ref, above_ref, group_ref, gain_ref, shift_ref, bias_ref, weight_ref,
     hidden_ref, out_parts_ref,
-    own_ref, act_ref, *acc_refs,
+    act_ref, *acc_refs,
 ):
     frames, height, columns, channels = field_ref.shape
     length = frames_ref[lax.axis_index("tm")]
     zero = jnp.minimum(length, 0)
-    top, bottom = band_ends()
+    top, _ = band_ends()
+    taken = [(0, jnp.where(top, 2, 1)), (1, 2), (jnp.where(top, 1, 2), 3)]
     mean, inverse = combine_stats(parts_ref[:, 0], length, height * columns, group_ref[...])
     slope = inverse * gain_ref[...] * 0.5
     offset = shift_ref[...] * 0.5 - mean * slope
 
     def rows(f, r):
-        if r < 2:
-            row = above_ref[f, height - 2 + r]
-            return jnp.where(top, field_ref[f, 0], row) if r == 1 else row
-        if r >= height + 2:
-            row = below_ref[f, r - height - 2]
-            return jnp.where(bottom, field_ref[f, height - 1], row) if r == height + 2 else row
-        return field_ref[f, r - 2]
-
-    convolve(rows, act_ref, weight_ref, acc_refs, slope, offset)
+        return above_ref[f, r] if r < 2 else field_ref[f, r - 2]
+
+    convolve(rows, act_ref, weight_ref, acc_refs, slope, offset, taken)
     for f in range(frames):
-        hidden = (frame_sum(acc_refs, f, zero) + bias_ref[...]).astype(BF16)
-        hidden_ref[f] = hidden
-        own_ref[f] = hidden[1 : height + 1]
-    row = local_stats(own_ref, length, group_ref[...])
+        hidden_ref[f] = (frame_sum(acc_refs, f, zero) + bias_ref[...]).astype(BF16)
+    row = local_stats(hidden_ref, length, group_ref[...])
     out_parts_ref[...] = jnp.broadcast_to(row[None], out_parts_ref.shape)
 
 
 def second_kernel(
-    frames_ref, rank_ref, parts_ref, hidden_ref, latent_ref, group_ref, gain_ref, shift_ref, bias_ref, weight_ref,
+    frames_ref, rank_ref, parts_ref, hidden_ref, below_ref, latent_ref, group_ref, gain_ref, shift_ref, bias_ref, weight_ref,
     keep_ref, send_ref,
     act_ref, *acc_refs,
 ):
@@ -192,17 +187,15 @@
     zero = jnp.minimum(length, 0)
     start = clip_start_of(frames_ref, rank_ref, clip)
     top, bottom = band_ends()
+    taken = [(jnp.where(top, 1, 0), 1), (1, 2), (2, jnp.where(bottom, 2, 3))]
     mean, inverse = combine_stats(parts_ref[:, 0], length, height * columns, group_ref[...])
     slope = inverse * gain_ref[...] * 0.5
     offset = shift_ref[...] * 0.5 - mean * slope
 
     def rows(f, r):
-        row = hidden_ref[f, r]
-        if r == 0:
-            return jnp.where(top, hidden_ref[f, 1], row)
-        return jnp.where(bottom, hidden_ref[f, height], row) if r == height + 1 else row
-
-    convolve(rows, act_ref, weight_ref, acc_refs, slope, offset)
+        return hidden_ref[f, r] if r < 2 else below_ref[f, r - 2]
+
+    convolve(rows, act_ref, weight_ref, acc_refs, slope, offset, taken)
     for f in range(frames):
         total = (latent_ref[f].astype(F32) + (frame_sum(acc_refs, f, zero) + bias_ref[...])).astype(BF16)
         place = lax.rem(start + f, 4)
@@ -290,12 +283,10 @@
     def gather(parts):
         return lax.all_to_all(parts, "space", 0, 0, tiled=True)
 
-    def work(height):
-        accs = [pltpu.VMEM((frames - 2 + i, height, columns, channels), F32) for i in range(3)]
-        return [pltpu.VMEM((frames, height + 2, columns, 3 * channels), BF16)] + accs
+    work = [pltpu.VMEM((frames, 4, columns, 3 * channels), BF16)]
+    work += [pltpu.VMEM((frames - 2 + i, height, columns, channels), F32) for i in range(3)]
 
     above = lax.ppermute(latent, "space", [(i, (i + 1) % bands) for i in range(bands)])
-    below = lax.ppermute(latent, "space", [((i + 1) % bands, i) for i in range(bands)])
     vectors = [row(v) for v in (group_of, gain_first, shift_first, bias_first, gain_second, shift_second, bias_second)]
     outs = [parts_out, (latent.shape, BF16), (clip_frames.shape, jnp.int32), (clip_rank.shape, jnp.int32)]
     outs += [(v.shape, v.dtype) for v in vectors]
@@ -306,15 +297,14 @@
     )(*map(in_hbm, (clip_frames, clip_rank, latent, *vectors)))
     group_row = vectors[0]
     parts = gather(parts)
-    hidden, parts = call(
-        first_kernel, [SMEM] + [VMEM] * 9,
-        [((frames, height + 2, columns, channels), BF16), parts_out],
-        [pltpu.VMEM(latent.shape, BF16)] + work(height + 2),
-    )(clip_frames, parts, latent, above, below, *vectors[:4], taps(conv_first))
+    hidden, parts = call(first_kernel, [SMEM] + [VMEM] * 8, [(latent.shape, BF16), parts_out], work)(
+        clip_frames, parts, latent, above, *vectors[:4], taps(conv_first)
+    )
+    below = lax.ppermute(hidden, "space", [((i + 1) % bands, i) for i in range(bands)])
     parts = gather(parts)
     half = ((2, height, columns, channels), BF16)
-    keep, send = call(second_kernel, [SMEM] * 2 + [VMEM] * 8, [half, half], work(height))(
-        clip_frames, clip_rank, parts, hidden, latent, group_row, *vectors[4:], taps(conv_second),
+    keep, send = call(second_kernel, [SMEM] * 2 + [VMEM] * 9, [half, half], work)(
+        clip_frames, clip_rank, parts, hidden, below, latent, group_row, *vectors[4:], taps(conv_second),
     )
     got = lax.ppermute(send, "tm", [(i, i ^ 1) for i in range(clips)])
     chips = clips // 2

time: 61 us -> 59.7 us (0.979)
  starting transfers between devices: 17.6 us -> 12.6 us
  blocking collectives: 26.8 us -> 31.5 us
  Pallas kernels: 10.5 us -> 9.29 us
    ppermute x1, starting transfers between devices: 8.6 us -> 0.93 us  [local(): lax.ppermute(hidden, 'space', [((i + 1) % bands, i) for i in range(bands)])]
    all_to_all x2, blocking collectives: 26.8 us -> 31.5 us  [gather(): return lax.all_to_all(parts, 'space', 0, 0, tiled=True)]
    ppermute x1, starting transfers between devices: 0.01 us -> 2.47 us  [local(): lax.ppermute(latent, 'space', [(i, (i + 1) % bands) for i in range(bands)])]
    pallas_call x2, Pallas kernels: 6.89 us -> 5.71 us  [the longest x1 3.05 us: local(): call(first_kernel, [SMEM] + [VMEM] * 8, [(latent.shape, BF16), parts_out]...]
where the time goes in v7:
time: 59.7 us; the launch traced here: 59.5 us
  blocking collectives  31.5 us (53%)
  starting transfers between devices  12.6 us (21%)
  Pallas kernels  9.29 us (16%)
  waiting for transfers between devices  5.99 us (10%)
    all_to_all x2, blocking collectives, gather(): return lax.all_to_all(parts, 'space', 0, 0, tiled=True)  31.5 us
    ppermute x3, starting transfers between devices, local(): got[step] = lax.ppermute(got[step], 'tm', along)  5.06 us
    ppermute x3, waiting for transfers between devices, local(): got[step] = lax.ppermute(got[step], 'tm', along)  5 us
    ppermute x1, starting transfers between devices, local(): got = lax.ppermute(send, 'tm', [(i, i ^ 1) for i in range(clips)])  4.18 us
    pallas_call x1, Pallas kernels, local(): call(first_kernel, [SMEM] + [VMEM] * 8, [(latent.shape, BF16), parts_out]...  3.05 us
    pallas_call x1, Pallas kernels, local(): call(second_kernel, [SMEM] * 2 + [VMEM] * 9, [half, half], work)  2.66 us
    ppermute x1, starting transfers between devices, local(): lax.ppermute(latent, 'space', [(i, (i + 1) % bands) for i in range(bands)])  2.47 us
    pallas_call x1, Pallas kernels, local(): call(stats_kernel, [HBM] * (3 + len(vectors)), outs, [pltpu.SMEM(clip_fra...  1.68 us
  transfers between devices with their start and end apart: 6, of which 3 were waited for; matrix products, arithmetic and copies ran while one was open for 0% of the time, Pallas kernels for 3%

profile of v7, /device:TPU:1, one launch (start us, length us, event | category | flops | bytes accessed | tf_op | source)
XLA Modules:
  0.0 59.5 jit_solution(3259535113559854877)
XLA Ops:
  0.0 2.5 %collective-permute-start = (bf16[4,2,64,256]{3,2,1,0:T(8,128)(2,1)}, bf16[4,2,64,256]{3,2,1,0:T(8,128)(2,1)S(1)}, u32[]{:S(2)}, u32[]{:S(2)}) collective-permute-start(bf16[4,2,64,256]{3,2,1,0:T(8,128)(2,1)} %latent_hbm.1), channel_id=1, source_target_pairs={{0,1},{1,2},{2,3},{3,4},{4,5},{5,6},{6,7},{7,8},{8,9},{9,10},{10,1... | collective-permute-start | bytes 786440 | tf_op jit(solution)/shard_map/ppermute | solution.py:289
  2.5 0.0 copy-start
  2.5 1.7 %shard_map.118 = (f32[32,1,128]{2,1,0:T(1,128)S(1)}, bf16[4,2,64,256]{3,2,1,0:T(8,128)(2,1)S(1)}, s32[8]{0:T(128)S(1)}, s32[8]{0:T(128)S(1)}, s32[1,256]{1,0:T(1...) custom-call(s32[8]{0:T(128)} %frames_hbm.1, ...), custom_call_target="tpu_custom_call" | custom-call | flops 4294967296 | bytes 16777216 | tf_op jit(solution)/shard_map/pallas_call | solution.py:293
  4.2 0.0 copy-start.1
  4.2 18.8 %all_to_all.10.parts_ref = f32[32,1,128]{2,1,0:T(1,128)S(1)} all-to-all(f32[32,1,128]{2,1,0:T(1,128)S(1)} %get-tuple-element.26), channel_id=1, replica_groups=mesh['tm'=8,'space'=32] {'space'}, dimensions={0} | all-to-all | bytes 32768 | tf_op jit(solution)/shard_map/all_to_all | solution.py:284
  23.0 0.0 collective-permute-done.above_ref
  23.0 0.0 copy-done
  23.0 3.0 %shard_map.119 = (bf16[4,2,64,256]{3,2,1,0:T(8,128)(2,1)S(1)}, f32[32,1,128]{2,1,0:T(1,128)S(1)}) custom-call(s32[8]{0:T(128)S(1)} %get-tuple-element.24.frames_ref, f32[32,1,128]{2,1,0:T(1,128)S(1)} %all_to_all.10.parts_ref, bf16[4,2,64,256]{3,2,1,0:T(8,128)(2,1)S(1)} %get-tuple-element.27.field_ref.latent_ref, ...), custom_call_target="tpu_custom_call" | custom-call | tf_op jit(solution)/shard_map/pallas_call | solution.py:300
  26.1 0.9 %collective-permute-start.1 = (bf16[4,2,64,256]{3,2,1,0:T(8,128)(2,1)S(1)}, bf16[4,2,64,256]{3,2,1,0:T(8,128)(2,1)S(1)}, u32[]{:S(2)}, u32[]{:S(2)}) collective-permute-start(bf16[4,2,64,256]{3,2,1,0:T(8,128)(2,1)S(1)} %get-tuple-element.33.hidden_ref), channel_id=1, source_target_pairs={{1,0},{2,1},{3,2},{4,3},{5,4},{6,5},{7,6},{8,7},{9,8},{10,9},{11,1... | collective-permute-start | bytes 786440 | tf_op jit(solution)/shard_map/ppermute | solution.py:303
  27.0 12.7 %all_to_all.11.parts_ref = f32[32,1,128]{2,1,0:T(1,128)S(1)} all-to-all(f32[32,1,128]{2,1,0:T(1,128)S(1)} %get-tuple-element.32), channel_id=1, replica_groups=mesh['tm'=8,'space'=32] {'space'}, dimensions={0} | all-to-all | bytes 32768 | tf_op jit(solution)/shard_map/all_to_all | solution.py:284
  39.7 0.0 collective-permute-done.1.below_ref
  39.7 0.0 copy-done.1
  39.7 2.7 %shard_map.120 = (bf16[2,2,64,256]{3,2,1,0:T(8,128)(2,1)S(1)}, bf16[2,2,64,256]{3,2,1,0:T(8,128)(2,1)S(1)}) custom-call(s32[8]{0:T(128)S(1)} %get-tuple-element.24.frames_ref, s32[8]{0:T(128)S(1)} %get-tuple-element.25.rank_ref, f32[32,1,128]{2,1,0:T(1,128)S(1)} %all_to_all.11.parts_ref, bf16[4,2,64,256]{3,2,1,0:T(8,128)(2,1)S(1)} %get-tuple-element.33.hidden_ref, ...), custom_call_target="tpu_custom_call" | custom-call | tf_op jit(solution)/shard_map/pallas_call | solution.py:306
  42.4 4.2 %collective-permute-start.2 = (bf16[2,2,64,256]{3,2,1,0:T(8,128)(2,1)S(1)}, bf16[2,2,64,256]{3,2,1,0:T(8,128)(2,1)S(1)}, u32[]{:S(2)}, u32[]{:S(2)}) collective-permute-start(bf16[2,2,64,256]{3,2,1,0:T(8,128)(2,1)S(1)} %get-tuple-element.38), channel_id=1, source_target_pairs={{0,32},{32,0},{64,96},{96,64},{128,160},{160,128},{192,224},{224,1... | collective-permute-start | bytes 393224 | tf_op jit(solution)/shard_map/ppermute | solution.py:309
  46.6 1.0 %collective-permute-done.2.got_ref = bf16[2,2,64,256]{3,2,1,0:T(8,128)(2,1)S(1)} collective-permute-done((bf16[2,2,64,256]{3,2,1,0:T(8,128)(2,1)S(1)}, bf16[2,2,64,256]{3,2,1,0:T(8,128)(2,1)S(1)}, u32[]{:S(2)}, u32[]{:S(2)}) %collective-permute-start.2) | collective-permute-done | bytes 131104 | tf_op jit(solution)/shard_map/ppermute | solution.py:309
  47.5 0.6 %shard_map.121 = (bf16[2,2,64,256]{3,2,1,0:T(8,128)(2,1)S(1)}, bf16[2,2,64,256]{3,2,1,0:T(8,128)(2,1)S(1)}, bf16[2,2,64,256]{3,2,1,0:T(8,128)(2,1)S(1)}, bf16[2,2,64,256]{3,2,1,0:T(8,128)(2,1)S(1)}) custom-call(s32[8]{0:T(128)S(1)} %get-tuple-element.24.frames_ref, s32[8]{0:T(128)S(1)} %get-tuple-element.25.rank_ref, ...), custom_call_target="tpu_custom_call" | custom-call | tf_op jit(solution)/shard_map/pallas_call | solution.py:311
  48.2 1.4 %collective-permute-start.3 = (bf16[2,2,64,256]{3,2,1,0:T(8,128)(2,1)S(1)}, bf16[2,2,64,256]{3,2,1,0:T(8,128)(2,1)S(1)}, u32[]{:S(2)}, u32[]{:S(2)}) collective-permute-start(bf16[2,2,64,256]{3,2,1,0:T(8,128)(2,1)S(1)} %get-tuple-element.40), channel_id=1, source_target_pairs={{0,64},{32,96},{64,128},{96,160},{128,192},{160,224},{192,0},{224,... | collective-permute-start | bytes 393224 | tf_op jit(solution)/shard_map/ppermute | solution.py:314
  49.5 2.6 %collective-permute-start.4 = (bf16[2,2,64,256]{3,2,1,0:T(8,128)(2,1)S(1)}, bf16[2,2,64,256]{3,2,1,0:T(8,128)(2,1)S(1)}, u32[]{:S(2)}, u32[]{:S(2)}) collective-permute-start(bf16[2,2,64,256]{3,2,1,0:T(8,128)(2,1)S(1)} %get-tuple-element.41), channel_id=1, source_target_pairs={{0,128},{32,160},{64,192},{96,224},{128,0},{160,32},{192,64},{224,... | collective-permute-start | bytes 393224 | tf_op jit(solution)/shard_map/ppermute | solution.py:314
  52.1 1.1 %collective-permute-start.5 = (bf16[2,2,64,256]{3,2,1,0:T(8,128)(2,1)S(1)}, bf16[2,2,64,256]{3,2,1,0:T(8,128)(2,1)S(1)}, u32[]{:S(2)}, u32[]{:S(2)}) collective-permute-start(bf16[2,2,64,256]{3,2,1,0:T(8,128)(2,1)S(1)} %get-tuple-element.42), channel_id=1, source_target_pairs={{0,192},{32,224},{64,0},{96,32},{128,64},{160,96},{192,128},{224,1... | collective-permute-start | bytes 393224 | tf_op jit(solution)/shard_map/ppermute | solution.py:314
  53.2 1.1 %collective-permute-done.3.rest_1_ = bf16[2,2,64,256]{3,2,1,0:T(8,128)(2,1)S(1)} collective-permute-done((bf16[2,2,64,256]{3,2,1,0:T(8,128)(2,1)S(1)}, bf16[2,2,64,256]{3,2,1,0:T(8,128)(2,1)S(1)}, u32[]{:S(2)}, u32[]{:S(2)}) %collective-permute-start.3) | collective-permute-done | bytes 131104 | tf_op jit(solution)/shard_map/ppermute | solution.py:314
  54.3 3.9 %collective-permute-done.4.rest_2_ = bf16[2,2,64,256]{3,2,1,0:T(8,128)(2,1)S(1)} collective-permute-done((bf16[2,2,64,256]{3,2,1,0:T(8,128)(2,1)S(1)}, bf16[2,2,64,256]{3,2,1,0:T(8,128)(2,1)S(1)}, u32[]{:S(2)}, u32[]{:S(2)}) %collective-permute-start.4) | collective-permute-done | bytes 131104 | tf_op jit(solution)/shard_map/ppermute | solution.py:314
  58.2 0.0 collective-permute-done.5.rest_3_
  58.2 1.3 %shard_map.122 = bf16[2,2,64,256]{3,2,1,0:T(8,128)(2,1)} custom-call(s32[8]{0:T(128)S(1)} %get-tuple-element.24.frames_ref, s32[8]{0:T(128)S(1)} %get-tuple-element.25.rank_ref, bf16[2,2,64,256]{3,2,1,0:T(8,128)(2,1)S(1)} %get-tuple-element.39.rest_0_, bf16[2,2,64,256]{3,2,1,0:T(8,128)(2,1)S(1)} %collective-permute-done.3.rest_1_, ...), custom_call_target="tpu_custom_call" | custom-call | tf_op jit(solution)/shard_map/pallas_call | solution.py:315
Async XLA Ops:
  0.0 23.0 %collective-permute-start = (bf16[4,2,64,256]{3,2,1,0:T(8,128)(2,1)}, bf16[4,2,64,256]{3,2,1,0:T(8,128)(2,1)S(1)}, u32[]{:S(2)}, u32[]{:S(2)}) collective-permute-start(bf16[4,2,64,256]{3,2,1,0:T(8,128)(2,1)} %latent_hbm.1), channel_id=1, source_target_pairs={{0,1},{1,2},{2,3},{3,4},{4,5},{5,6},{6,7},{7,8},{8,9},{9,10},{10,1... | collective-permute-start | bytes 786440 | tf_op jit(solution)/shard_map/ppermute | solution.py:289
  2.5 20.5 %copy-start = (bf16[3,3,3,256,256]{4,3,2,1,0:T(8,128)(2,1)S(1)}, bf16[3,3,3,256,256]{4,3,2,1,0:T(8,128)(2,1)}, u32[]{:S(2)}) copy-start(bf16[3,3,3,256,256]{4,3,2,1,0:T(8,128)(2,1)} %param.18) | copy-start | bytes 10616836
  4.2 35.5 %copy-start.1 = (bf16[3,3,3,256,256]{4,3,2,1,0:T(8,128)(2,1)S(1)}, bf16[3,3,3,256,256]{4,3,2,1,0:T(8,128)(2,1)}, u32[]{:S(2)}) copy-start(bf16[3,3,3,256,256]{4,3,2,1,0:T(8,128)(2,1)} %param.22) | copy-start | bytes 10616836
  26.1 13.6 %collective-permute-start.1 = (bf16[4,2,64,256]{3,2,1,0:T(8,128)(2,1)S(1)}, bf16[4,2,64,256]{3,2,1,0:T(8,128)(2,1)S(1)}, u32[]{:S(2)}, u32[]{:S(2)}) collective-permute-start(bf16[4,2,64,256]{3,2,1,0:T(8,128)(2,1)S(1)} %get-tuple-element.33.hidden_ref), channel_id=1, source_target_pairs={{1,0},{2,1},{3,2},{4,3},{5,4},{6,5},{7,6},{8,7},{9,8},{10,9},{11,1... | collective-permute-start | bytes 786440 | tf_op jit(solution)/shard_map/ppermute | solution.py:303
  42.4 5.2 %collective-permute-start.2 = (bf16[2,2,64,256]{3,2,1,0:T(8,128)(2,1)S(1)}, bf16[2,2,64,256]{3,2,1,0:T(8,128)(2,1)S(1)}, u32[]{:S(2)}, u32[]{:S(2)}) collective-permute-start(bf16[2,2,64,256]{3,2,1,0:T(8,128)(2,1)S(1)} %get-tuple-element.38), channel_id=1, source_target_pairs={{0,32},{32,0},{64,96},{96,64},{128,160},{160,128},{192,224},{224,1... | collective-permute-start | bytes 393224 | tf_op jit(solution)/shard_map/ppermute | solution.py:309
  48.2 6.1 %collective-permute-start.3 = (bf16[2,2,64,256]{3,2,1,0:T(8,128)(2,1)S(1)}, bf16[2,2,64,256]{3,2,1,0:T(8,128)(2,1)S(1)}, u32[]{:S(2)}, u32[]{:S(2)}) collective-permute-start(bf16[2,2,64,256]{3,2,1,0:T(8,128)(2,1)S(1)} %get-tuple-element.40), channel_id=1, source_target_pairs={{0,64},{32,96},{64,128},{96,160},{128,192},{160,224},{192,0},{224,... | collective-permute-start | bytes 393224 | tf_op jit(solution)/shard_map/ppermute | solution.py:314
  49.5 8.7 %collective-permute-start.4 = (bf16[2,2,64,256]{3,2,1,0:T(8,128)(2,1)S(1)}, bf16[2,2,64,256]{3,2,1,0:T(8,128)(2,1)S(1)}, u32[]{:S(2)}, u32[]{:S(2)}) collective-permute-start(bf16[2,2,64,256]{3,2,1,0:T(8,128)(2,1)S(1)} %get-tuple-element.41), channel_id=1, source_target_pairs={{0,128},{32,160},{64,192},{96,224},{128,0},{160,32},{192,64},{224,... | collective-permute-start | bytes 393224 | tf_op jit(solution)/shard_map/ppermute | solution.py:314
  52.1 6.1 %collective-permute-start.5 = (bf16[2,2,64,256]{3,2,1,0:T(8,128)(2,1)S(1)}, bf16[2,2,64,256]{3,2,1,0:T(8,128)(2,1)S(1)}, u32[]{:S(2)}, u32[]{:S(2)}) collective-permute-start(bf16[2,2,64,256]{3,2,1,0:T(8,128)(2,1)S(1)} %get-tuple-element.42), channel_id=1, source_target_pairs={{0,192},{32,224},{64,0},{96,32},{128,64},{160,96},{192,128},{224,1... | collective-permute-start | bytes 393224 | tf_op jit(solution)/shard_map/ppermute | solution.py:314

commit v8 on v7

v8 whole, which is shorter than its diff:
```python
import functools

import jax
import jax.numpy as jnp
from jax import lax
from jax.experimental import pallas as pl
from jax.experimental.pallas import tpu as pltpu
from jax.sharding import PartitionSpec as P

G = 32
LANES = 128
EPSILON = 1e-06
F32 = jnp.float32
BF16 = jnp.bfloat16
VMEM = pl.BlockSpec(memory_space=pltpu.VMEM)
SMEM = pl.BlockSpec(memory_space=pltpu.SMEM)
HBM = pl.BlockSpec(memory_space=pltpu.HBM)
ANY = pl.BlockSpec(memory_space=pl.ANY)
LIMIT = 20 * 1024 * 1024


def member_rows(group_row):
    rows = lax.broadcasted_iota(jnp.int32, (LANES, group_row.shape[1]), 0)
    return ((rows == group_row) | (rows - G == group_row)).astype(F32).astype(BF16)


def clip_start_of(frames_ref, rank_ref, clip):
    start = jnp.int32(0)
    for k in range(frames_ref.shape[0]):
        start = start + jnp.where(rank_ref[k] < rank_ref[clip], frames_ref[k], 0)
    return start


def in_thirds(row):
    first = row.astype(BF16)
    row = row - first.astype(F32)
    second = row.astype(BF16)
    return [first, second, (row - second.astype(F32)).astype(BF16)]


def dot_rows(rows, members, side):
    pieces = [piece for row in rows for piece in in_thirds(row)]
    pad = jnp.zeros((16 - len(pieces), pieces[0].shape[1]), BF16)
    left = jnp.concatenate(pieces + [pad], axis=0)
    product = lax.dot_general(left, members, (((1,), (side,)), ((), ())), preferred_element_type=F32)
    return [jnp.sum(product[3 * i : 3 * i + 3], axis=0, keepdims=True) for i in range(len(rows))]


def local_stats(field_ref, length_row, group_row):
    frames, height, columns, channels = field_ref.shape
    pixels = height * columns
    entries = length_row * float(pixels)
    live = [jnp.where(length_row > f, 1.0, 0.0) for f in range(frames)]
    members = member_rows(group_row)
    share = float(G) / channels

    def frame(f):
        return field_ref[f].astype(F32).reshape(pixels, channels)

    mean = jnp.zeros((1, channels), F32)
    for f in range(frames):
        mean = mean + live[f] * jnp.sum(frame(f), axis=0, keepdims=True)
    mean = mean * (1.0 / entries)
    (group_mean,) = dot_rows([mean], members, 1)
    group_mean = group_mean * share
    lane = lax.broadcasted_iota(jnp.int32, (1, LANES), 1)
    group_mean = jnp.where(lane < G, group_mean, 0.0)
    (mean_back,) = dot_rows([group_mean], members, 0)
    spread = jnp.zeros((1, channels), F32)
    for f in range(frames):
        centred = frame(f) - mean
        spread = spread + live[f] * jnp.sum(centred * centred, axis=0, keepdims=True)
    away = mean - mean_back
    (group_spread,) = dot_rows([spread + away * away * entries], members, 1)
    return jnp.where(lane < G, group_mean, group_spread)


def combine_stats(parts, length_row, pixels, group_row):
    bands = parts.shape[0]
    channels = group_row.shape[1]
    per_band = length_row * float(pixels * (channels // G))
    lane = lax.broadcasted_iota(jnp.int32, (1, LANES), 1)
    sums = jnp.sum(parts, axis=0, keepdims=True)
    mean = sums * (1.0 / bands)
    away = parts - mean
    between = jnp.sum(away * away, axis=0, keepdims=True) * per_band[:, :LANES]
    spread = jnp.where(lane < G, between, jnp.where(lane < 2 * G, sums, 0.0))
    mean = jnp.where(lane < G, mean, 0.0)
    mean_back, spread_back = dot_rows([mean, spread], member_rows(group_row), 0)
    return mean_back, lax.rsqrt(spread_back / (per_band * bands) + EPSILON)


def activate(rows, act_ref, slope, offset, f):
    channels = slope.shape[1]
    for r in range(act_ref.shape[0]):
        half = rows(f, r).astype(F32) * slope + offset
        act = half * jnp.tanh(half) + half
        left = jnp.concatenate([act[:1], act[:-1]], axis=0)
        right = jnp.concatenate([act[1:], act[-1:]], axis=0)
        for step, taken in enumerate((left, act, right)):
            act_ref[r, :, step * channels : (step + 1) * channels] = taken.astype(BF16)


def convolve(rows, act_refs, weight_ref, acc_refs, slope, offset, taken):
    frames = len(act_refs)
    _, columns, width = act_refs[0].shape
    ready = 0
    for back_step, acc_ref in enumerate(acc_refs):
        used = frames - 2 + back_step
        for f in range(ready, used):
            activate(rows, act_refs[f], slope, offset, f)
        ready = used
        slabs = []
        for places in taken:
            pieces = [act_refs[f][place] for f in range(used) for place in places]
            slabs.append(jnp.concatenate(pieces, axis=0))
        kernel = weight_ref[3 * back_step : 3 * back_step + 3].reshape(3 * width, -1)
        part = jnp.dot(jnp.concatenate(slabs, axis=1), kernel, preferred_element_type=F32)
        acc_ref[...] = part.reshape(acc_ref.shape)


def frame_sum(acc_refs, f, zero):
    return acc_refs[0][max(f - 2, 0) + zero] + acc_refs[1][max(f - 1, 0) + zero] + acc_refs[2][f + zero]


def band_ends():
    band = lax.axis_index("space")
    return band == 0, band == lax.axis_size("space") - 1


def in_hbm(array):
    return pltpu.with_memory_space_constraint(array, pltpu.HBM)


def plan_row(frames_ref, rank_ref):
    count = frames_ref.shape[0]
    starts = [clip_start_of(frames_ref, rank_ref, k) for k in range(count)]
    clip = lax.axis_index("tm")
    core = lax.rem(clip, 2)
    other = clip + 1 - 2 * core
    chips = count // 2

    def entry(values, index):
        taken = jnp.int32(0)
        for k, value in enumerate(values):
            taken = taken + jnp.where(index == k, value, 0)
        return taken

    plan = [lax.rem(entry(starts, clip), 4), entry(starts, other), frames_ref[other]]
    for slot in range(2):
        place = 2 * clip + slot
        source = jnp.int32(0)
        for k, start in enumerate(starts):
            source = source + jnp.where((place >= start) & (place < start + frames_ref[k]), k // 2, 0)
        plan.append(lax.rem(clip // 2 - source + chips, chips))
    lane = lax.broadcasted_iota(jnp.int32, (1, LANES), 1)
    row = jnp.zeros((1, LANES), jnp.int32)
    for k, value in enumerate(plan):
        row = jnp.where(lane == k, value, row)
    return row


def stats_kernel(frames_hbm, rank_hbm, latent_hbm, *rest):
    rows = len(rest) // 2 - 3
    rows_hbm, rest = rest[:rows], rest[rows:]
    parts_ref, latent_ref, plan_ref, length_ref = rest[:4]
    rows_ref, (frames_ref, rank_ref, sem) = rest[4 : 4 + rows], rest[4 + rows :]
    group_ref = rows_ref[0]
    pairs = [(frames_hbm, frames_ref), (rank_hbm, rank_ref), (latent_hbm, latent_ref)] + list(zip(rows_hbm, rows_ref))
    copies = [pltpu.make_async_copy(source, target, sem.at[i]) for i, (source, target) in enumerate(pairs)]
    for copy in copies:
        copy.start()
    for copy in copies[:4]:
        copy.wait()
    length = frames_ref[lax.axis_index("tm")].astype(F32)
    length_row = jnp.full(length_ref.shape, length, F32)
    length_ref[...] = length_row
    row = local_stats(latent_ref, length_row, group_ref[...])
    parts_ref[...] = jnp.broadcast_to(row[None], parts_ref.shape)
    plan_ref[...] = plan_row(frames_ref, rank_ref)
    for copy in copies[4:]:
        copy.wait()


def first_kernel(
    length_ref, parts_ref, field_ref, above_ref, group_ref, gain_ref, shift_ref, bias_ref, weight_ref,
    hidden_ref, out_parts_ref,
    *work_refs,
):
    frames, height, columns, channels = field_ref.shape
    zero = jnp.minimum(lax.axis_index("tm"), 0)
    top, _ = band_ends()
    taken = [(0, jnp.where(top, 2, 1)), (1, 2), (jnp.where(top, 1, 2), 3)]
    mean, inverse = combine_stats(parts_ref[:, 0], length_ref[...], height * columns, group_ref[...])
    slope = inverse * gain_ref[...] * 0.5
    offset = shift_ref[...] * 0.5 - mean * slope

    def rows(f, r):
        return above_ref[f, r] if r < 2 else field_ref[f, r - 2]

    act_refs, acc_refs = work_refs[:frames], work_refs[frames:]
    convolve(rows, act_refs, weight_ref, acc_refs, slope, offset, taken)
    for f in range(frames):
        hidden_ref[f] = (frame_sum(acc_refs, f, zero) + bias_ref[...]).astype(BF16)
    row = local_stats(hidden_ref, length_ref[...], group_ref[...])
    out_parts_ref[...] = jnp.broadcast_to(row[None], out_parts_ref.shape)


def second_kernel(
    plan_vmem, length_ref, parts_ref, hidden_ref, below_ref, latent_ref, group_ref, gain_ref, shift_ref, bias_ref,
    weight_ref,
    keep_ref, send_ref,
    plan_ref, sem, *work_refs,
):
    plan_copy = pltpu.make_async_copy(plan_vmem, plan_ref, sem)
    plan_copy.start()
    frames, height, columns, channels = latent_ref.shape
    clip = lax.axis_index("tm")
    core = lax.rem(clip, 2)
    zero = jnp.minimum(clip, 0)
    top, bottom = band_ends()
    taken = [(jnp.where(top, 1, 0), 1), (1, 2), (2, jnp.where(bottom, 2, 3))]
    mean, inverse = combine_stats(parts_ref[:, 0], length_ref[...], height * columns, group_ref[...])
    slope = inverse * gain_ref[...] * 0.5
    offset = shift_ref[...] * 0.5 - mean * slope

    def rows(f, r):
        return hidden_ref[f, r] if r < 2 else below_ref[f, r - 2]

    act_refs, acc_refs = work_refs[:frames], work_refs[frames:]
    convolve(rows, act_refs, weight_ref, acc_refs, slope, offset, taken)
    plan_copy.wait()
    for f in range(frames):
        total = (latent_ref[f].astype(F32) + (frame_sum(acc_refs, f, zero) + bias_ref[...])).astype(BF16)
        place = lax.rem(plan_ref[0, 0] + f, 4)
        slot = lax.rem(place, 2)
        stays = place // 2 == core

        @pl.when(stays)
        def _():
            keep_ref[slot] = total

        @pl.when(jnp.logical_not(stays))
        def _():
            send_ref[slot] = total


def spread_kernel(plan_ref, keep_ref, got_ref, *out_refs):
    clip = lax.axis_index("tm")
    core = lax.rem(clip, 2)
    chips = len(out_refs)
    start, length = plan_ref[0, 1], plan_ref[0, 2]
    for step, out_ref in enumerate(out_refs):
        chip = lax.rem(clip // 2 + step, chips)
        for slot in range(2):
            place = 4 * chip + 2 * core + slot - start
            theirs = (place >= 0) & (place < length)
            out_ref[slot] = jnp.where(theirs, got_ref[slot], keep_ref[slot])


def pick_kernel(plan_ref, *rest):
    *got_refs, out_hbm, sem = rest
    copies = []
    for slot in range(2):
        step = plan_ref[0, 3 + slot]
        for k, got_ref in enumerate(got_refs):
            copy = pltpu.make_async_copy(got_ref.at[slot], out_hbm.at[slot], sem.at[slot])
            pl.when(step == k)(copy.start)
        copies.append(copy)
    for copy in copies:
        copy.wait()


def call(kernel, in_specs, outs, scratch=(), out_spec=VMEM, cost=None):
    return pl.pallas_call(
        kernel,
        in_specs=in_specs,
        out_specs=[out_spec] * len(outs),
        out_shape=[jax.ShapeDtypeStruct(shape, kind) for shape, kind in outs],
        scratch_shapes=list(scratch),
        compiler_params=pltpu.CompilerParams(vmem_limit_bytes=LIMIT),
        cost_estimate=cost,
    )


def local(
    latent,
    clip_frames,
    clip_rank,
    group_of,
    gain_first,
    shift_first,
    conv_first,
    bias_first,
    gain_second,
    shift_second,
    conv_second,
    bias_second,
):
    frames, height, columns, channels = latent.shape
    bands = lax.axis_size("space")
    clips = lax.axis_size("tm")
    row = lambda v: v.reshape(1, channels)
    taps = lambda k: k.reshape(9, 3 * channels, channels)
    group_row = row(group_of)
    parts_out = ((bands, 1, LANES), F32)

    def gather(parts):
        return lax.all_to_all(parts, "space", 0, 0, tiled=True)

    work = [pltpu.VMEM((4, columns, 3 * channels), BF16)] * frames
    work += [pltpu.VMEM((frames - 2 + i, height, columns, channels), F32) for i in range(3)]

    above = lax.ppermute(latent, "space", [(i, (i + 1) % bands) for i in range(bands)])
    vectors = [row(v) for v in (group_of, gain_first, shift_first, bias_first, gain_second, shift_second, bias_second)]
    outs = [parts_out, (latent.shape, BF16), ((1, LANES), jnp.int32), ((1, channels), F32)]
    outs += [(v.shape, v.dtype) for v in vectors]
    scalars = pltpu.SMEM(clip_frames.shape, jnp.int32)
    parts, latent, plan, length, *vectors = call(
        stats_kernel, [HBM] * (3 + len(vectors)), outs,
        [scalars, scalars, pltpu.SemaphoreType.DMA((3 + len(vectors),))],
        cost=pl.CostEstimate(flops=1 << 32, bytes_accessed=1 << 24, transcendentals=0),
    )(*map(in_hbm, (clip_frames, clip_rank, latent, *vectors)))
    group_row = vectors[0]
    parts = gather(parts)
    hidden, parts = call(first_kernel, [VMEM] * 9, [(latent.shape, BF16), parts_out], work)(
        length, parts, latent, above, *vectors[:4], taps(conv_first)
    )
    below = lax.ppermute(hidden, "space", [((i + 1) % bands, i) for i in range(bands)])
    parts = gather(parts)
    half = ((2, height, columns, channels), BF16)
    work = [pltpu.SMEM(plan.shape, jnp.int32), pltpu.SemaphoreType.DMA] + work
    keep, send = call(second_kernel, [ANY] + [VMEM] * 10, [half, half], work)(
        plan, length, parts, hidden, below, latent, group_row, *vectors[4:], taps(conv_second),
    )
    got = lax.ppermute(send, "tm", [(i, i ^ 1) for i in range(clips)])
    chips = clips // 2
    got = list(call(spread_kernel, [SMEM] + [VMEM] * 2, [half] * chips)(plan, keep, got))
    for step in range(1, chips):
        along = [(i, (i + 2 * step) % clips) for i in range(clips)]
        got[step] = lax.ppermute(got[step], "tm", along)
    (out,) = call(pick_kernel, [SMEM] + [ANY] * chips, [half], [pltpu.SemaphoreType.DMA((2,))], HBM)(plan, *got)
    return out


def solution(mesh):
    placed = (P("tm", "space", None, None), P(), P(), P(), P(), P(), P(), P(), P(), P(), P(), P())
    return jax.shard_map(
        local, mesh=mesh, in_specs=placed, out_specs=P("tm", "space", None, None), check_vma=False
    )
```

time: 59.7 us -> 58.7 us (0.983)
  Pallas kernels: 9.29 us -> 8.31 us
    pallas_call x5, Pallas kernels: 9.29 us -> 8.31 us  [the longest x1 2.54 us: local(): call(first_kernel, [VMEM] * 9, [(latent.shape, BF16), parts_out], work)]
where the time goes in v8:
time: 58.7 us; the launch traced here: 58.5 us
  blocking collectives  31.5 us (54%)
  starting transfers between devices  12.6 us (21%)
  Pallas kernels  8.31 us (14%)
  waiting for transfers between devices  5.99 us (10%)
    all_to_all x2, blocking collectives, gather(): return lax.all_to_all(parts, 'space', 0, 0, tiled=True)  31.5 us
    ppermute x3, starting transfers between devices, local(): got[step] = lax.ppermute(got[step], 'tm', along)  5.06 us
    ppermute x3, waiting for transfers between devices, local(): got[step] = lax.ppermute(got[step], 'tm', along)  5 us
    ppermute x1, starting transfers between devices, local(): got = lax.ppermute(send, 'tm', [(i, i ^ 1) for i in range(clips)])  4.18 us
    pallas_call x1, Pallas kernels, local(): call(first_kernel, [VMEM] * 9, [(latent.shape, BF16), parts_out], work)  2.54 us
    ppermute x1, starting transfers between devices, local(): lax.ppermute(latent, 'space', [(i, (i + 1) % bands) for i in range(bands)])  2.47 us
    pallas_call x1, Pallas kernels, local(): call(second_kernel, [ANY] + [VMEM] * 10, [half, half], work)  2.3 us
    pallas_call x1, Pallas kernels, local(): call(stats_kernel, [HBM] * (3 + len(vectors)), outs, [scalars, scalars, p...  1.67 us
  transfers between devices with their start and end apart: 6, of which 3 were waited for; matrix products, arithmetic and copies ran while one was open for 0% of the time, Pallas kernels for 3%

profile of v8, /device:TPU:1, one launch (start us, length us, event | category | flops | bytes accessed | tf_op | source)
XLA Modules:
  0.0 58.5 jit_solution(12769556286770740724)
XLA Ops:
  0.0 2.5 %collective-permute-start = (bf16[4,2,64,256]{3,2,1,0:T(8,128)(2,1)}, bf16[4,2,64,256]{3,2,1,0:T(8,128)(2,1)S(1)}, u32[]{:S(2)}, u32[]{:S(2)}) collective-permute-start(bf16[4,2,64,256]{3,2,1,0:T(8,128)(2,1)} %latent_hbm.1), channel_id=1, source_target_pairs={{0,1},{1,2},{2,3},{3,4},{4,5},{5,6},{6,7},{7,8},{8,9},{9,10},{10,1... | collective-permute-start | bytes 786440 | tf_op jit(solution)/shard_map/ppermute | solution.py:314
  2.5 0.0 copy-start.1
  2.5 1.7 %shard_map.118 = (f32[32,1,128]{2,1,0:T(1,128)S(1)}, bf16[4,2,64,256]{3,2,1,0:T(8,128)(2,1)S(1)}, s32[1,128]{1,0:T(1,128)S(1)}, f32[1,256]{1,0:T(1,128)S(1)}, s3...) custom-call(s32[8]{0:T(128)} %frames_hbm.1, ...), custom_call_target="tpu_custom_call" | custom-call | flops 4294967296 | bytes 16777216 | tf_op jit(solution)/shard_map/pallas_call | solution.py:319
  4.1 0.0 copy-start
  4.2 18.8 %all_to_all.10.parts_ref = f32[32,1,128]{2,1,0:T(1,128)S(1)} all-to-all(f32[32,1,128]{2,1,0:T(1,128)S(1)} %get-tuple-element.26), channel_id=1, replica_groups=mesh['tm'=8,'space'=32] {'space'}, dimensions={0} | all-to-all | bytes 32768 | tf_op jit(solution)/shard_map/all_to_all | solution.py:309
  23.0 0.0 collective-permute-done.above_ref
  23.0 0.0 copy-done.1
  23.0 2.5 %shard_map.119 = (bf16[4,2,64,256]{3,2,1,0:T(8,128)(2,1)S(1)}, f32[32,1,128]{2,1,0:T(1,128)S(1)}) custom-call(f32[1,256]{1,0:T(1,128)S(1)} %get-tuple-element.25.length_ref, f32[32,1,128]{2,1,0:T(1,128)S(1)} %all_to_all.10.parts_ref, bf16[4,2,64,256]{3,2,1,0:T(8,128)(2,1)S(1)} %get-tuple-element.27.field_ref.latent_ref, ...), custom_call_target="tpu_custom_call" | custom-call | tf_op jit(solution)/shard_map/pallas_call | solution.py:326
  25.5 0.9 %collective-permute-start.1 = (bf16[4,2,64,256]{3,2,1,0:T(8,128)(2,1)S(1)}, bf16[4,2,64,256]{3,2,1,0:T(8,128)(2,1)S(1)}, u32[]{:S(2)}, u32[]{:S(2)}) collective-permute-start(bf16[4,2,64,256]{3,2,1,0:T(8,128)(2,1)S(1)} %get-tuple-element.33.hidden_ref), channel_id=1, source_target_pairs={{1,0},{2,1},{3,2},{4,3},{5,4},{6,5},{7,6},{8,7},{9,8},{10,9},{11,1... | collective-permute-start | bytes 786440 | tf_op jit(solution)/shard_map/ppermute | solution.py:329
  26.5 12.7 %all_to_all.11.parts_ref = f32[32,1,128]{2,1,0:T(1,128)S(1)} all-to-all(f32[32,1,128]{2,1,0:T(1,128)S(1)} %get-tuple-element.32), channel_id=1, replica_groups=mesh['tm'=8,'space'=32] {'space'}, dimensions={0} | all-to-all | bytes 32768 | tf_op jit(solution)/shard_map/all_to_all | solution.py:309
  39.2 0.0 collective-permute-done.1.below_ref
  39.2 0.0 copy-done
  39.2 2.3 %shard_map.120 = (bf16[2,2,64,256]{3,2,1,0:T(8,128)(2,1)S(1)}, bf16[2,2,64,256]{3,2,1,0:T(8,128)(2,1)S(1)}) custom-call(s32[1,128]{1,0:T(1,128)S(1)} %get-tuple-element.24.plan_vmem.plan_ref, f32[1,256]{1,0:T(1,128)S(1)} %get-tuple-element.25.length_ref, f32[32,1,128]{2,1,0:T(1,128)S(1)} %all_to_all.11.parts_ref, ...), custom_call_target="tpu_custom_call" | custom-call | tf_op jit(solution)/shard_map/pallas_call | solution.py:333
  41.5 4.2 %collective-permute-start.2 = (bf16[2,2,64,256]{3,2,1,0:T(8,128)(2,1)S(1)}, bf16[2,2,64,256]{3,2,1,0:T(8,128)(2,1)S(1)}, u32[]{:S(2)}, u32[]{:S(2)}) collective-permute-start(bf16[2,2,64,256]{3,2,1,0:T(8,128)(2,1)S(1)} %get-tuple-element.38), channel_id=1, source_target_pairs={{0,32},{32,0},{64,96},{96,64},{128,160},{160,128},{192,224},{224,1... | collective-permute-start | bytes 393224 | tf_op jit(solution)/shard_map/ppermute | solution.py:336
  45.6 1.0 %collective-permute-done.2.got_ref = bf16[2,2,64,256]{3,2,1,0:T(8,128)(2,1)S(1)} collective-permute-done((bf16[2,2,64,256]{3,2,1,0:T(8,128)(2,1)S(1)}, bf16[2,2,64,256]{3,2,1,0:T(8,128)(2,1)S(1)}, u32[]{:S(2)}, u32[]{:S(2)}) %collective-permute-start.2) | collective-permute-done | bytes 131104 | tf_op jit(solution)/shard_map/ppermute | solution.py:336
  46.6 0.6 %shard_map.121 = (bf16[2,2,64,256]{3,2,1,0:T(8,128)(2,1)S(1)}, bf16[2,2,64,256]{3,2,1,0:T(8,128)(2,1)S(1)}, bf16[2,2,64,256]{3,2,1,0:T(8,128)(2,1)S(1)}, bf16[2,2,64,256]{3,2,1,0:T(8,128)(2,1)S(1)}) custom-call(s32[1,128]{1,0:T(1,128)S(1)} %get-tuple-element.24.plan_vmem.plan_ref, bf16[2,2,64,256]{3,2,1,0:T(8,128)(2,1)S(1)} %get-tuple-element.37.keep_ref, ...), custom_call_target="tpu_custom_call" | custom-call | tf_op jit(solution)/shard_map/pallas_call | solution.py:338
  47.2 1.4 %collective-permute-start.3 = (bf16[2,2,64,256]{3,2,1,0:T(8,128)(2,1)S(1)}, bf16[2,2,64,256]{3,2,1,0:T(8,128)(2,1)S(1)}, u32[]{:S(2)}, u32[]{:S(2)}) collective-permute-start(bf16[2,2,64,256]{3,2,1,0:T(8,128)(2,1)S(1)} %get-tuple-element.40), channel_id=1, source_target_pairs={{0,64},{32,96},{64,128},{96,160},{128,192},{160,224},{192,0},{224,... | collective-permute-start | bytes 393224 | tf_op jit(solution)/shard_map/ppermute | solution.py:341
  48.6 2.6 %collective-permute-start.4 = (bf16[2,2,64,256]{3,2,1,0:T(8,128)(2,1)S(1)}, bf16[2,2,64,256]{3,2,1,0:T(8,128)(2,1)S(1)}, u32[]{:S(2)}, u32[]{:S(2)}) collective-permute-start(bf16[2,2,64,256]{3,2,1,0:T(8,128)(2,1)S(1)} %get-tuple-element.41), channel_id=1, source_target_pairs={{0,128},{32,160},{64,192},{96,224},{128,0},{160,32},{192,64},{224,... | collective-permute-start | bytes 393224 | tf_op jit(solution)/shard_map/ppermute | solution.py:341
  51.2 1.1 %collective-permute-start.5 = (bf16[2,2,64,256]{3,2,1,0:T(8,128)(2,1)S(1)}, bf16[2,2,64,256]{3,2,1,0:T(8,128)(2,1)S(1)}, u32[]{:S(2)}, u32[]{:S(2)}) collective-permute-start(bf16[2,2,64,256]{3,2,1,0:T(8,128)(2,1)S(1)} %get-tuple-element.42), channel_id=1, source_target_pairs={{0,192},{32,224},{64,0},{96,32},{128,64},{160,96},{192,128},{224,1... | collective-permute-start | bytes 393224 | tf_op jit(solution)/shard_map/ppermute | solution.py:341
  52.3 1.1 %collective-permute-done.3.rest_1_ = bf16[2,2,64,256]{3,2,1,0:T(8,128)(2,1)S(1)} collective-permute-done((bf16[2,2,64,256]{3,2,1,0:T(8,128)(2,1)S(1)}, bf16[2,2,64,256]{3,2,1,0:T(8,128)(2,1)S(1)}, u32[]{:S(2)}, u32[]{:S(2)}) %collective-permute-start.3) | collective-permute-done | bytes 131104 | tf_op jit(solution)/shard_map/ppermute | solution.py:341
  53.4 3.9 %collective-permute-done.4.rest_2_ = bf16[2,2,64,256]{3,2,1,0:T(8,128)(2,1)S(1)} collective-permute-done((bf16[2,2,64,256]{3,2,1,0:T(8,128)(2,1)S(1)}, bf16[2,2,64,256]{3,2,1,0:T(8,128)(2,1)S(1)}, u32[]{:S(2)}, u32[]{:S(2)}) %collective-permute-start.4) | collective-permute-done | bytes 131104 | tf_op jit(solution)/shard_map/ppermute | solution.py:341
  57.3 0.0 collective-permute-done.5.rest_3_
  57.3 1.2 %shard_map.122 = bf16[2,2,64,256]{3,2,1,0:T(8,128)(2,1)} custom-call(s32[1,128]{1,0:T(1,128)S(1)} %get-tuple-element.24.plan_vmem.plan_ref, bf16[2,2,64,256]{3,2,1,0:T(8,128)(2,1)S(1)} %get-tuple-element.39.rest_0_, bf16[2,2,64,256]{3,2,1,0:T(8,128)(2,1)S(1)} %collective-permute-done.3.rest_1_, bf16[2,2,64,256]{3,2,1,0:T(8,128)(2,1)S(1)} %collective-permute-done.4.rest_2_, ...), custom_call_target="tpu_custom_call" | custom-call | tf_op jit(solution)/shard_map/pallas_call | solution.py:342
Async XLA Ops:
  0.0 23.0 %collective-permute-start = (bf16[4,2,64,256]{3,2,1,0:T(8,128)(2,1)}, bf16[4,2,64,256]{3,2,1,0:T(8,128)(2,1)S(1)}, u32[]{:S(2)}, u32[]{:S(2)}) collective-permute-start(bf16[4,2,64,256]{3,2,1,0:T(8,128)(2,1)} %latent_hbm.1), channel_id=1, source_target_pairs={{0,1},{1,2},{2,3},{3,4},{4,5},{5,6},{6,7},{7,8},{8,9},{9,10},{10,1... | collective-permute-start | bytes 786440 | tf_op jit(solution)/shard_map/ppermute | solution.py:314
  2.5 20.5 %copy-start.1 = (bf16[3,3,3,256,256]{4,3,2,1,0:T(8,128)(2,1)S(1)}, bf16[3,3,3,256,256]{4,3,2,1,0:T(8,128)(2,1)}, u32[]{:S(2)}) copy-start(bf16[3,3,3,256,256]{4,3,2,1,0:T(8,128)(2,1)} %param.18) | copy-start | bytes 10616836
  4.1 35.0 %copy-start = (bf16[3,3,3,256,256]{4,3,2,1,0:T(8,128)(2,1)S(1)}, bf16[3,3,3,256,256]{4,3,2,1,0:T(8,128)(2,1)}, u32[]{:S(2)}) copy-start(bf16[3,3,3,256,256]{4,3,2,1,0:T(8,128)(2,1)} %param.22) | copy-start | bytes 10616836
  25.5 13.6 %collective-permute-start.1 = (bf16[4,2,64,256]{3,2,1,0:T(8,128)(2,1)S(1)}, bf16[4,2,64,256]{3,2,1,0:T(8,128)(2,1)S(1)}, u32[]{:S(2)}, u32[]{:S(2)}) collective-permute-start(bf16[4,2,64,256]{3,2,1,0:T(8,128)(2,1)S(1)} %get-tuple-element.33.hidden_ref), channel_id=1, source_target_pairs={{1,0},{2,1},{3,2},{4,3},{5,4},{6,5},{7,6},{8,7},{9,8},{10,9},{11,1... | collective-permute-start | bytes 786440 | tf_op jit(solution)/shard_map/ppermute | solution.py:329
  41.5 5.2 %collective-permute-start.2 = (bf16[2,2,64,256]{3,2,1,0:T(8,128)(2,1)S(1)}, bf16[2,2,64,256]{3,2,1,0:T(8,128)(2,1)S(1)}, u32[]{:S(2)}, u32[]{:S(2)}) collective-permute-start(bf16[2,2,64,256]{3,2,1,0:T(8,128)(2,1)S(1)} %get-tuple-element.38), channel_id=1, source_target_pairs={{0,32},{32,0},{64,96},{96,64},{128,160},{160,128},{192,224},{224,1... | collective-permute-start | bytes 393224 | tf_op jit(solution)/shard_map/ppermute | solution.py:336
  47.2 6.1 %collective-permute-start.3 = (bf16[2,2,64,256]{3,2,1,0:T(8,128)(2,1)S(1)}, bf16[2,2,64,256]{3,2,1,0:T(8,128)(2,1)S(1)}, u32[]{:S(2)}, u32[]{:S(2)}) collective-permute-start(bf16[2,2,64,256]{3,2,1,0:T(8,128)(2,1)S(1)} %get-tuple-element.40), channel_id=1, source_target_pairs={{0,64},{32,96},{64,128},{96,160},{128,192},{160,224},{192,0},{224,... | collective-permute-start | bytes 393224 | tf_op jit(solution)/shard_map/ppermute | solution.py:341
  48.6 8.7 %collective-permute-start.4 = (bf16[2,2,64,256]{3,2,1,0:T(8,128)(2,1)S(1)}, bf16[2,2,64,256]{3,2,1,0:T(8,128)(2,1)S(1)}, u32[]{:S(2)}, u32[]{:S(2)}) collective-permute-start(bf16[2,2,64,256]{3,2,1,0:T(8,128)(2,1)S(1)} %get-tuple-element.41), channel_id=1, source_target_pairs={{0,128},{32,160},{64,192},{96,224},{128,0},{160,32},{192,64},{224,... | collective-permute-start | bytes 393224 | tf_op jit(solution)/shard_map/ppermute | solution.py:341
  51.2 6.1 %collective-permute-start.5 = (bf16[2,2,64,256]{3,2,1,0:T(8,128)(2,1)S(1)}, bf16[2,2,64,256]{3,2,1,0:T(8,128)(2,1)S(1)}, u32[]{:S(2)}, u32[]{:S(2)}) collective-permute-start(bf16[2,2,64,256]{3,2,1,0:T(8,128)(2,1)S(1)} %get-tuple-element.42), channel_id=1, source_target_pairs={{0,192},{32,224},{64,0},{96,32},{128,64},{160,96},{192,128},{224,1... | collective-permute-start | bytes 393224 | tf_op jit(solution)/shard_map/ppermute | solution.py:341

commit v9 on v8

--- a/solution.py
+++ b/solution.py
@@ -132,7 +132,11 @@
     return pltpu.with_memory_space_constraint(array, pltpu.HBM)
 
 
-def plan_row(frames_ref, rank_ref):
+def in_smem(array):
+    return pltpu.with_memory_space_constraint(array, pltpu.SMEM)
+
+
+def plan_of(frames_ref, rank_ref):
     count = frames_ref.shape[0]
     starts = [clip_start_of(frames_ref, rank_ref, k) for k in range(count)]
     clip = lax.axis_index("tm")
@@ -153,11 +157,7 @@
         for k, start in enumerate(starts):
             source = source + jnp.where((place >= start) & (place < start + frames_ref[k]), k // 2, 0)
         plan.append(lax.rem(clip // 2 - source + chips, chips))
-    lane = lax.broadcasted_iota(jnp.int32, (1, LANES), 1)
-    row = jnp.zeros((1, LANES), jnp.int32)
-    for k, value in enumerate(plan):
-        row = jnp.where(lane == k, value, row)
-    return row
+    return plan
 
 
 def stats_kernel(frames_hbm, rank_hbm, latent_hbm, *rest):
@@ -177,18 +177,19 @@
     length_ref[...] = length_row
     row = local_stats(latent_ref, length_row, group_ref[...])
     parts_ref[...] = jnp.broadcast_to(row[None], parts_ref.shape)
-    plan_ref[...] = plan_row(frames_ref, rank_ref)
+    for k, value in enumerate(plan_of(frames_ref, rank_ref)):
+        plan_ref[k] = value
     for copy in copies[4:]:
         copy.wait()
 
 
 def first_kernel(
-    length_ref, parts_ref, field_ref, above_ref, group_ref, gain_ref, shift_ref, bias_ref, weight_ref,
+    plan_ref, length_ref, parts_ref, field_ref, above_ref, group_ref, gain_ref, shift_ref, bias_ref, weight_ref,
     hidden_ref, out_parts_ref,
     *work_refs,
 ):
     frames, height, columns, channels = field_ref.shape
-    zero = jnp.minimum(lax.axis_index("tm"), 0)
+    zero = jnp.minimum(plan_ref[0], 0)
     top, _ = band_ends()
     taken = [(0, jnp.where(top, 2, 1)), (1, 2), (jnp.where(top, 1, 2), 3)]
     mean, inverse = combine_stats(parts_ref[:, 0], length_ref[...], height * columns, group_ref[...])
@@ -207,17 +208,14 @@
 
 
 def second_kernel(
-    plan_vmem, length_ref, parts_ref, hidden_ref, below_ref, latent_ref, group_ref, gain_ref, shift_ref, bias_ref,
+    plan_ref, length_ref, parts_ref, hidden_ref, below_ref, latent_ref, group_ref, gain_ref, shift_ref, bias_ref,
     weight_ref,
     keep_ref, send_ref,
-    plan_ref, sem, *work_refs,
+    *work_refs,
 ):
-    plan_copy = pltpu.make_async_copy(plan_vmem, plan_ref, sem)
-    plan_copy.start()
     frames, height, columns, channels = latent_ref.shape
-    clip = lax.axis_index("tm")
-    core = lax.rem(clip, 2)
-    zero = jnp.minimum(clip, 0)
+    core = lax.rem(lax.axis_index("tm"), 2)
+    zero = jnp.minimum(plan_ref[0], 0)
     top, bottom = band_ends()
     taken = [(jnp.where(top, 1, 0), 1), (1, 2), (2, jnp.where(bottom, 2, 3))]
     mean, inverse = combine_stats(parts_ref[:, 0], length_ref[...], height * columns, group_ref[...])
@@ -229,10 +227,9 @@
 
     act_refs, acc_refs = work_refs[:frames], work_refs[frames:]
     convolve(rows, act_refs, weight_ref, acc_refs, slope, offset, taken)
-    plan_copy.wait()
     for f in range(frames):
         total = (latent_ref[f].astype(F32) + (frame_sum(acc_refs, f, zero) + bias_ref[...])).astype(BF16)
-        place = lax.rem(plan_ref[0, 0] + f, 4)
+        place = lax.rem(plan_ref[0] + f, 4)
         slot = lax.rem(place, 2)
         stays = place // 2 == core
 
@@ -249,7 +246,7 @@
     clip = lax.axis_index("tm")
     core = lax.rem(clip, 2)
     chips = len(out_refs)
-    start, length = plan_ref[0, 1], plan_ref[0, 2]
+    start, length = plan_ref[1], plan_ref[2]
     for step, out_ref in enumerate(out_refs):
         chip = lax.rem(clip // 2 + step, chips)
         for slot in range(2):
@@ -262,7 +259,7 @@
     *got_refs, out_hbm, sem = rest
     copies = []
     for slot in range(2):
-        step = plan_ref[0, 3 + slot]
+        step = plan_ref[3 + slot]
         for k, got_ref in enumerate(got_refs):
             copy = pltpu.make_async_copy(got_ref.at[slot], out_hbm.at[slot], sem.at[slot])
             pl.when(step == k)(copy.start)
@@ -275,8 +272,8 @@
     return pl.pallas_call(
         kernel,
         in_specs=in_specs,
-        out_specs=[out_spec] * len(outs),
-        out_shape=[jax.ShapeDtypeStruct(shape, kind) for shape, kind in outs],
+        out_specs=[out_spec if isinstance(out, tuple) else SMEM for out in outs],
+        out_shape=[jax.ShapeDtypeStruct(*out) if isinstance(out, tuple) else out for out in outs],
         scratch_shapes=list(scratch),
         compiler_params=pltpu.CompilerParams(vmem_limit_bytes=LIMIT),
         cost_estimate=cost,
@@ -313,7 +310,7 @@
 
     above = lax.ppermute(latent, "space", [(i, (i + 1) % bands) for i in range(bands)])
     vectors = [row(v) for v in (group_of, gain_first, shift_first, bias_first, gain_second, shift_second, bias_second)]
-    outs = [parts_out, (latent.shape, BF16), ((1, LANES), jnp.int32), ((1, channels), F32)]
+    outs = [parts_out, (latent.shape, BF16), pltpu.SMEM((8,), jnp.int32), ((1, channels), F32)]
     outs += [(v.shape, v.dtype) for v in vectors]
     scalars = pltpu.SMEM(clip_frames.shape, jnp.int32)
     parts, latent, plan, length, *vectors = call(
@@ -323,23 +320,22 @@
     )(*map(in_hbm, (clip_frames, clip_rank, latent, *vectors)))
     group_row = vectors[0]
     parts = gather(parts)
-    hidden, parts = call(first_kernel, [VMEM] * 9, [(latent.shape, BF16), parts_out], work)(
-        length, parts, latent, above, *vectors[:4], taps(conv_first)
+    hidden, parts = call(first_kernel, [SMEM] + [VMEM] * 9, [(latent.shape, BF16), parts_out], work)(
+        in_smem(plan), length, parts, latent, above, *vectors[:4], taps(conv_first)
     )
     below = lax.ppermute(hidden, "space", [((i + 1) % bands, i) for i in range(bands)])
     parts = gather(parts)
     half = ((2, height, columns, channels), BF16)
-    work = [pltpu.SMEM(plan.shape, jnp.int32), pltpu.SemaphoreType.DMA] + work
-    keep, send = call(second_kernel, [ANY] + [VMEM] * 10, [half, half], work)(
-        plan, length, parts, hidden, below, latent, group_row, *vectors[4:], taps(conv_second),
+    keep, send = call(second_kernel, [SMEM] + [VMEM] * 10, [half, half], work)(
+        in_smem(plan), length, parts, hidden, below, latent, group_row, *vectors[4:], taps(conv_second),
     )
     got = lax.ppermute(send, "tm", [(i, i ^ 1) for i in range(clips)])
     chips = clips // 2
-    got = list(call(spread_kernel, [SMEM] + [VMEM] * 2, [half] * chips)(plan, keep, got))
+    got = list(call(spread_kernel, [SMEM] + [VMEM] * 2, [half] * chips)(in_smem(plan), keep, got))
     for step in range(1, chips):
         along = [(i, (i + 2 * step) % clips) for i in range(clips)]
         got[step] = lax.ppermute(got[step], "tm", along)
-    (out,) = call(pick_kernel, [SMEM] + [ANY] * chips, [half], [pltpu.SemaphoreType.DMA((2,))], HBM)(plan, *got)
+    (out,) = call(pick_kernel, [SMEM] + [ANY] * chips, [half], [pltpu.SemaphoreType.DMA((2,))], HBM)(in_smem(plan), *got)
     return out
 
 

time: 58.7 us -> 57.2 us (0.974)
  Pallas kernels: 8.31 us -> 6.83 us
    pallas_call x3, Pallas kernels: 5.43 us -> 4.49 us  [the longest x1 2.44 us: local(): call(first_kernel, [SMEM] + [VMEM] * 9, [(latent.shape, BF16), parts_out]...]
where the time goes in v9:
time: 57.2 us; the launch traced here: 57 us
  blocking collectives  31.5 us (55%)
  starting transfers between devices  12.6 us (22%)
  Pallas kernels  6.83 us (12%)
  waiting for transfers between devices  5.99 us (10%)
    all_to_all x2, blocking collectives, gather(): return lax.all_to_all(parts, 'space', 0, 0, tiled=True)  31.5 us
    ppermute x3, starting transfers between devices, local(): got[step] = lax.ppermute(got[step], 'tm', along)  5.06 us
    ppermute x3, waiting for transfers between devices, local(): got[step] = lax.ppermute(got[step], 'tm', along)  5 us
    ppermute x1, starting transfers between devices, local(): got = lax.ppermute(send, 'tm', [(i, i ^ 1) for i in range(clips)])  4.18 us
    ppermute x1, starting transfers between devices, local(): lax.ppermute(latent, 'space', [(i, (i + 1) % bands) for i in range(bands)])  2.47 us
    pallas_call x1, Pallas kernels, local(): call(first_kernel, [SMEM] + [VMEM] * 9, [(latent.shape, BF16), parts_out]...  2.44 us
    pallas_call x1, Pallas kernels, local(): call(second_kernel, [SMEM] + [VMEM] * 10, [half, half], work)  1.99 us
    pallas_call x1, Pallas kernels, local(): call(stats_kernel, [HBM] * (3 + len(vectors)), outs, [scalars, scalars, p...  1.67 us
  transfers between devices with their start and end apart: 6, of which 3 were waited for; matrix products, arithmetic and copies ran while one was open for 0% of the time, Pallas kernels for 3%

profile of v9, /device:TPU:1, one launch (start us, length us, event | category | flops | bytes accessed | tf_op | source)
XLA Modules:
  0.0 57.0 jit_solution(7223615155744373401)
XLA Ops:
  0.0 2.5 %collective-permute-start = (bf16[4,2,64,256]{3,2,1,0:T(8,128)(2,1)}, bf16[4,2,64,256]{3,2,1,0:T(8,128)(2,1)S(1)}, u32[]{:S(2)}, u32[]{:S(2)}) collective-permute-start(bf16[4,2,64,256]{3,2,1,0:T(8,128)(2,1)} %latent_hbm.1), channel_id=1, source_target_pairs={{0,1},{1,2},{2,3},{3,4},{4,5},{5,6},{6,7},{7,8},{8,9},{9,10},{10,1... | collective-permute-start | bytes 786440 | tf_op jit(solution)/shard_map/ppermute | solution.py:311
  2.5 0.0 copy-start.1
  2.5 1.7 %shard_map.118 = (f32[32,1,128]{2,1,0:T(1,128)S(1)}, bf16[4,2,64,256]{3,2,1,0:T(8,128)(2,1)S(1)}, s32[8]{0:T(128)S(4)}, f32[1,256]{1,0:T(1,128)S(1)}, s32[1,256]...) custom-call(s32[8]{0:T(128)} %frames_hbm.1, ...), custom_call_target="tpu_custom_call" | custom-call | flops 4294967296 | bytes 16777216 | tf_op jit(solution)/shard_map/pallas_call | solution.py:316
  4.1 0.0 copy-start
  4.2 18.8 %all_to_all.10.parts_ref = f32[32,1,128]{2,1,0:T(1,128)S(1)} all-to-all(f32[32,1,128]{2,1,0:T(1,128)S(1)} %get-tuple-element.26), channel_id=1, replica_groups=mesh['tm'=8,'space'=32] {'space'}, dimensions={0} | all-to-all | bytes 32768 | tf_op jit(solution)/shard_map/all_to_all | solution.py:306
  23.0 0.0 collective-permute-done.above_ref
  23.0 0.0 copy-done.1
  23.0 2.4 %shard_map.119 = (bf16[4,2,64,256]{3,2,1,0:T(8,128)(2,1)S(1)}, f32[32,1,128]{2,1,0:T(1,128)S(1)}) custom-call(s32[8]{0:T(128)S(4)} %get-tuple-element.24.plan_ref, f32[1,256]{1,0:T(1,128)S(1)} %get-tuple-element.25.length_ref, f32[32,1,128]{2,1,0:T(1,128)S(1)} %all_to_all.10.parts_ref, bf16[4,2,64,256]{3,2,1,0:T(8,128)(2,1)S(1)} %get-tuple-element.27.field_ref.latent_ref, ...), custom_call_target="tpu_custom_call" | custom-call | tf_op jit(solution)/shard_map/pallas_call | solution.py:323
  25.5 0.9 %collective-permute-start.1 = (bf16[4,2,64,256]{3,2,1,0:T(8,128)(2,1)S(1)}, bf16[4,2,64,256]{3,2,1,0:T(8,128)(2,1)S(1)}, u32[]{:S(2)}, u32[]{:S(2)}) collective-permute-start(bf16[4,2,64,256]{3,2,1,0:T(8,128)(2,1)S(1)} %get-tuple-element.33.hidden_ref), channel_id=1, source_target_pairs={{1,0},{2,1},{3,2},{4,3},{5,4},{6,5},{7,6},{8,7},{9,8},{10,9},{11,1... | collective-permute-start | bytes 786440 | tf_op jit(solution)/shard_map/ppermute | solution.py:326
  26.4 12.7 %all_to_all.11.parts_ref = f32[32,1,128]{2,1,0:T(1,128)S(1)} all-to-all(f32[32,1,128]{2,1,0:T(1,128)S(1)} %get-tuple-element.32), channel_id=1, replica_groups=mesh['tm'=8,'space'=32] {'space'}, dimensions={0} | all-to-all | bytes 32768 | tf_op jit(solution)/shard_map/all_to_all | solution.py:306
  39.1 0.0 collective-permute-done.1.below_ref
  39.1 0.0 copy-done
  39.1 2.0 %shard_map.120 = (bf16[2,2,64,256]{3,2,1,0:T(8,128)(2,1)S(1)}, bf16[2,2,64,256]{3,2,1,0:T(8,128)(2,1)S(1)}) custom-call(s32[8]{0:T(128)S(4)} %get-tuple-element.24.plan_ref, f32[1,256]{1,0:T(1,128)S(1)} %get-tuple-element.25.length_ref, f32[32,1,128]{2,1,0:T(1,128)S(1)} %all_to_all.11.parts_ref, bf16[4,2,64,256]{3,2,1,0:T(8,128)(2,1)S(1)} %get-tuple-element.33.hidden_ref, ...), custom_call_target="tpu_custom_call" | custom-call | tf_op jit(solution)/shard_map/pallas_call | solution.py:329
  41.1 4.2 %collective-permute-start.2 = (bf16[2,2,64,256]{3,2,1,0:T(8,128)(2,1)S(1)}, bf16[2,2,64,256]{3,2,1,0:T(8,128)(2,1)S(1)}, u32[]{:S(2)}, u32[]{:S(2)}) collective-permute-start(bf16[2,2,64,256]{3,2,1,0:T(8,128)(2,1)S(1)} %get-tuple-element.38), channel_id=1, source_target_pairs={{0,32},{32,0},{64,96},{96,64},{128,160},{160,128},{192,224},{224,1... | collective-permute-start | bytes 393224 | tf_op jit(solution)/shard_map/ppermute | solution.py:332
  45.3 1.0 %collective-permute-done.2.got_ref = bf16[2,2,64,256]{3,2,1,0:T(8,128)(2,1)S(1)} collective-permute-done((bf16[2,2,64,256]{3,2,1,0:T(8,128)(2,1)S(1)}, bf16[2,2,64,256]{3,2,1,0:T(8,128)(2,1)S(1)}, u32[]{:S(2)}, u32[]{:S(2)}) %collective-permute-start.2) | collective-permute-done | bytes 131104 | tf_op jit(solution)/shard_map/ppermute | solution.py:332
  46.2 0.1 shard_map.121
  46.3 1.4 %collective-permute-start.3 = (bf16[2,2,64,256]{3,2,1,0:T(8,128)(2,1)S(1)}, bf16[2,2,64,256]{3,2,1,0:T(8,128)(2,1)S(1)}, u32[]{:S(2)}, u32[]{:S(2)}) collective-permute-start(bf16[2,2,64,256]{3,2,1,0:T(8,128)(2,1)S(1)} %get-tuple-element.40), channel_id=1, source_target_pairs={{0,64},{32,96},{64,128},{96,160},{128,192},{160,224},{192,0},{224,... | collective-permute-start | bytes 393224 | tf_op jit(solution)/shard_map/ppermute | solution.py:337
  47.7 2.6 %collective-permute-start.4 = (bf16[2,2,64,256]{3,2,1,0:T(8,128)(2,1)S(1)}, bf16[2,2,64,256]{3,2,1,0:T(8,128)(2,1)S(1)}, u32[]{:S(2)}, u32[]{:S(2)}) collective-permute-start(bf16[2,2,64,256]{3,2,1,0:T(8,128)(2,1)S(1)} %get-tuple-element.41), channel_id=1, source_target_pairs={{0,128},{32,160},{64,192},{96,224},{128,0},{160,32},{192,64},{224,... | collective-permute-start | bytes 393224 | tf_op jit(solution)/shard_map/ppermute | solution.py:337
  50.3 1.1 %collective-permute-start.5 = (bf16[2,2,64,256]{3,2,1,0:T(8,128)(2,1)S(1)}, bf16[2,2,64,256]{3,2,1,0:T(8,128)(2,1)S(1)}, u32[]{:S(2)}, u32[]{:S(2)}) collective-permute-start(bf16[2,2,64,256]{3,2,1,0:T(8,128)(2,1)S(1)} %get-tuple-element.42), channel_id=1, source_target_pairs={{0,192},{32,224},{64,0},{96,32},{128,64},{160,96},{192,128},{224,1... | collective-permute-start | bytes 393224 | tf_op jit(solution)/shard_map/ppermute | solution.py:337
  51.4 1.1 %collective-permute-done.3.rest_1_ = bf16[2,2,64,256]{3,2,1,0:T(8,128)(2,1)S(1)} collective-permute-done((bf16[2,2,64,256]{3,2,1,0:T(8,128)(2,1)S(1)}, bf16[2,2,64,256]{3,2,1,0:T(8,128)(2,1)S(1)}, u32[]{:S(2)}, u32[]{:S(2)}) %collective-permute-start.3) | collective-permute-done | bytes 131104 | tf_op jit(solution)/shard_map/ppermute | solution.py:337
  52.4 3.9 %collective-permute-done.4.rest_2_ = bf16[2,2,64,256]{3,2,1,0:T(8,128)(2,1)S(1)} collective-permute-done((bf16[2,2,64,256]{3,2,1,0:T(8,128)(2,1)S(1)}, bf16[2,2,64,256]{3,2,1,0:T(8,128)(2,1)S(1)}, u32[]{:S(2)}, u32[]{:S(2)}) %collective-permute-start.4) | collective-permute-done | bytes 131104 | tf_op jit(solution)/shard_map/ppermute | solution.py:337
  56.4 0.0 collective-permute-done.5.rest_3_
  56.4 0.7 %shard_map.122 = bf16[2,2,64,256]{3,2,1,0:T(8,128)(2,1)} custom-call(s32[8]{0:T(128)S(4)} %get-tuple-element.24.plan_ref, bf16[2,2,64,256]{3,2,1,0:T(8,128)(2,1)S(1)} %get-tuple-element.39.rest_0_, bf16[2,2,64,256]{3,2,1,0:T(8,128)(2,1)S(1)} %collective-permute-done.3.rest_1_, bf16[2,2,64,256]{3,2,1,0:T(8,128)(2,1)S(1)} %collective-permute-done.4.rest_2_, ...), custom_call_target="tpu_custom_call" | custom-call | tf_op jit(solution)/shard_map/pallas_call | solution.py:338
Async XLA Ops:
  0.0 23.0 %collective-permute-start = (bf16[4,2,64,256]{3,2,1,0:T(8,128)(2,1)}, bf16[4,2,64,256]{3,2,1,0:T(8,128)(2,1)S(1)}, u32[]{:S(2)}, u32[]{:S(2)}) collective-permute-start(bf16[4,2,64,256]{3,2,1,0:T(8,128)(2,1)} %latent_hbm.1), channel_id=1, source_target_pairs={{0,1},{1,2},{2,3},{3,4},{4,5},{5,6},{6,7},{7,8},{8,9},{9,10},{10,1... | collective-permute-start | bytes 786440 | tf_op jit(solution)/shard_map/ppermute | solution.py:311
  2.5 20.5 %copy-start.1 = (bf16[3,3,3,256,256]{4,3,2,1,0:T(8,128)(2,1)S(1)}, bf16[3,3,3,256,256]{4,3,2,1,0:T(8,128)(2,1)}, u32[]{:S(2)}) copy-start(bf16[3,3,3,256,256]{4,3,2,1,0:T(8,128)(2,1)} %param.18) | copy-start | bytes 10616836
  4.1 34.9 %copy-start = (bf16[3,3,3,256,256]{4,3,2,1,0:T(8,128)(2,1)S(1)}, bf16[3,3,3,256,256]{4,3,2,1,0:T(8,128)(2,1)}, u32[]{:S(2)}) copy-start(bf16[3,3,3,256,256]{4,3,2,1,0:T(8,128)(2,1)} %param.22) | copy-start | bytes 10616836
  25.5 13.6 %collective-permute-start.1 = (bf16[4,2,64,256]{3,2,1,0:T(8,128)(2,1)S(1)}, bf16[4,2,64,256]{3,2,1,0:T(8,128)(2,1)S(1)}, u32[]{:S(2)}, u32[]{:S(2)}) collective-permute-start(bf16[4,2,64,256]{3,2,1,0:T(8,128)(2,1)S(1)} %get-tuple-element.33.hidden_ref), channel_id=1, source_target_pairs={{1,0},{2,1},{3,2},{4,3},{5,4},{6,5},{7,6},{8,7},{9,8},{10,9},{11,1... | collective-permute-start | bytes 786440 | tf_op jit(solution)/shard_map/ppermute | solution.py:326
  41.1 5.2 %collective-permute-start.2 = (bf16[2,2,64,256]{3,2,1,0:T(8,128)(2,1)S(1)}, bf16[2,2,64,256]{3,2,1,0:T(8,128)(2,1)S(1)}, u32[]{:S(2)}, u32[]{:S(2)}) collective-permute-start(bf16[2,2,64,256]{3,2,1,0:T(8,128)(2,1)S(1)} %get-tuple-element.38), channel_id=1, source_target_pairs={{0,32},{32,0},{64,96},{96,64},{128,160},{160,128},{192,224},{224,1... | collective-permute-start | bytes 393224 | tf_op jit(solution)/shard_map/ppermute | solution.py:332
  46.3 6.1 %collective-permute-start.3 = (bf16[2,2,64,256]{3,2,1,0:T(8,128)(2,1)S(1)}, bf16[2,2,64,256]{3,2,1,0:T(8,128)(2,1)S(1)}, u32[]{:S(2)}, u32[]{:S(2)}) collective-permute-start(bf16[2,2,64,256]{3,2,1,0:T(8,128)(2,1)S(1)} %get-tuple-element.40), channel_id=1, source_target_pairs={{0,64},{32,96},{64,128},{96,160},{128,192},{160,224},{192,0},{224,... | collective-permute-start | bytes 393224 | tf_op jit(solution)/shard_map/ppermute | solution.py:337
  47.7 8.7 %collective-permute-start.4 = (bf16[2,2,64,256]{3,2,1,0:T(8,128)(2,1)S(1)}, bf16[2,2,64,256]{3,2,1,0:T(8,128)(2,1)S(1)}, u32[]{:S(2)}, u32[]{:S(2)}) collective-permute-start(bf16[2,2,64,256]{3,2,1,0:T(8,128)(2,1)S(1)} %get-tuple-element.41), channel_id=1, source_target_pairs={{0,128},{32,160},{64,192},{96,224},{128,0},{160,32},{192,64},{224,... | collective-permute-start | bytes 393224 | tf_op jit(solution)/shard_map/ppermute | solution.py:337
  50.3 6.1 %collective-permute-start.5 = (bf16[2,2,64,256]{3,2,1,0:T(8,128)(2,1)S(1)}, bf16[2,2,64,256]{3,2,1,0:T(8,128)(2,1)S(1)}, u32[]{:S(2)}, u32[]{:S(2)}) collective-permute-start(bf16[2,2,64,256]{3,2,1,0:T(8,128)(2,1)S(1)} %get-tuple-element.42), channel_id=1, source_target_pairs={{0,192},{32,224},{64,0},{96,32},{128,64},{160,96},{192,128},{224,1... | collective-permute-start | bytes 393224 | tf_op jit(solution)/shard_map/ppermute | solution.py:337

commit v10 on v9

--- a/solution.py
+++ b/solution.py
@@ -90,25 +90,28 @@
     return mean_back, lax.rsqrt(spread_back / (per_band * bands) + EPSILON)
 
 
-def activate(rows, act_ref, slope, offset, f):
+def activate(value, act_ref, slope, offset, place):
     channels = slope.shape[1]
-    for r in range(act_ref.shape[0]):
-        half = rows(f, r).astype(F32) * slope + offset
-        act = half * jnp.tanh(half) + half
-        left = jnp.concatenate([act[:1], act[:-1]], axis=0)
-        right = jnp.concatenate([act[1:], act[-1:]], axis=0)
-        for step, taken in enumerate((left, act, right)):
-            act_ref[r, :, step * channels : (step + 1) * channels] = taken.astype(BF16)
-
-
-def convolve(rows, act_refs, weight_ref, acc_refs, slope, offset, taken):
+    half = value.astype(F32) * slope + offset
+    act = half * jnp.tanh(half) + half
+    left = jnp.concatenate([act[:1], act[:-1]], axis=0)
+    right = jnp.concatenate([act[1:], act[-1:]], axis=0)
+    for step, taken in enumerate((left, act, right)):
+        act_ref[place, :, step * channels : (step + 1) * channels] = taken.astype(BF16)
+
+
+def convolve(own_ref, other_ref, own_first, act_refs, weight_ref, acc_refs, slope, offset, taken):
     frames = len(act_refs)
-    _, columns, width = act_refs[0].shape
+    height = own_ref.shape[1]
+    width = act_refs[0].shape[2]
+    own_place = jnp.where(own_first, 0, height)
     ready = 0
     for back_step, acc_ref in enumerate(acc_refs):
         used = frames - 2 + back_step
         for f in range(ready, used):
-            activate(rows, act_refs[f], slope, offset, f)
+            for r in range(height):
+                activate(own_ref[f, r], act_refs[f], slope, offset, own_place + r)
+                activate(other_ref[f, r], act_refs[f], slope, offset, height - own_place + r)
         ready = used
         slabs = []
         for places in taken:
@@ -156,7 +159,7 @@
         source = jnp.int32(0)
         for k, start in enumerate(starts):
             source = source + jnp.where((place >= start) & (place < start + frames_ref[k]), k // 2, 0)
-        plan.append(lax.rem(clip // 2 - source + chips, chips))
+        plan.append(lax.rem((1 - 2 * core) * (clip // 2 - source) + chips, chips))
     return plan
 
 
@@ -184,23 +187,21 @@
 
 
 def first_kernel(
-    plan_ref, length_ref, parts_ref, field_ref, above_ref, group_ref, gain_ref, shift_ref, bias_ref, weight_ref,
+    plan_ref, length_ref, parts_ref, field_ref, other_ref, group_ref, gain_ref, shift_ref, bias_ref, weight_ref,
     hidden_ref, out_parts_ref,
     *work_refs,
 ):
     frames, height, columns, channels = field_ref.shape
     zero = jnp.minimum(plan_ref[0], 0)
-    top, _ = band_ends()
-    taken = [(0, jnp.where(top, 2, 1)), (1, 2), (jnp.where(top, 1, 2), 3)]
+    core = lax.rem(lax.axis_index("tm"), 2)
+    top, bottom = band_ends()
+    ends = jnp.where(core == 0, top, bottom)
+    taken = [(0, jnp.where(ends, 2, 1)), (1, 2), (jnp.where(ends, 1, 2), 3)]
     mean, inverse = combine_stats(parts_ref[:, 0], length_ref[...], height * columns, group_ref[...])
     slope = inverse * gain_ref[...] * 0.5
     offset = shift_ref[...] * 0.5 - mean * slope
-
-    def rows(f, r):
-        return above_ref[f, r] if r < 2 else field_ref[f, r - 2]
-
     act_refs, acc_refs = work_refs[:frames], work_refs[frames:]
-    convolve(rows, act_refs, weight_ref, acc_refs, slope, offset, taken)
+    convolve(field_ref, other_ref, core == 1, act_refs, weight_ref, acc_refs, slope, offset, taken)
     for f in range(frames):
         hidden_ref[f] = (frame_sum(acc_refs, f, zero) + bias_ref[...]).astype(BF16)
     row = local_stats(hidden_ref, length_ref[...], group_ref[...])
@@ -208,7 +209,7 @@
 
 
 def second_kernel(
-    plan_ref, length_ref, parts_ref, hidden_ref, below_ref, latent_ref, group_ref, gain_ref, shift_ref, bias_ref,
+    plan_ref, length_ref, parts_ref, hidden_ref, other_ref, latent_ref, group_ref, gain_ref, shift_ref, bias_ref,
     weight_ref,
     keep_ref, send_ref,
     *work_refs,
@@ -221,12 +222,8 @@
     mean, inverse = combine_stats(parts_ref[:, 0], length_ref[...], height * columns, group_ref[...])
     slope = inverse * gain_ref[...] * 0.5
     offset = shift_ref[...] * 0.5 - mean * slope
-
-    def rows(f, r):
-        return hidden_ref[f, r] if r < 2 else below_ref[f, r - 2]
-
     act_refs, acc_refs = work_refs[:frames], work_refs[frames:]
-    convolve(rows, act_refs, weight_ref, acc_refs, slope, offset, taken)
+    convolve(hidden_ref, other_ref, core == 0, act_refs, weight_ref, acc_refs, slope, offset, taken)
     for f in range(frames):
         total = (latent_ref[f].astype(F32) + (frame_sum(acc_refs, f, zero) + bias_ref[...])).astype(BF16)
         place = lax.rem(plan_ref[0] + f, 4)
@@ -248,7 +245,7 @@
     chips = len(out_refs)
     start, length = plan_ref[1], plan_ref[2]
     for step, out_ref in enumerate(out_refs):
-        chip = lax.rem(clip // 2 + step, chips)
+        chip = lax.rem(clip // 2 + chips + (1 - 2 * core) * step, chips)
         for slot in range(2):
             place = 4 * chip + 2 * core + slot - start
             theirs = (place >= 0) & (place < length)
@@ -308,7 +305,16 @@
     work = [pltpu.VMEM((4, columns, 3 * channels), BF16)] * frames
     work += [pltpu.VMEM((frames - 2 + i, height, columns, channels), F32) for i in range(3)]
 
-    above = lax.ppermute(latent, "space", [(i, (i + 1) % bands) for i in range(bands)])
+
+    def from_neighbour(field, step):
+        pairs = [
+            (clip * bands + i, clip * bands + (i + (step if clip % 2 == 0 else -step)) % bands)
+            for clip in range(clips)
+            for i in range(bands)
+        ]
+        return lax.ppermute(field, ("tm", "space"), pairs)
+
+    other = from_neighbour(latent, 1)
     vectors = [row(v) for v in (group_of, gain_first, shift_first, bias_first, gain_second, shift_second, bias_second)]
     outs = [parts_out, (latent.shape, BF16), pltpu.SMEM((8,), jnp.int32), ((1, channels), F32)]
     outs += [(v.shape, v.dtype) for v in vectors]
@@ -321,19 +327,19 @@
     group_row = vectors[0]
     parts = gather(parts)
     hidden, parts = call(first_kernel, [SMEM] + [VMEM] * 9, [(latent.shape, BF16), parts_out], work)(
-        in_smem(plan), length, parts, latent, above, *vectors[:4], taps(conv_first)
+        in_smem(plan), length, parts, latent, other, *vectors[:4], taps(conv_first)
     )
-    below = lax.ppermute(hidden, "space", [((i + 1) % bands, i) for i in range(bands)])
+    hidden_other = from_neighbour(hidden, -1)
     parts = gather(parts)
     half = ((2, height, columns, channels), BF16)
     keep, send = call(second_kernel, [SMEM] + [VMEM] * 10, [half, half], work)(
-        in_smem(plan), length, parts, hidden, below, latent, group_row, *vectors[4:], taps(conv_second),
+        in_smem(plan), length, parts, hidden, hidden_other, latent, group_row, *vectors[4:], taps(conv_second),
     )
     got = lax.ppermute(send, "tm", [(i, i ^ 1) for i in range(clips)])
     chips = clips // 2
     got = list(call(spread_kernel, [SMEM] + [VMEM] * 2, [half] * chips)(in_smem(plan), keep, got))
     for step in range(1, chips):
-        along = [(i, (i + 2 * step) % clips) for i in range(clips)]
+        along = [(i, (i + (2 * step if i % 2 == 0 else -2 * step)) % clips) for i in range(clips)]
         got[step] = lax.ppermute(got[step], "tm", along)
     (out,) = call(pick_kernel, [SMEM] + [ANY] * chips, [half], [pltpu.SemaphoreType.DMA((2,))], HBM)(in_smem(plan), *got)
     return out

time: 57.2 us -> 58.3 us (1.019)
  blocking collectives: 31.5 us -> 26.7 us
  starting transfers between devices: 12.6 us -> 16.2 us
  waiting for transfers between devices: 5.99 us -> 8.11 us
    ppermute x2, starting transfers between devices: 3.39 us -> 9.07 us  [from_neighbour(): return lax.ppermute(field, ('tm', 'space'), pairs)]
    all_to_all x2, blocking collectives: 31.5 us -> 26.7 us  [gather(): return lax.all_to_all(parts, 'space', 0, 0, tiled=True)]
    ppermute x3, waiting for transfers between devices: 5 us -> 7.12 us  [local(): got[step] = lax.ppermute(got[step], 'tm', along)]
    ppermute x3, starting transfers between devices: 5.06 us -> 3.85 us  [local(): got[step] = lax.ppermute(got[step], 'tm', along)]
    ppermute x1, starting transfers between devices: 4.18 us -> 3.31 us  [local(): got = lax.ppermute(send, 'tm', [(i, i ^ 1) for i in range(clips)])]
  transfers between devices with their start and end apart: 6 -> 6, of which waited for: 3 -> 4; matrix products, arithmetic and copies ran while one was open for 0% -> 0% of each run, Pallas kernels for 3% -> 3%
where the time goes in v10:
time: 58.3 us; the launch traced here: 58.2 us
  blocking collectives  26.7 us (46%)
  starting transfers between devices  16.2 us (28%)
  waiting for transfers between devices  8.11 us (14%)
  Pallas kernels  7.04 us (12%)
    all_to_all x2, blocking collectives, gather(): return lax.all_to_all(parts, 'space', 0, 0, tiled=True)  26.7 us
    ppermute x2, starting transfers between devices, from_neighbour(): return lax.ppermute(field, ('tm', 'space'), pairs)  9.07 us
    ppermute x3, waiting for transfers between devices, local(): got[step] = lax.ppermute(got[step], 'tm', along)  7.12 us
    ppermute x3, starting transfers between devices, local(): got[step] = lax.ppermute(got[step], 'tm', along)  3.85 us
    ppermute x1, starting transfers between devices, local(): got = lax.ppermute(send, 'tm', [(i, i ^ 1) for i in range(clips)])  3.31 us
    pallas_call x1, Pallas kernels, local(): call(first_kernel, [SMEM] + [VMEM] * 9, [(latent.shape, BF16), parts_out]...  2.55 us
    pallas_call x1, Pallas kernels, local(): call(second_kernel, [SMEM] + [VMEM] * 10, [half, half], work)  2.1 us
    pallas_call x1, Pallas kernels, local(): call(stats_kernel, [HBM] * (3 + len(vectors)), outs, [scalars, scalars, p...  1.67 us
  transfers between devices with their start and end apart: 6, of which 4 were waited for; matrix products, arithmetic and copies ran while one was open for 0% of the time, Pallas kernels for 3%

profile of v10, /device:TPU:1, one launch (start us, length us, event | category | flops | bytes accessed | tf_op | source)
XLA Modules:
  0.0 58.2 jit_solution(875480311602179189)
XLA Ops:
  0.0 8.6 %collective-permute-start = (bf16[4,2,64,256]{3,2,1,0:T(8,128)(2,1)}, bf16[4,2,64,256]{3,2,1,0:T(8,128)(2,1)S(1)}, u32[]{:S(2)}, u32[]{:S(2)}) collective-permute-start(bf16[4,2,64,256]{3,2,1,0:T(8,128)(2,1)} %latent_hbm.1), channel_id=1, source_target_pairs={{0,1},{1,2},{2,3},{3,4},{4,5},{5,6},{6,7},{7,8},{8,9},{9,10},{10,1... | collective-permute-start | bytes 786440 | tf_op jit(solution)/shard_map/ppermute | solution.py:315
  8.6 0.0 copy-start.1
  8.6 1.7 %shard_map.118 = (f32[32,1,128]{2,1,0:T(1,128)S(1)}, bf16[4,2,64,256]{3,2,1,0:T(8,128)(2,1)S(1)}, s32[8]{0:T(128)S(4)}, f32[1,256]{1,0:T(1,128)S(1)}, s32[1,256]...) custom-call(s32[8]{0:T(128)} %frames_hbm.1, ...), custom_call_target="tpu_custom_call" | custom-call | flops 4294967296 | bytes 16777216 | tf_op jit(solution)/shard_map/pallas_call | solution.py:322
  10.3 0.0 copy-start
  10.3 12.2 %all_to_all.10.parts_ref = f32[32,1,128]{2,1,0:T(1,128)S(1)} all-to-all(f32[32,1,128]{2,1,0:T(1,128)S(1)} %get-tuple-element.26), channel_id=1, replica_groups=mesh['tm'=8,'space'=32] {'space'}, dimensions={0} | all-to-all | bytes 32768 | tf_op jit(solution)/shard_map/all_to_all | solution.py:303
  22.5 0.0 collective-permute-done.other_ref
  22.5 0.0 copy-done.1
  22.5 2.5 %shard_map.119 = (bf16[4,2,64,256]{3,2,1,0:T(8,128)(2,1)S(1)}, f32[32,1,128]{2,1,0:T(1,128)S(1)}) custom-call(s32[8]{0:T(128)S(4)} %get-tuple-element.24.plan_ref, f32[1,256]{1,0:T(1,128)S(1)} %get-tuple-element.25.length_ref, f32[32,1,128]{2,1,0:T(1,128)S(1)} %all_to_all.10.parts_ref, bf16[4,2,64,256]{3,2,1,0:T(8,128)(2,1)S(1)} %get-tuple-element.27.field_ref.latent_ref, ...), custom_call_target="tpu_custom_call" | custom-call | tf_op jit(solution)/shard_map/pallas_call | solution.py:329
  25.1 0.5 collective-permute-start.1
  25.6 14.5 %all_to_all.11.parts_ref = f32[32,1,128]{2,1,0:T(1,128)S(1)} all-to-all(f32[32,1,128]{2,1,0:T(1,128)S(1)} %get-tuple-element.32), channel_id=1, replica_groups=mesh['tm'=8,'space'=32] {'space'}, dimensions={0} | all-to-all | bytes 32768 | tf_op jit(solution)/shard_map/all_to_all | solution.py:303
  40.1 0.0 collective-permute-done.1.other_ref
  40.1 0.0 copy-done
  40.1 2.1 %shard_map.120 = (bf16[2,2,64,256]{3,2,1,0:T(8,128)(2,1)S(1)}, bf16[2,2,64,256]{3,2,1,0:T(8,128)(2,1)S(1)}) custom-call(s32[8]{0:T(128)S(4)} %get-tuple-element.24.plan_ref, f32[1,256]{1,0:T(1,128)S(1)} %get-tuple-element.25.length_ref, f32[32,1,128]{2,1,0:T(1,128)S(1)} %all_to_all.11.parts_ref, bf16[4,2,64,256]{3,2,1,0:T(8,128)(2,1)S(1)} %get-tuple-element.33.hidden_ref, ...), custom_call_target="tpu_custom_call" | custom-call | tf_op jit(solution)/shard_map/pallas_call | solution.py:335
  42.2 3.3 %collective-permute-start.2 = (bf16[2,2,64,256]{3,2,1,0:T(8,128)(2,1)S(1)}, bf16[2,2,64,256]{3,2,1,0:T(8,128)(2,1)S(1)}, u32[]{:S(2)}, u32[]{:S(2)}) collective-permute-start(bf16[2,2,64,256]{3,2,1,0:T(8,128)(2,1)S(1)} %get-tuple-element.38), channel_id=1, source_target_pairs={{0,32},{32,0},{64,96},{96,64},{128,160},{160,128},{192,224},{224,1... | collective-permute-start | bytes 393224 | tf_op jit(solution)/shard_map/ppermute | solution.py:338
  45.5 1.0 %collective-permute-done.2.got_ref = bf16[2,2,64,256]{3,2,1,0:T(8,128)(2,1)S(1)} collective-permute-done((bf16[2,2,64,256]{3,2,1,0:T(8,128)(2,1)S(1)}, bf16[2,2,64,256]{3,2,1,0:T(8,128)(2,1)S(1)}, u32[]{:S(2)}, u32[]{:S(2)}) %collective-permute-start.2) | collective-permute-done | bytes 131104 | tf_op jit(solution)/shard_map/ppermute | solution.py:338
  46.5 0.1 shard_map.121
  46.5 2.8 %collective-permute-start.3 = (bf16[2,2,64,256]{3,2,1,0:T(8,128)(2,1)S(1)}, bf16[2,2,64,256]{3,2,1,0:T(8,128)(2,1)S(1)}, u32[]{:S(2)}, u32[]{:S(2)}) collective-permute-start(bf16[2,2,64,256]{3,2,1,0:T(8,128)(2,1)S(1)} %get-tuple-element.40), channel_id=1, source_target_pairs={{0,64},{32,224},{64,128},{96,32},{128,192},{160,96},{192,0},{224,1... | collective-permute-start | bytes 393224 | tf_op jit(solution)/shard_map/ppermute | solution.py:343
  49.3 0.3 collective-permute-start.4
  49.7 0.7 %collective-permute-start.5 = (bf16[2,2,64,256]{3,2,1,0:T(8,128)(2,1)S(1)}, bf16[2,2,64,256]{3,2,1,0:T(8,128)(2,1)S(1)}, u32[]{:S(2)}, u32[]{:S(2)}) collective-permute-start(bf16[2,2,64,256]{3,2,1,0:T(8,128)(2,1)S(1)} %get-tuple-element.42), channel_id=1, source_target_pairs={{0,192},{32,96},{64,0},{96,160},{128,64},{160,224},{192,128},{224,... | collective-permute-start | bytes 393224 | tf_op jit(solution)/shard_map/ppermute | solution.py:343
  50.4 4.0 %collective-permute-done.3.rest_1_ = bf16[2,2,64,256]{3,2,1,0:T(8,128)(2,1)S(1)} collective-permute-done((bf16[2,2,64,256]{3,2,1,0:T(8,128)(2,1)S(1)}, bf16[2,2,64,256]{3,2,1,0:T(8,128)(2,1)S(1)}, u32[]{:S(2)}, u32[]{:S(2)}) %collective-permute-start.3) | collective-permute-done | bytes 131104 | tf_op jit(solution)/shard_map/ppermute | solution.py:343
  54.4 2.0 %collective-permute-done.4.rest_2_ = bf16[2,2,64,256]{3,2,1,0:T(8,128)(2,1)S(1)} collective-permute-done((bf16[2,2,64,256]{3,2,1,0:T(8,128)(2,1)S(1)}, bf16[2,2,64,256]{3,2,1,0:T(8,128)(2,1)S(1)}, u32[]{:S(2)}, u32[]{:S(2)}) %collective-permute-start.4) | collective-permute-done | bytes 131104 | tf_op jit(solution)/shard_map/ppermute | solution.py:343
  56.4 1.1 %collective-permute-done.5.rest_3_ = bf16[2,2,64,256]{3,2,1,0:T(8,128)(2,1)S(1)} collective-permute-done((bf16[2,2,64,256]{3,2,1,0:T(8,128)(2,1)S(1)}, bf16[2,2,64,256]{3,2,1,0:T(8,128)(2,1)S(1)}, u32[]{:S(2)}, u32[]{:S(2)}) %collective-permute-start.5) | collective-permute-done | bytes 131104 | tf_op jit(solution)/shard_map/ppermute | solution.py:343
  57.5 0.7 %shard_map.122 = bf16[2,2,64,256]{3,2,1,0:T(8,128)(2,1)} custom-call(s32[8]{0:T(128)S(4)} %get-tuple-element.24.plan_ref, bf16[2,2,64,256]{3,2,1,0:T(8,128)(2,1)S(1)} %get-tuple-element.39.rest_0_, bf16[2,2,64,256]{3,2,1,0:T(8,128)(2,1)S(1)} %collective-permute-done.3.rest_1_, bf16[2,2,64,256]{3,2,1,0:T(8,128)(2,1)S(1)} %collective-permute-done.4.rest_2_, ...), custom_call_target="tpu_custom_call" | custom-call | tf_op jit(solution)/shard_map/pallas_call | solution.py:344
Async XLA Ops:
  0.0 22.5 %collective-permute-start = (bf16[4,2,64,256]{3,2,1,0:T(8,128)(2,1)}, bf16[4,2,64,256]{3,2,1,0:T(8,128)(2,1)S(1)}, u32[]{:S(2)}, u32[]{:S(2)}) collective-permute-start(bf16[4,2,64,256]{3,2,1,0:T(8,128)(2,1)} %latent_hbm.1), channel_id=1, source_target_pairs={{0,1},{1,2},{2,3},{3,4},{4,5},{5,6},{6,7},{7,8},{8,9},{9,10},{10,1... | collective-permute-start | bytes 786440 | tf_op jit(solution)/shard_map/ppermute | solution.py:315
  8.6 13.9 %copy-start.1 = (bf16[3,3,3,256,256]{4,3,2,1,0:T(8,128)(2,1)S(1)}, bf16[3,3,3,256,256]{4,3,2,1,0:T(8,128)(2,1)}, u32[]{:S(2)}) copy-start(bf16[3,3,3,256,256]{4,3,2,1,0:T(8,128)(2,1)} %param.18) | copy-start | bytes 10616836
  10.3 29.8 %copy-start = (bf16[3,3,3,256,256]{4,3,2,1,0:T(8,128)(2,1)S(1)}, bf16[3,3,3,256,256]{4,3,2,1,0:T(8,128)(2,1)}, u32[]{:S(2)}) copy-start(bf16[3,3,3,256,256]{4,3,2,1,0:T(8,128)(2,1)} %param.22) | copy-start | bytes 10616836
  25.1 15.0 %collective-permute-start.1 = (bf16[4,2,64,256]{3,2,1,0:T(8,128)(2,1)S(1)}, bf16[4,2,64,256]{3,2,1,0:T(8,128)(2,1)S(1)}, u32[]{:S(2)}, u32[]{:S(2)}) collective-permute-start(bf16[4,2,64,256]{3,2,1,0:T(8,128)(2,1)S(1)} %get-tuple-element.33.hidden_ref), channel_id=1, source_target_pairs={{0,31},{1,0},{2,1},{3,2},{4,3},{5,4},{6,5},{7,6},{8,7},{9,8},{10,9... | collective-permute-start | bytes 786440 | tf_op jit(solution)/shard_map/ppermute | solution.py:315
  42.2 4.3 %collective-permute-start.2 = (bf16[2,2,64,256]{3,2,1,0:T(8,128)(2,1)S(1)}, bf16[2,2,64,256]{3,2,1,0:T(8,128)(2,1)S(1)}, u32[]{:S(2)}, u32[]{:S(2)}) collective-permute-start(bf16[2,2,64,256]{3,2,1,0:T(8,128)(2,1)S(1)} %get-tuple-element.38), channel_id=1, source_target_pairs={{0,32},{32,0},{64,96},{96,64},{128,160},{160,128},{192,224},{224,1... | collective-permute-start | bytes 393224 | tf_op jit(solution)/shard_map/ppermute | solution.py:338
  46.5 7.9 %collective-permute-start.3 = (bf16[2,2,64,256]{3,2,1,0:T(8,128)(2,1)S(1)}, bf16[2,2,64,256]{3,2,1,0:T(8,128)(2,1)S(1)}, u32[]{:S(2)}, u32[]{:S(2)}) collective-permute-start(bf16[2,2,64,256]{3,2,1,0:T(8,128)(2,1)S(1)} %get-tuple-element.40), channel_id=1, source_target_pairs={{0,64},{32,224},{64,128},{96,32},{128,192},{160,96},{192,0},{224,1... | collective-permute-start | bytes 393224 | tf_op jit(solution)/shard_map/ppermute | solution.py:343
  49.3 7.1 %collective-permute-start.4 = (bf16[2,2,64,256]{3,2,1,0:T(8,128)(2,1)S(1)}, bf16[2,2,64,256]{3,2,1,0:T(8,128)(2,1)S(1)}, u32[]{:S(2)}, u32[]{:S(2)}) collective-permute-start(bf16[2,2,64,256]{3,2,1,0:T(8,128)(2,1)S(1)} %get-tuple-element.41), channel_id=1, source_target_pairs={{0,128},{32,160},{64,192},{96,224},{128,0},{160,32},{192,64},{224,... | collective-permute-start | bytes 393224 | tf_op jit(solution)/shard_map/ppermute | solution.py:343
  49.7 7.8 %collective-permute-start.5 = (bf16[2,2,64,256]{3,2,1,0:T(8,128)(2,1)S(1)}, bf16[2,2,64,256]{3,2,1,0:T(8,128)(2,1)S(1)}, u32[]{:S(2)}, u32[]{:S(2)}) collective-permute-start(bf16[2,2,64,256]{3,2,1,0:T(8,128)(2,1)S(1)} %get-tuple-element.42), channel_id=1, source_target_pairs={{0,192},{32,96},{64,0},{96,160},{128,64},{160,224},{192,128},{224,... | collective-permute-start | bytes 393224 | tf_op jit(solution)/shard_map/ppermute | solution.py:343

commit v11 on v9

--- a/solution.py
+++ b/solution.py
@@ -302,8 +302,9 @@
     group_row = row(group_of)
     parts_out = ((bands, 1, LANES), F32)
 
-    def gather(parts):
-        return lax.all_to_all(parts, "space", 0, 0, tiled=True)
+    def gather(parts, leader):
+        order = [(leader + i) % bands for i in range(bands)]
+        return lax.all_to_all(parts, "space", 0, 0, axis_index_groups=[order], tiled=True)
 
     work = [pltpu.VMEM((4, columns, 3 * channels), BF16)] * frames
     work += [pltpu.VMEM((frames - 2 + i, height, columns, channels), F32) for i in range(3)]
@@ -319,12 +320,12 @@
         cost=pl.CostEstimate(flops=1 << 32, bytes_accessed=1 << 24, transcendentals=0),
     )(*map(in_hbm, (clip_frames, clip_rank, latent, *vectors)))
     group_row = vectors[0]
-    parts = gather(parts)
+    parts = gather(parts, 3 * bands // 8)
     hidden, parts = call(first_kernel, [SMEM] + [VMEM] * 9, [(latent.shape, BF16), parts_out], work)(
         in_smem(plan), length, parts, latent, above, *vectors[:4], taps(conv_first)
     )
     below = lax.ppermute(hidden, "space", [((i + 1) % bands, i) for i in range(bands)])
-    parts = gather(parts)
+    parts = gather(parts, 5 * bands // 8)
     half = ((2, height, columns, channels), BF16)
     keep, send = call(second_kernel, [SMEM] + [VMEM] * 10, [half, half], work)(
         in_smem(plan), length, parts, hidden, below, latent, group_row, *vectors[4:], taps(conv_second),

time: 57.2 us -> 53.3 us (0.932)
  blocking collectives: 31.5 us -> 26 us
  starting transfers between devices: 12.6 us -> 14.3 us
    all_to_all x2, blocking collectives: 31.5 us -> 26 us  [gather(): lax.all_to_all(parts, 'space', 0, 0, axis_index_groups=[order], tiled=True)]
    ppermute x1, starting transfers between devices: 0.92 us -> 2.55 us  [local(): lax.ppermute(hidden, 'space', [((i + 1) % bands, i) for i in range(bands)])]
where the time goes in v11:
time: 53.3 us; the launch traced here: 53.2 us
  blocking collectives  26 us (49%)
  starting transfers between devices  14.3 us (27%)
  Pallas kernels  6.83 us (13%)
  waiting for transfers between devices  5.99 us (11%)
    all_to_all x2, blocking collectives, gather(): lax.all_to_all(parts, 'space', 0, 0, axis_index_groups=[order], tiled=True)  26 us
    ppermute x3, starting transfers between devices, local(): got[step] = lax.ppermute(got[step], 'tm', along)  5.06 us
    ppermute x3, waiting for transfers between devices, local(): got[step] = lax.ppermute(got[step], 'tm', along)  5 us
    ppermute x1, starting transfers between devices, local(): got = lax.ppermute(send, 'tm', [(i, i ^ 1) for i in range(clips)])  4.18 us
    ppermute x1, starting transfers between devices, local(): lax.ppermute(hidden, 'space', [((i + 1) % bands, i) for i in range(bands)])  2.55 us
    ppermute x1, starting transfers between devices, local(): lax.ppermute(latent, 'space', [(i, (i + 1) % bands) for i in range(bands)])  2.47 us
    pallas_call x1, Pallas kernels, local(): call(first_kernel, [SMEM] + [VMEM] * 9, [(latent.shape, BF16), parts_out]...  2.44 us
    pallas_call x1, Pallas kernels, local(): call(second_kernel, [SMEM] + [VMEM] * 10, [half, half], work)  1.99 us
  transfers between devices with their start and end apart: 6, of which 3 were waited for; matrix products, arithmetic and copies ran while one was open for 0% of the time, Pallas kernels for 3%

profile of v11, /device:TPU:1, one launch (start us, length us, event | category | flops | bytes accessed | tf_op | source)
XLA Modules:
  0.0 53.2 jit_solution(17014633884932593920)
XLA Ops:
  0.0 2.5 %collective-permute-start = (bf16[4,2,64,256]{3,2,1,0:T(8,128)(2,1)}, bf16[4,2,64,256]{3,2,1,0:T(8,128)(2,1)S(1)}, u32[]{:S(2)}, u32[]{:S(2)}) collective-permute-start(bf16[4,2,64,256]{3,2,1,0:T(8,128)(2,1)} %latent_hbm.1), channel_id=1, source_target_pairs={{0,1},{1,2},{2,3},{3,4},{4,5},{5,6},{6,7},{7,8},{8,9},{9,10},{10,1... | collective-permute-start | bytes 786440 | tf_op jit(solution)/shard_map/ppermute | solution.py:312
  2.5 0.0 copy-start.1
  2.5 1.7 %shard_map.118 = (f32[32,1,128]{2,1,0:T(1,128)S(1)}, bf16[4,2,64,256]{3,2,1,0:T(8,128)(2,1)S(1)}, s32[8]{0:T(128)S(4)}, f32[1,256]{1,0:T(1,128)S(1)}, s32[1,256]...) custom-call(s32[8]{0:T(128)} %frames_hbm.1, ...), custom_call_target="tpu_custom_call" | custom-call | flops 4294967296 | bytes 16777216 | tf_op jit(solution)/shard_map/pallas_call | solution.py:317
  4.1 0.0 copy-start
  4.2 15.5 %all_to_all.10.parts_ref = f32[32,1,128]{2,1,0:T(1,128)S(1)} all-to-all(f32[32,1,128]{2,1,0:T(1,128)S(1)} %get-tuple-element.26), channel_id=1, replica_groups={{12,13,14,15,16,17,18,19,20,21,22,23,24,25,26,27,28,29,30,31,0,1,2,3,4,..., dimensions={0} | all-to-all | bytes 32768 | tf_op jit(solution)/shard_map/all_to_all | solution.py:307
  19.7 0.0 collective-permute-done.above_ref
  19.7 0.0 copy-done.1
  19.7 2.4 %shard_map.119 = (bf16[4,2,64,256]{3,2,1,0:T(8,128)(2,1)S(1)}, f32[32,1,128]{2,1,0:T(1,128)S(1)}) custom-call(s32[8]{0:T(128)S(4)} %get-tuple-element.24.plan_ref, f32[1,256]{1,0:T(1,128)S(1)} %get-tuple-element.25.length_ref, f32[32,1,128]{2,1,0:T(1,128)S(1)} %all_to_all.10.parts_ref, bf16[4,2,64,256]{3,2,1,0:T(8,128)(2,1)S(1)} %get-tuple-element.27.field_ref.latent_ref, ...), custom_call_target="tpu_custom_call" | custom-call | tf_op jit(solution)/shard_map/pallas_call | solution.py:324
  22.1 2.5 %collective-permute-start.1 = (bf16[4,2,64,256]{3,2,1,0:T(8,128)(2,1)S(1)}, bf16[4,2,64,256]{3,2,1,0:T(8,128)(2,1)S(1)}, u32[]{:S(2)}, u32[]{:S(2)}) collective-permute-start(bf16[4,2,64,256]{3,2,1,0:T(8,128)(2,1)S(1)} %get-tuple-element.33.hidden_ref), channel_id=1, source_target_pairs={{1,0},{2,1},{3,2},{4,3},{5,4},{6,5},{7,6},{8,7},{9,8},{10,9},{11,1... | collective-permute-start | bytes 786440 | tf_op jit(solution)/shard_map/ppermute | solution.py:327
  24.7 10.5 %all_to_all.11.parts_ref = f32[32,1,128]{2,1,0:T(1,128)S(1)} all-to-all(f32[32,1,128]{2,1,0:T(1,128)S(1)} %get-tuple-element.32), channel_id=1, replica_groups={{20,21,22,23,24,25,26,27,28,29,30,31,0,1,2,3,4,5,6,7,8,9,10,11,12,13,14..., dimensions={0} | all-to-all | bytes 32768 | tf_op jit(solution)/shard_map/all_to_all | solution.py:307
  35.2 0.0 collective-permute-done.1.below_ref
  35.2 0.0 copy-done
  35.2 2.0 %shard_map.120 = (bf16[2,2,64,256]{3,2,1,0:T(8,128)(2,1)S(1)}, bf16[2,2,64,256]{3,2,1,0:T(8,128)(2,1)S(1)}) custom-call(s32[8]{0:T(128)S(4)} %get-tuple-element.24.plan_ref, f32[1,256]{1,0:T(1,128)S(1)} %get-tuple-element.25.length_ref, f32[32,1,128]{2,1,0:T(1,128)S(1)} %all_to_all.11.parts_ref, bf16[4,2,64,256]{3,2,1,0:T(8,128)(2,1)S(1)} %get-tuple-element.33.hidden_ref, ...), custom_call_target="tpu_custom_call" | custom-call | tf_op jit(solution)/shard_map/pallas_call | solution.py:330
  37.2 4.2 %collective-permute-start.2 = (bf16[2,2,64,256]{3,2,1,0:T(8,128)(2,1)S(1)}, bf16[2,2,64,256]{3,2,1,0:T(8,128)(2,1)S(1)}, u32[]{:S(2)}, u32[]{:S(2)}) collective-permute-start(bf16[2,2,64,256]{3,2,1,0:T(8,128)(2,1)S(1)} %get-tuple-element.38), channel_id=1, source_target_pairs={{0,32},{32,0},{64,96},{96,64},{128,160},{160,128},{192,224},{224,1... | collective-permute-start | bytes 393224 | tf_op jit(solution)/shard_map/ppermute | solution.py:333
  41.4 1.0 %collective-permute-done.2.got_ref = bf16[2,2,64,256]{3,2,1,0:T(8,128)(2,1)S(1)} collective-permute-done((bf16[2,2,64,256]{3,2,1,0:T(8,128)(2,1)S(1)}, bf16[2,2,64,256]{3,2,1,0:T(8,128)(2,1)S(1)}, u32[]{:S(2)}, u32[]{:S(2)}) %collective-permute-start.2) | collective-permute-done | bytes 131104 | tf_op jit(solution)/shard_map/ppermute | solution.py:333
  42.4 0.1 shard_map.121
  42.4 1.4 %collective-permute-start.3 = (bf16[2,2,64,256]{3,2,1,0:T(8,128)(2,1)S(1)}, bf16[2,2,64,256]{3,2,1,0:T(8,128)(2,1)S(1)}, u32[]{:S(2)}, u32[]{:S(2)}) collective-permute-start(bf16[2,2,64,256]{3,2,1,0:T(8,128)(2,1)S(1)} %get-tuple-element.40), channel_id=1, source_target_pairs={{0,64},{32,96},{64,128},{96,160},{128,192},{160,224},{192,0},{224,... | collective-permute-start | bytes 393224 | tf_op jit(solution)/shard_map/ppermute | solution.py:338
  43.8 2.6 %collective-permute-start.4 = (bf16[2,2,64,256]{3,2,1,0:T(8,128)(2,1)S(1)}, bf16[2,2,64,256]{3,2,1,0:T(8,128)(2,1)S(1)}, u32[]{:S(2)}, u32[]{:S(2)}) collective-permute-start(bf16[2,2,64,256]{3,2,1,0:T(8,128)(2,1)S(1)} %get-tuple-element.41), channel_id=1, source_target_pairs={{0,128},{32,160},{64,192},{96,224},{128,0},{160,32},{192,64},{224,... | collective-permute-start | bytes 393224 | tf_op jit(solution)/shard_map/ppermute | solution.py:338
  46.4 1.1 %collective-permute-start.5 = (bf16[2,2,64,256]{3,2,1,0:T(8,128)(2,1)S(1)}, bf16[2,2,64,256]{3,2,1,0:T(8,128)(2,1)S(1)}, u32[]{:S(2)}, u32[]{:S(2)}) collective-permute-start(bf16[2,2,64,256]{3,2,1,0:T(8,128)(2,1)S(1)} %get-tuple-element.42), channel_id=1, source_target_pairs={{0,192},{32,224},{64,0},{96,32},{128,64},{160,96},{192,128},{224,1... | collective-permute-start | bytes 393224 | tf_op jit(solution)/shard_map/ppermute | solution.py:338
  47.5 1.1 %collective-permute-done.3.rest_1_ = bf16[2,2,64,256]{3,2,1,0:T(8,128)(2,1)S(1)} collective-permute-done((bf16[2,2,64,256]{3,2,1,0:T(8,128)(2,1)S(1)}, bf16[2,2,64,256]{3,2,1,0:T(8,128)(2,1)S(1)}, u32[]{:S(2)}, u32[]{:S(2)}) %collective-permute-start.3) | collective-permute-done | bytes 131104 | tf_op jit(solution)/shard_map/ppermute | solution.py:338
  48.6 3.9 %collective-permute-done.4.rest_2_ = bf16[2,2,64,256]{3,2,1,0:T(8,128)(2,1)S(1)} collective-permute-done((bf16[2,2,64,256]{3,2,1,0:T(8,128)(2,1)S(1)}, bf16[2,2,64,256]{3,2,1,0:T(8,128)(2,1)S(1)}, u32[]{:S(2)}, u32[]{:S(2)}) %collective-permute-start.4) | collective-permute-done | bytes 131104 | tf_op jit(solution)/shard_map/ppermute | solution.py:338
  52.5 0.0 collective-permute-done.5.rest_3_
  52.5 0.7 %shard_map.122 = bf16[2,2,64,256]{3,2,1,0:T(8,128)(2,1)} custom-call(s32[8]{0:T(128)S(4)} %get-tuple-element.24.plan_ref, bf16[2,2,64,256]{3,2,1,0:T(8,128)(2,1)S(1)} %get-tuple-element.39.rest_0_, bf16[2,2,64,256]{3,2,1,0:T(8,128)(2,1)S(1)} %collective-permute-done.3.rest_1_, bf16[2,2,64,256]{3,2,1,0:T(8,128)(2,1)S(1)} %collective-permute-done.4.rest_2_, ...), custom_call_target="tpu_custom_call" | custom-call | tf_op jit(solution)/shard_map/pallas_call | solution.py:339
Async XLA Ops:
  0.0 19.7 %collective-permute-start = (bf16[4,2,64,256]{3,2,1,0:T(8,128)(2,1)}, bf16[4,2,64,256]{3,2,1,0:T(8,128)(2,1)S(1)}, u32[]{:S(2)}, u32[]{:S(2)}) collective-permute-start(bf16[4,2,64,256]{3,2,1,0:T(8,128)(2,1)} %latent_hbm.1), channel_id=1, source_target_pairs={{0,1},{1,2},{2,3},{3,4},{4,5},{5,6},{6,7},{7,8},{8,9},{9,10},{10,1... | collective-permute-start | bytes 786440 | tf_op jit(solution)/shard_map/ppermute | solution.py:312
  2.5 17.2 %copy-start.1 = (bf16[3,3,3,256,256]{4,3,2,1,0:T(8,128)(2,1)S(1)}, bf16[3,3,3,256,256]{4,3,2,1,0:T(8,128)(2,1)}, u32[]{:S(2)}) copy-start(bf16[3,3,3,256,256]{4,3,2,1,0:T(8,128)(2,1)} %param.18) | copy-start | bytes 10616836
  4.1 31.1 %copy-start = (bf16[3,3,3,256,256]{4,3,2,1,0:T(8,128)(2,1)S(1)}, bf16[3,3,3,256,256]{4,3,2,1,0:T(8,128)(2,1)}, u32[]{:S(2)}) copy-start(bf16[3,3,3,256,256]{4,3,2,1,0:T(8,128)(2,1)} %param.22) | copy-start | bytes 10616836
  22.1 13.1 %collective-permute-start.1 = (bf16[4,2,64,256]{3,2,1,0:T(8,128)(2,1)S(1)}, bf16[4,2,64,256]{3,2,1,0:T(8,128)(2,1)S(1)}, u32[]{:S(2)}, u32[]{:S(2)}) collective-permute-start(bf16[4,2,64,256]{3,2,1,0:T(8,128)(2,1)S(1)} %get-tuple-element.33.hidden_ref), channel_id=1, source_target_pairs={{1,0},{2,1},{3,2},{4,3},{5,4},{6,5},{7,6},{8,7},{9,8},{10,9},{11,1... | collective-permute-start | bytes 786440 | tf_op jit(solution)/shard_map/ppermute | solution.py:327
  37.2 5.2 %collective-permute-start.2 = (bf16[2,2,64,256]{3,2,1,0:T(8,128)(2,1)S(1)}, bf16[2,2,64,256]{3,2,1,0:T(8,128)(2,1)S(1)}, u32[]{:S(2)}, u32[]{:S(2)}) collective-permute-start(bf16[2,2,64,256]{3,2,1,0:T(8,128)(2,1)S(1)} %get-tuple-element.38), channel_id=1, source_target_pairs={{0,32},{32,0},{64,96},{96,64},{128,160},{160,128},{192,224},{224,1... | collective-permute-start | bytes 393224 | tf_op jit(solution)/shard_map/ppermute | solution.py:333
  42.4 6.1 %collective-permute-start.3 = (bf16[2,2,64,256]{3,2,1,0:T(8,128)(2,1)S(1)}, bf16[2,2,64,256]{3,2,1,0:T(8,128)(2,1)S(1)}, u32[]{:S(2)}, u32[]{:S(2)}) collective-permute-start(bf16[2,2,64,256]{3,2,1,0:T(8,128)(2,1)S(1)} %get-tuple-element.40), channel_id=1, source_target_pairs={{0,64},{32,96},{64,128},{96,160},{128,192},{160,224},{192,0},{224,... | collective-permute-start | bytes 393224 | tf_op jit(solution)/shard_map/ppermute | solution.py:338
  43.8 8.7 %collective-permute-start.4 = (bf16[2,2,64,256]{3,2,1,0:T(8,128)(2,1)S(1)}, bf16[2,2,64,256]{3,2,1,0:T(8,128)(2,1)S(1)}, u32[]{:S(2)}, u32[]{:S(2)}) collective-permute-start(bf16[2,2,64,256]{3,2,1,0:T(8,128)(2,1)S(1)} %get-tuple-element.41), channel_id=1, source_target_pairs={{0,128},{32,160},{64,192},{96,224},{128,0},{160,32},{192,64},{224,... | collective-permute-start | bytes 393224 | tf_op jit(solution)/shard_map/ppermute | solution.py:338
  46.4 6.1 %collective-permute-start.5 = (bf16[2,2,64,256]{3,2,1,0:T(8,128)(2,1)S(1)}, bf16[2,2,64,256]{3,2,1,0:T(8,128)(2,1)S(1)}, u32[]{:S(2)}, u32[]{:S(2)}) collective-permute-start(bf16[2,2,64,256]{3,2,1,0:T(8,128)(2,1)S(1)} %get-tuple-element.42), channel_id=1, source_target_pairs={{0,192},{32,224},{64,0},{96,32},{128,64},{160,96},{192,128},{224,1... | collective-permute-start | bytes 393224 | tf_op jit(solution)/shard_map/ppermute | solution.py:338

commit v12 on v11

--- a/solution.py
+++ b/solution.py
@@ -303,7 +303,7 @@
     parts_out = ((bands, 1, LANES), F32)
 
     def gather(parts, leader):
-        order = [(leader + i) % bands for i in range(bands)]
+        order = [(leader + bands // 4 * i + i // 4) % bands for i in range(bands)]
         return lax.all_to_all(parts, "space", 0, 0, axis_index_groups=[order], tiled=True)
 
     work = [pltpu.VMEM((4, columns, 3 * channels), BF16)] * frames
@@ -320,7 +320,7 @@
         cost=pl.CostEstimate(flops=1 << 32, bytes_accessed=1 << 24, transcendentals=0),
     )(*map(in_hbm, (clip_frames, clip_rank, latent, *vectors)))
     group_row = vectors[0]
-    parts = gather(parts, 3 * bands // 8)
+    parts = gather(parts, 3 * bands // 8 - 1)
     hidden, parts = call(first_kernel, [SMEM] + [VMEM] * 9, [(latent.shape, BF16), parts_out], work)(
         in_smem(plan), length, parts, latent, above, *vectors[:4], taps(conv_first)
     )

time: 53.3 us -> 52.5 us (0.985)
  starting transfers between devices: 14.3 us -> 12.1 us
  blocking collectives: 26 us -> 27.4 us
    ppermute x1, starting transfers between devices: 2.55 us -> 0.37 us  [local(): lax.ppermute(hidden, 'space', [((i + 1) % bands, i) for i in range(bands)])]
    all_to_all x2, blocking collectives: 26 us -> 27.4 us  [gather(): lax.all_to_all(parts, 'space', 0, 0, axis_index_groups=[order], tiled=True)]
where the time goes in v12:
time: 52.5 us; the launch traced here: 52.3 us
  blocking collectives  27.4 us (52%)
  starting transfers between devices  12.1 us (23%)
  Pallas kernels  6.83 us (13%)
  waiting for transfers between devices  5.99 us (11%)
    all_to_all x2, blocking collectives, gather(): lax.all_to_all(parts, 'space', 0, 0, axis_index_groups=[order], tiled=True)  27.4 us
    ppermute x3, starting transfers between devices, local(): got[step] = lax.ppermute(got[step], 'tm', along)  5.06 us
    ppermute x3, waiting for transfers between devices, local(): got[step] = lax.ppermute(got[step], 'tm', along)  5 us
    ppermute x1, starting transfers between devices, local(): got = lax.ppermute(send, 'tm', [(i, i ^ 1) for i in range(clips)])  4.17 us
    ppermute x1, starting transfers between devices, local(): lax.ppermute(latent, 'space', [(i, (i + 1) % bands) for i in range(bands)])  2.47 us
    pallas_call x1, Pallas kernels, local(): call(first_kernel, [SMEM] + [VMEM] * 9, [(latent.shape, BF16), parts_out]...  2.44 us
    pallas_call x1, Pallas kernels, local(): call(second_kernel, [SMEM] + [VMEM] * 10, [half, half], work)  1.99 us
    pallas_call x1, Pallas kernels, local(): call(stats_kernel, [HBM] * (3 + len(vectors)), outs, [scalars, scalars, p...  1.67 us
  transfers between devices with their start and end apart: 6, of which 3 were waited for; matrix products, arithmetic and copies ran while one was open for 0% of the time, Pallas kernels for 3%

profile of v12, /device:TPU:1, one launch (start us, length us, event | category | flops | bytes accessed | tf_op | source)
XLA Modules:
  0.0 52.3 jit_solution(4248382008386910112)
XLA Ops:
  0.0 2.5 %collective-permute-start = (bf16[4,2,64,256]{3,2,1,0:T(8,128)(2,1)}, bf16[4,2,64,256]{3,2,1,0:T(8,128)(2,1)S(1)}, u32[]{:S(2)}, u32[]{:S(2)}) collective-permute-start(bf16[4,2,64,256]{3,2,1,0:T(8,128)(2,1)} %latent_hbm.1), channel_id=1, source_target_pairs={{0,1},{1,2},{2,3},{3,4},{4,5},{5,6},{6,7},{7,8},{8,9},{9,10},{10,1... | collective-permute-start | bytes 786440 | tf_op jit(solution)/shard_map/ppermute | solution.py:312
  2.5 0.0 copy-start.1
  2.5 1.7 %shard_map.118 = (f32[32,1,128]{2,1,0:T(1,128)S(1)}, bf16[4,2,64,256]{3,2,1,0:T(8,128)(2,1)S(1)}, s32[8]{0:T(128)S(4)}, f32[1,256]{1,0:T(1,128)S(1)}, s32[1,256]...) custom-call(s32[8]{0:T(128)} %frames_hbm.1, ...), custom_call_target="tpu_custom_call" | custom-call | flops 4294967296 | bytes 16777216 | tf_op jit(solution)/shard_map/pallas_call | solution.py:317
  4.1 0.0 copy-start
  4.2 16.9 %all_to_all.10.parts_ref = f32[32,1,128]{2,1,0:T(1,128)S(1)} all-to-all(f32[32,1,128]{2,1,0:T(1,128)S(1)} %get-tuple-element.26), channel_id=1, replica_groups={{11,19,27,3,12,20,28,4,13,21,29,5,14,22,30,6,15,23,31,7,16,24,0,8,17,25..., dimensions={0} | all-to-all | bytes 32768 | tf_op jit(solution)/shard_map/all_to_all | solution.py:307
  21.0 0.0 collective-permute-done.above_ref
  21.0 0.0 copy-done.1
  21.0 2.4 %shard_map.119 = (bf16[4,2,64,256]{3,2,1,0:T(8,128)(2,1)S(1)}, f32[32,1,128]{2,1,0:T(1,128)S(1)}) custom-call(s32[8]{0:T(128)S(4)} %get-tuple-element.24.plan_ref, f32[1,256]{1,0:T(1,128)S(1)} %get-tuple-element.25.length_ref, f32[32,1,128]{2,1,0:T(1,128)S(1)} %all_to_all.10.parts_ref, bf16[4,2,64,256]{3,2,1,0:T(8,128)(2,1)S(1)} %get-tuple-element.27.field_ref.latent_ref, ...), custom_call_target="tpu_custom_call" | custom-call | tf_op jit(solution)/shard_map/pallas_call | solution.py:324
  23.5 0.4 collective-permute-start.1
  23.9 10.5 %all_to_all.11.parts_ref = f32[32,1,128]{2,1,0:T(1,128)S(1)} all-to-all(f32[32,1,128]{2,1,0:T(1,128)S(1)} %get-tuple-element.32), channel_id=1, replica_groups={{20,28,4,12,21,29,5,13,22,30,6,14,23,31,7,15,24,0,8,16,25,1,9,17,26,2,1..., dimensions={0} | all-to-all | bytes 32768 | tf_op jit(solution)/shard_map/all_to_all | solution.py:307
  34.4 0.0 collective-permute-done.1.below_ref
  34.4 0.0 copy-done
  34.4 2.0 %shard_map.120 = (bf16[2,2,64,256]{3,2,1,0:T(8,128)(2,1)S(1)}, bf16[2,2,64,256]{3,2,1,0:T(8,128)(2,1)S(1)}) custom-call(s32[8]{0:T(128)S(4)} %get-tuple-element.24.plan_ref, f32[1,256]{1,0:T(1,128)S(1)} %get-tuple-element.25.length_ref, f32[32,1,128]{2,1,0:T(1,128)S(1)} %all_to_all.11.parts_ref, bf16[4,2,64,256]{3,2,1,0:T(8,128)(2,1)S(1)} %get-tuple-element.33.hidden_ref, ...), custom_call_target="tpu_custom_call" | custom-call | tf_op jit(solution)/shard_map/pallas_call | solution.py:330
  36.4 4.2 %collective-permute-start.2 = (bf16[2,2,64,256]{3,2,1,0:T(8,128)(2,1)S(1)}, bf16[2,2,64,256]{3,2,1,0:T(8,128)(2,1)S(1)}, u32[]{:S(2)}, u32[]{:S(2)}) collective-permute-start(bf16[2,2,64,256]{3,2,1,0:T(8,128)(2,1)S(1)} %get-tuple-element.38), channel_id=1, source_target_pairs={{0,32},{32,0},{64,96},{96,64},{128,160},{160,128},{192,224},{224,1... | collective-permute-start | bytes 393224 | tf_op jit(solution)/shard_map/ppermute | solution.py:333
  40.5 1.0 %collective-permute-done.2.got_ref = bf16[2,2,64,256]{3,2,1,0:T(8,128)(2,1)S(1)} collective-permute-done((bf16[2,2,64,256]{3,2,1,0:T(8,128)(2,1)S(1)}, bf16[2,2,64,256]{3,2,1,0:T(8,128)(2,1)S(1)}, u32[]{:S(2)}, u32[]{:S(2)}) %collective-permute-start.2) | collective-permute-done | bytes 131104 | tf_op jit(solution)/shard_map/ppermute | solution.py:333
  41.5 0.1 shard_map.121
  41.6 1.4 %collective-permute-start.3 = (bf16[2,2,64,256]{3,2,1,0:T(8,128)(2,1)S(1)}, bf16[2,2,64,256]{3,2,1,0:T(8,128)(2,1)S(1)}, u32[]{:S(2)}, u32[]{:S(2)}) collective-permute-start(bf16[2,2,64,256]{3,2,1,0:T(8,128)(2,1)S(1)} %get-tuple-element.40), channel_id=1, source_target_pairs={{0,64},{32,96},{64,128},{96,160},{128,192},{160,224},{192,0},{224,... | collective-permute-start | bytes 393224 | tf_op jit(solution)/shard_map/ppermute | solution.py:338
  43.0 2.6 %collective-permute-start.4 = (bf16[2,2,64,256]{3,2,1,0:T(8,128)(2,1)S(1)}, bf16[2,2,64,256]{3,2,1,0:T(8,128)(2,1)S(1)}, u32[]{:S(2)}, u32[]{:S(2)}) collective-permute-start(bf16[2,2,64,256]{3,2,1,0:T(8,128)(2,1)S(1)} %get-tuple-element.41), channel_id=1, source_target_pairs={{0,128},{32,160},{64,192},{96,224},{128,0},{160,32},{192,64},{224,... | collective-permute-start | bytes 393224 | tf_op jit(solution)/shard_map/ppermute | solution.py:338
  45.6 1.1 %collective-permute-start.5 = (bf16[2,2,64,256]{3,2,1,0:T(8,128)(2,1)S(1)}, bf16[2,2,64,256]{3,2,1,0:T(8,128)(2,1)S(1)}, u32[]{:S(2)}, u32[]{:S(2)}) collective-permute-start(bf16[2,2,64,256]{3,2,1,0:T(8,128)(2,1)S(1)} %get-tuple-element.42), channel_id=1, source_target_pairs={{0,192},{32,224},{64,0},{96,32},{128,64},{160,96},{192,128},{224,1... | collective-permute-start | bytes 393224 | tf_op jit(solution)/shard_map/ppermute | solution.py:338
  46.7 1.1 %collective-permute-done.3.rest_1_ = bf16[2,2,64,256]{3,2,1,0:T(8,128)(2,1)S(1)} collective-permute-done((bf16[2,2,64,256]{3,2,1,0:T(8,128)(2,1)S(1)}, bf16[2,2,64,256]{3,2,1,0:T(8,128)(2,1)S(1)}, u32[]{:S(2)}, u32[]{:S(2)}) %collective-permute-start.3) | collective-permute-done | bytes 131104 | tf_op jit(solution)/shard_map/ppermute | solution.py:338
  47.7 3.9 %collective-permute-done.4.rest_2_ = bf16[2,2,64,256]{3,2,1,0:T(8,128)(2,1)S(1)} collective-permute-done((bf16[2,2,64,256]{3,2,1,0:T(8,128)(2,1)S(1)}, bf16[2,2,64,256]{3,2,1,0:T(8,128)(2,1)S(1)}, u32[]{:S(2)}, u32[]{:S(2)}) %collective-permute-start.4) | collective-permute-done | bytes 131104 | tf_op jit(solution)/shard_map/ppermute | solution.py:338
  51.6 0.0 collective-permute-done.5.rest_3_
  51.7 0.7 %shard_map.122 = bf16[2,2,64,256]{3,2,1,0:T(8,128)(2,1)} custom-call(s32[8]{0:T(128)S(4)} %get-tuple-element.24.plan_ref, bf16[2,2,64,256]{3,2,1,0:T(8,128)(2,1)S(1)} %get-tuple-element.39.rest_0_, bf16[2,2,64,256]{3,2,1,0:T(8,128)(2,1)S(1)} %collective-permute-done.3.rest_1_, bf16[2,2,64,256]{3,2,1,0:T(8,128)(2,1)S(1)} %collective-permute-done.4.rest_2_, ...), custom_call_target="tpu_custom_call" | custom-call | tf_op jit(solution)/shard_map/pallas_call | solution.py:339
Async XLA Ops:
  0.0 21.0 %collective-permute-start = (bf16[4,2,64,256]{3,2,1,0:T(8,128)(2,1)}, bf16[4,2,64,256]{3,2,1,0:T(8,128)(2,1)S(1)}, u32[]{:S(2)}, u32[]{:S(2)}) collective-permute-start(bf16[4,2,64,256]{3,2,1,0:T(8,128)(2,1)} %latent_hbm.1), channel_id=1, source_target_pairs={{0,1},{1,2},{2,3},{3,4},{4,5},{5,6},{6,7},{7,8},{8,9},{9,10},{10,1... | collective-permute-start | bytes 786440 | tf_op jit(solution)/shard_map/ppermute | solution.py:312
  2.5 18.6 %copy-start.1 = (bf16[3,3,3,256,256]{4,3,2,1,0:T(8,128)(2,1)S(1)}, bf16[3,3,3,256,256]{4,3,2,1,0:T(8,128)(2,1)}, u32[]{:S(2)}) copy-start(bf16[3,3,3,256,256]{4,3,2,1,0:T(8,128)(2,1)} %param.18) | copy-start | bytes 10616836
  4.1 30.2 %copy-start = (bf16[3,3,3,256,256]{4,3,2,1,0:T(8,128)(2,1)S(1)}, bf16[3,3,3,256,256]{4,3,2,1,0:T(8,128)(2,1)}, u32[]{:S(2)}) copy-start(bf16[3,3,3,256,256]{4,3,2,1,0:T(8,128)(2,1)} %param.22) | copy-start | bytes 10616836
  23.5 10.9 %collective-permute-start.1 = (bf16[4,2,64,256]{3,2,1,0:T(8,128)(2,1)S(1)}, bf16[4,2,64,256]{3,2,1,0:T(8,128)(2,1)S(1)}, u32[]{:S(2)}, u32[]{:S(2)}) collective-permute-start(bf16[4,2,64,256]{3,2,1,0:T(8,128)(2,1)S(1)} %get-tuple-element.33.hidden_ref), channel_id=1, source_target_pairs={{1,0},{2,1},{3,2},{4,3},{5,4},{6,5},{7,6},{8,7},{9,8},{10,9},{11,1... | collective-permute-start | bytes 786440 | tf_op jit(solution)/shard_map/ppermute | solution.py:327
  36.4 5.2 %collective-permute-start.2 = (bf16[2,2,64,256]{3,2,1,0:T(8,128)(2,1)S(1)}, bf16[2,2,64,256]{3,2,1,0:T(8,128)(2,1)S(1)}, u32[]{:S(2)}, u32[]{:S(2)}) collective-permute-start(bf16[2,2,64,256]{3,2,1,0:T(8,128)(2,1)S(1)} %get-tuple-element.38), channel_id=1, source_target_pairs={{0,32},{32,0},{64,96},{96,64},{128,160},{160,128},{192,224},{224,1... | collective-permute-start | bytes 393224 | tf_op jit(solution)/shard_map/ppermute | solution.py:333
  41.6 6.1 %collective-permute-start.3 = (bf16[2,2,64,256]{3,2,1,0:T(8,128)(2,1)S(1)}, bf16[2,2,64,256]{3,2,1,0:T(8,128)(2,1)S(1)}, u32[]{:S(2)}, u32[]{:S(2)}) collective-permute-start(bf16[2,2,64,256]{3,2,1,0:T(8,128)(2,1)S(1)} %get-tuple-element.40), channel_id=1, source_target_pairs={{0,64},{32,96},{64,128},{96,160},{128,192},{160,224},{192,0},{224,... | collective-permute-start | bytes 393224 | tf_op jit(solution)/shard_map/ppermute | solution.py:338
  43.0 8.7 %collective-permute-start.4 = (bf16[2,2,64,256]{3,2,1,0:T(8,128)(2,1)S(1)}, bf16[2,2,64,256]{3,2,1,0:T(8,128)(2,1)S(1)}, u32[]{:S(2)}, u32[]{:S(2)}) collective-permute-start(bf16[2,2,64,256]{3,2,1,0:T(8,128)(2,1)S(1)} %get-tuple-element.41), channel_id=1, source_target_pairs={{0,128},{32,160},{64,192},{96,224},{128,0},{160,32},{192,64},{224,... | collective-permute-start | bytes 393224 | tf_op jit(solution)/shard_map/ppermute | solution.py:338
  45.6 6.1 %collective-permute-start.5 = (bf16[2,2,64,256]{3,2,1,0:T(8,128)(2,1)S(1)}, bf16[2,2,64,256]{3,2,1,0:T(8,128)(2,1)S(1)}, u32[]{:S(2)}, u32[]{:S(2)}) collective-permute-start(bf16[2,2,64,256]{3,2,1,0:T(8,128)(2,1)S(1)} %get-tuple-element.42), channel_id=1, source_target_pairs={{0,192},{32,224},{64,0},{96,32},{128,64},{160,96},{192,128},{224,1... | collective-permute-start | bytes 393224 | tf_op jit(solution)/shard_map/ppermute | solution.py:338

commit v13 on v9

--- a/solution.py
+++ b/solution.py
@@ -166,12 +166,13 @@
     parts_ref, latent_ref, plan_ref, length_ref = rest[:4]
     rows_ref, (frames_ref, rank_ref, sem) = rest[4 : 4 + rows], rest[4 + rows :]
     group_ref = rows_ref[0]
-    pairs = [(frames_hbm, frames_ref), (rank_hbm, rank_ref), (latent_hbm, latent_ref)] + list(zip(rows_hbm, rows_ref))
+    pairs = [(latent_hbm, latent_ref), (frames_hbm, frames_ref), (rank_hbm, rank_ref)] + list(zip(rows_hbm, rows_ref))
     copies = [pltpu.make_async_copy(source, target, sem.at[i]) for i, (source, target) in enumerate(pairs)]
     for copy in copies:
         copy.start()
-    for copy in copies[:4]:
+    for copy in copies[1:4]:
         copy.wait()
+    copies[0].wait()
     length = frames_ref[lax.axis_index("tm")].astype(F32)
     length_row = jnp.full(length_ref.shape, length, F32)
     length_ref[...] = length_row
@@ -302,13 +303,16 @@
     group_row = row(group_of)
     parts_out = ((bands, 1, LANES), F32)
 
-    def gather(parts):
-        return lax.all_to_all(parts, "space", 0, 0, tiled=True)
+    def gather(parts, leaders):
+        groups = [
+            [clip * bands + (leaders[clip % 2] + bands // 4 * i + i // 4) % bands for i in range(bands)]
+            for clip in range(clips)
+        ]
+        return lax.all_to_all(parts, ("tm", "space"), 0, 0, axis_index_groups=groups, tiled=True)
 
     work = [pltpu.VMEM((4, columns, 3 * channels), BF16)] * frames
     work += [pltpu.VMEM((frames - 2 + i, height, columns, channels), F32) for i in range(3)]
 
-    above = lax.ppermute(latent, "space", [(i, (i + 1) % bands) for i in range(bands)])
     vectors = [row(v) for v in (group_of, gain_first, shift_first, bias_first, gain_second, shift_second, bias_second)]
     outs = [parts_out, (latent.shape, BF16), pltpu.SMEM((8,), jnp.int32), ((1, channels), F32)]
     outs += [(v.shape, v.dtype) for v in vectors]
@@ -319,12 +323,13 @@
         cost=pl.CostEstimate(flops=1 << 32, bytes_accessed=1 << 24, transcendentals=0),
     )(*map(in_hbm, (clip_frames, clip_rank, latent, *vectors)))
     group_row = vectors[0]
-    parts = gather(parts)
+    above = lax.ppermute(latent, "space", [(i, (i + 1) % bands) for i in range(bands)])
+    parts = gather(parts, (11, 20))
     hidden, parts = call(first_kernel, [SMEM] + [VMEM] * 9, [(latent.shape, BF16), parts_out], work)(
         in_smem(plan), length, parts, latent, above, *vectors[:4], taps(conv_first)
     )
     below = lax.ppermute(hidden, "space", [((i + 1) % bands, i) for i in range(bands)])
-    parts = gather(parts)
+    parts = gather(parts, (20, 21))
     half = ((2, height, columns, channels), BF16)
     keep, send = call(second_kernel, [SMEM] + [VMEM] * 10, [half, half], work)(
         in_smem(plan), length, parts, hidden, below, latent, group_row, *vectors[4:], taps(conv_second),

time: 57.2 us -> 52.3 us (0.914)
  blocking collectives: 31.5 us -> 24.4 us
  starting transfers between devices: 12.6 us -> 14.8 us
    all_to_all x2, blocking collectives: 31.5 us -> 24.4 us  [gather(): lax.all_to_all(parts, ('tm', 'space'), 0, 0, axis_index_groups=groups, ti...]
    ppermute x1, starting transfers between devices: 0.92 us -> 4.38 us  [local(): lax.ppermute(hidden, 'space', [((i + 1) % bands, i) for i in range(bands)])]
    ppermute x1, starting transfers between devices: 4.18 us -> 2.83 us  [local(): got = lax.ppermute(send, 'tm', [(i, i ^ 1) for i in range(clips)])]
  transfers between devices with their start and end apart: 6 -> 6, of which waited for: 3 -> 3; matrix products, arithmetic and copies ran while one was open for 0% -> 0% of each run, Pallas kernels for 3% -> 0%
where the time goes in v13:
time: 52.3 us; the launch traced here: 52.1 us
  blocking collectives  24.4 us (47%)
  starting transfers between devices  14.8 us (28%)
  Pallas kernels  6.83 us (13%)
  waiting for transfers between devices  5.99 us (11%)
    all_to_all x2, blocking collectives, gather(): lax.all_to_all(parts, ('tm', 'space'), 0, 0, axis_index_groups=groups, ti...  24.4 us
    ppermute x3, starting transfers between devices, local(): got[step] = lax.ppermute(got[step], 'tm', along)  5.06 us
    ppermute x3, waiting for transfers between devices, local(): got[step] = lax.ppermute(got[step], 'tm', along)  5 us
    ppermute x1, starting transfers between devices, local(): lax.ppermute(hidden, 'space', [((i + 1) % bands, i) for i in range(bands)])  4.38 us
    ppermute x1, starting transfers between devices, local(): got = lax.ppermute(send, 'tm', [(i, i ^ 1) for i in range(clips)])  2.83 us
    ppermute x1, starting transfers between devices, local(): lax.ppermute(latent, 'space', [(i, (i + 1) % bands) for i in range(bands)])  2.54 us
    pallas_call x1, Pallas kernels, local(): call(first_kernel, [SMEM] + [VMEM] * 9, [(latent.shape, BF16), parts_out]...  2.44 us
    pallas_call x1, Pallas kernels, local(): call(second_kernel, [SMEM] + [VMEM] * 10, [half, half], work)  1.99 us
  transfers between devices with their start and end apart: 6, of which 3 were waited for; matrix products, arithmetic and copies ran while one was open for 0% of the time, Pallas kernels for 0%

profile of v13, /device:TPU:1, one launch (start us, length us, event | category | flops | bytes accessed | tf_op | source)
XLA Modules:
  0.0 52.1 jit_solution(17095570468820126788)
XLA Ops:
  0.0 0.0 copy-start.1
  0.0 1.7 %shard_map.118 = (f32[32,1,128]{2,1,0:T(1,128)S(1)}, bf16[4,2,64,256]{3,2,1,0:T(8,128)(2,1)S(1)}, s32[8]{0:T(128)S(4)}, f32[1,256]{1,0:T(1,128)S(1)}, s32[1,256]...) custom-call(s32[8]{0:T(128)} %frames_hbm.1, ...), custom_call_target="tpu_custom_call" | custom-call | flops 4294967296 | bytes 16777216 | tf_op jit(solution)/shard_map/pallas_call | solution.py:320
  1.7 0.0 copy-start
  1.7 2.5 %collective-permute-start = (bf16[4,2,64,256]{3,2,1,0:T(8,128)(2,1)S(1)}, bf16[4,2,64,256]{3,2,1,0:T(8,128)(2,1)S(1)}, u32[]{:S(2)}, u32[]{:S(2)}) collective-permute-start(bf16[4,2,64,256]{3,2,1,0:T(8,128)(2,1)S(1)} %get-tuple-element.27.field_ref.latent_ref), channel_id=1, source_target_pairs={{0,1},{1,2},{2,3},{3,4},{4,5},{5,6},{6,7},{7,8},{8,9},{9,10},{10,1... | collective-permute-start | bytes 786440 | tf_op jit(solution)/shard_map/ppermute | solution.py:326
  4.2 13.9 %all_to_all.10.parts_ref = f32[32,1,128]{2,1,0:T(1,128)S(1)} all-to-all(f32[32,1,128]{2,1,0:T(1,128)S(1)} %get-tuple-element.26), channel_id=1, replica_groups={{11,19,27,3,12,20,28,4,13,21,29,5,14,22,30,6,15,23,31,7,16,24,0,8,17,25..., dimensions={0} | all-to-all | bytes 32768 | tf_op jit(solution)/shard_map/all_to_all | solution.py:311
  18.2 0.0 collective-permute-done.above_ref
  18.2 0.0 copy-done.1
  18.2 2.4 %shard_map.119 = (bf16[4,2,64,256]{3,2,1,0:T(8,128)(2,1)S(1)}, f32[32,1,128]{2,1,0:T(1,128)S(1)}) custom-call(s32[8]{0:T(128)S(4)} %get-tuple-element.24.plan_ref, f32[1,256]{1,0:T(1,128)S(1)} %get-tuple-element.25.length_ref, f32[32,1,128]{2,1,0:T(1,128)S(1)} %all_to_all.10.parts_ref, bf16[4,2,64,256]{3,2,1,0:T(8,128)(2,1)S(1)} %get-tuple-element.27.field_ref.latent_ref, ...), custom_call_target="tpu_custom_call" | custom-call | tf_op jit(solution)/shard_map/pallas_call | solution.py:328
  20.6 4.4 %collective-permute-start.1 = (bf16[4,2,64,256]{3,2,1,0:T(8,128)(2,1)S(1)}, bf16[4,2,64,256]{3,2,1,0:T(8,128)(2,1)S(1)}, u32[]{:S(2)}, u32[]{:S(2)}) collective-permute-start(bf16[4,2,64,256]{3,2,1,0:T(8,128)(2,1)S(1)} %get-tuple-element.33.hidden_ref), channel_id=1, source_target_pairs={{1,0},{2,1},{3,2},{4,3},{5,4},{6,5},{7,6},{8,7},{9,8},{10,9},{11,1... | collective-permute-start | bytes 786440 | tf_op jit(solution)/shard_map/ppermute | solution.py:331
  25.0 10.5 %all_to_all.11.parts_ref = f32[32,1,128]{2,1,0:T(1,128)S(1)} all-to-all(f32[32,1,128]{2,1,0:T(1,128)S(1)} %get-tuple-element.32), channel_id=1, replica_groups={{20,28,4,12,21,29,5,13,22,30,6,14,23,31,7,15,24,0,8,16,25,1,9,17,26,2,1..., dimensions={0} | all-to-all | bytes 32768 | tf_op jit(solution)/shard_map/all_to_all | solution.py:311
  35.5 0.0 collective-permute-done.1.below_ref
  35.5 0.0 copy-done
  35.5 2.0 %shard_map.120 = (bf16[2,2,64,256]{3,2,1,0:T(8,128)(2,1)S(1)}, bf16[2,2,64,256]{3,2,1,0:T(8,128)(2,1)S(1)}) custom-call(s32[8]{0:T(128)S(4)} %get-tuple-element.24.plan_ref, f32[1,256]{1,0:T(1,128)S(1)} %get-tuple-element.25.length_ref, f32[32,1,128]{2,1,0:T(1,128)S(1)} %all_to_all.11.parts_ref, bf16[4,2,64,256]{3,2,1,0:T(8,128)(2,1)S(1)} %get-tuple-element.33.hidden_ref, ...), custom_call_target="tpu_custom_call" | custom-call | tf_op jit(solution)/shard_map/pallas_call | solution.py:334
  37.5 2.8 %collective-permute-start.2 = (bf16[2,2,64,256]{3,2,1,0:T(8,128)(2,1)S(1)}, bf16[2,2,64,256]{3,2,1,0:T(8,128)(2,1)S(1)}, u32[]{:S(2)}, u32[]{:S(2)}) collective-permute-start(bf16[2,2,64,256]{3,2,1,0:T(8,128)(2,1)S(1)} %get-tuple-element.38), channel_id=1, source_target_pairs={{0,32},{32,0},{64,96},{96,64},{128,160},{160,128},{192,224},{224,1... | collective-permute-start | bytes 393224 | tf_op jit(solution)/shard_map/ppermute | solution.py:337
  40.3 1.0 %collective-permute-done.2.got_ref = bf16[2,2,64,256]{3,2,1,0:T(8,128)(2,1)S(1)} collective-permute-done((bf16[2,2,64,256]{3,2,1,0:T(8,128)(2,1)S(1)}, bf16[2,2,64,256]{3,2,1,0:T(8,128)(2,1)S(1)}, u32[]{:S(2)}, u32[]{:S(2)}) %collective-permute-start.2) | collective-permute-done | bytes 131104 | tf_op jit(solution)/shard_map/ppermute | solution.py:337
  41.3 0.1 shard_map.121
  41.4 1.4 %collective-permute-start.3 = (bf16[2,2,64,256]{3,2,1,0:T(8,128)(2,1)S(1)}, bf16[2,2,64,256]{3,2,1,0:T(8,128)(2,1)S(1)}, u32[]{:S(2)}, u32[]{:S(2)}) collective-permute-start(bf16[2,2,64,256]{3,2,1,0:T(8,128)(2,1)S(1)} %get-tuple-element.40), channel_id=1, source_target_pairs={{0,64},{32,96},{64,128},{96,160},{128,192},{160,224},{192,0},{224,... | collective-permute-start | bytes 393224 | tf_op jit(solution)/shard_map/ppermute | solution.py:342
  42.8 2.6 %collective-permute-start.4 = (bf16[2,2,64,256]{3,2,1,0:T(8,128)(2,1)S(1)}, bf16[2,2,64,256]{3,2,1,0:T(8,128)(2,1)S(1)}, u32[]{:S(2)}, u32[]{:S(2)}) collective-permute-start(bf16[2,2,64,256]{3,2,1,0:T(8,128)(2,1)S(1)} %get-tuple-element.41), channel_id=1, source_target_pairs={{0,128},{32,160},{64,192},{96,224},{128,0},{160,32},{192,64},{224,... | collective-permute-start | bytes 393224 | tf_op jit(solution)/shard_map/ppermute | solution.py:342
  45.4 1.1 %collective-permute-start.5 = (bf16[2,2,64,256]{3,2,1,0:T(8,128)(2,1)S(1)}, bf16[2,2,64,256]{3,2,1,0:T(8,128)(2,1)S(1)}, u32[]{:S(2)}, u32[]{:S(2)}) collective-permute-start(bf16[2,2,64,256]{3,2,1,0:T(8,128)(2,1)S(1)} %get-tuple-element.42), channel_id=1, source_target_pairs={{0,192},{32,224},{64,0},{96,32},{128,64},{160,96},{192,128},{224,1... | collective-permute-start | bytes 393224 | tf_op jit(solution)/shard_map/ppermute | solution.py:342
  46.5 1.1 %collective-permute-done.3.rest_1_ = bf16[2,2,64,256]{3,2,1,0:T(8,128)(2,1)S(1)} collective-permute-done((bf16[2,2,64,256]{3,2,1,0:T(8,128)(2,1)S(1)}, bf16[2,2,64,256]{3,2,1,0:T(8,128)(2,1)S(1)}, u32[]{:S(2)}, u32[]{:S(2)}) %collective-permute-start.3) | collective-permute-done | bytes 131104 | tf_op jit(solution)/shard_map/ppermute | solution.py:342
  47.5 3.9 %collective-permute-done.4.rest_2_ = bf16[2,2,64,256]{3,2,1,0:T(8,128)(2,1)S(1)} collective-permute-done((bf16[2,2,64,256]{3,2,1,0:T(8,128)(2,1)S(1)}, bf16[2,2,64,256]{3,2,1,0:T(8,128)(2,1)S(1)}, u32[]{:S(2)}, u32[]{:S(2)}) %collective-permute-start.4) | collective-permute-done | bytes 131104 | tf_op jit(solution)/shard_map/ppermute | solution.py:342
  51.4 0.0 collective-permute-done.5.rest_3_
  51.4 0.7 %shard_map.122 = bf16[2,2,64,256]{3,2,1,0:T(8,128)(2,1)} custom-call(s32[8]{0:T(128)S(4)} %get-tuple-element.24.plan_ref, bf16[2,2,64,256]{3,2,1,0:T(8,128)(2,1)S(1)} %get-tuple-element.39.rest_0_, bf16[2,2,64,256]{3,2,1,0:T(8,128)(2,1)S(1)} %collective-permute-done.3.rest_1_, bf16[2,2,64,256]{3,2,1,0:T(8,128)(2,1)S(1)} %collective-permute-done.4.rest_2_, ...), custom_call_target="tpu_custom_call" | custom-call | tf_op jit(solution)/shard_map/pallas_call | solution.py:343
Async XLA Ops:
  0.0 18.2 %copy-start.1 = (bf16[3,3,3,256,256]{4,3,2,1,0:T(8,128)(2,1)S(1)}, bf16[3,3,3,256,256]{4,3,2,1,0:T(8,128)(2,1)}, u32[]{:S(2)}) copy-start(bf16[3,3,3,256,256]{4,3,2,1,0:T(8,128)(2,1)} %param.18) | copy-start | bytes 10616836
  1.7 33.8 %copy-start = (bf16[3,3,3,256,256]{4,3,2,1,0:T(8,128)(2,1)S(1)}, bf16[3,3,3,256,256]{4,3,2,1,0:T(8,128)(2,1)}, u32[]{:S(2)}) copy-start(bf16[3,3,3,256,256]{4,3,2,1,0:T(8,128)(2,1)} %param.22) | copy-start | bytes 10616836
  1.7 16.5 %collective-permute-start = (bf16[4,2,64,256]{3,2,1,0:T(8,128)(2,1)S(1)}, bf16[4,2,64,256]{3,2,1,0:T(8,128)(2,1)S(1)}, u32[]{:S(2)}, u32[]{:S(2)}) collective-permute-start(bf16[4,2,64,256]{3,2,1,0:T(8,128)(2,1)S(1)} %get-tuple-element.27.field_ref.latent_ref), channel_id=1, source_target_pairs={{0,1},{1,2},{2,3},{3,4},{4,5},{5,6},{6,7},{7,8},{8,9},{9,10},{10,1... | collective-permute-start | bytes 786440 | tf_op jit(solution)/shard_map/ppermute | solution.py:326
  20.6 14.9 %collective-permute-start.1 = (bf16[4,2,64,256]{3,2,1,0:T(8,128)(2,1)S(1)}, bf16[4,2,64,256]{3,2,1,0:T(8,128)(2,1)S(1)}, u32[]{:S(2)}, u32[]{:S(2)}) collective-permute-start(bf16[4,2,64,256]{3,2,1,0:T(8,128)(2,1)S(1)} %get-tuple-element.33.hidden_ref), channel_id=1, source_target_pairs={{1,0},{2,1},{3,2},{4,3},{5,4},{6,5},{7,6},{8,7},{9,8},{10,9},{11,1... | collective-permute-start | bytes 786440 | tf_op jit(solution)/shard_map/ppermute | solution.py:331
  37.5 3.8 %collective-permute-start.2 = (bf16[2,2,64,256]{3,2,1,0:T(8,128)(2,1)S(1)}, bf16[2,2,64,256]{3,2,1,0:T(8,128)(2,1)S(1)}, u32[]{:S(2)}, u32[]{:S(2)}) collective-permute-start(bf16[2,2,64,256]{3,2,1,0:T(8,128)(2,1)S(1)} %get-tuple-element.38), channel_id=1, source_target_pairs={{0,32},{32,0},{64,96},{96,64},{128,160},{160,128},{192,224},{224,1... | collective-permute-start | bytes 393224 | tf_op jit(solution)/shard_map/ppermute | solution.py:337
  41.4 6.1 %collective-permute-start.3 = (bf16[2,2,64,256]{3,2,1,0:T(8,128)(2,1)S(1)}, bf16[2,2,64,256]{3,2,1,0:T(8,128)(2,1)S(1)}, u32[]{:S(2)}, u32[]{:S(2)}) collective-permute-start(bf16[2,2,64,256]{3,2,1,0:T(8,128)(2,1)S(1)} %get-tuple-element.40), channel_id=1, source_target_pairs={{0,64},{32,96},{64,128},{96,160},{128,192},{160,224},{192,0},{224,... | collective-permute-start | bytes 393224 | tf_op jit(solution)/shard_map/ppermute | solution.py:342
  42.8 8.7 %collective-permute-start.4 = (bf16[2,2,64,256]{3,2,1,0:T(8,128)(2,1)S(1)}, bf16[2,2,64,256]{3,2,1,0:T(8,128)(2,1)S(1)}, u32[]{:S(2)}, u32[]{:S(2)}) collective-permute-start(bf16[2,2,64,256]{3,2,1,0:T(8,128)(2,1)S(1)} %get-tuple-element.41), channel_id=1, source_target_pairs={{0,128},{32,160},{64,192},{96,224},{128,0},{160,32},{192,64},{224,... | collective-permute-start | bytes 393224 | tf_op jit(solution)/shard_map/ppermute | solution.py:342
  45.4 6.1 %collective-permute-start.5 = (bf16[2,2,64,256]{3,2,1,0:T(8,128)(2,1)S(1)}, bf16[2,2,64,256]{3,2,1,0:T(8,128)(2,1)S(1)}, u32[]{:S(2)}, u32[]{:S(2)}) collective-permute-start(bf16[2,2,64,256]{3,2,1,0:T(8,128)(2,1)S(1)} %get-tuple-element.42), channel_id=1, source_target_pairs={{0,192},{32,224},{64,0},{96,32},{128,64},{160,96},{192,128},{224,1... | collective-permute-start | bytes 393224 | tf_op jit(solution)/shard_map/ppermute | solution.py:342
